TPU v7x, 32 devices: a whole 2x2x4 slice. The times are simulated.
32 devices in a mesh: grp: 2 (over y), row: 16 (over z, x, core).
Axes of the slice: x: 2, y: 2, z: 4, core: 2. Of those that a mesh axis runs over, the one named last changes fastest.
Arguments:
- homolog_embedding: bfloat16 [32, 256, 256], P(None, ('grp', 'row')), parts along dimension 1, may hold values from -6 to 6
- presence_indicator: int32 [32, 256], P(None, ('grp', 'row')), parts along dimension 1, may hold values 0 or 1
- former_projection_matrix: bfloat16 [256, 32], replicated, may hold values from -0.375 to 0.375
- latter_projection_matrix: bfloat16 [256, 32], replicated, may hold values from -0.375 to 0.375
- final_projection_matrix: bfloat16 [1024, 128], replicated, may hold values from -1 to 1
- offset_vector: float32 [128], replicated, may hold values from -3 to 3
- couple_increment_cotangent: bfloat16 [256, 128, 128], P(('grp', 'row')), parts along dimension 0, may hold values from -6 to 6
Outputs:
- couple_increment: bfloat16 [256, 128, 128], P(('grp', 'row')), parts along dimension 0
- homolog_embedding_derivative: bfloat16 [32, 256, 256], P(None, ('grp', 'row')), parts along dimension 1
- former_projection_derivative: float32 [512, 32], P('grp'), parts along dimension 0
- latter_projection_derivative: float32 [512, 32], P('grp'), parts along dimension 0
- final_projection_derivative: float32 [2048, 128], P('grp'), parts along dimension 0
- offset_vector_derivative: float32 [256], P('grp'), parts along dimension 0
There are 2 independent parts, one for each index of `grp`. A program takes and returns all parts, laid end to end along the dimension named above; an argument that names none is the same for every part. Nothing has to cross between parts.
All inputs are finite; a program needn't handle non-finite values. No bound on the sum of `presence_indicator` on one device may be relied on, other than what follows from the above.
Results may differ from a plain program's by a relative error of at most 0.0073.
Values may be sent and summed in bfloat16 or wider, within the bound.
No kernel may reach another device: no remote copies, remote signals or barrier semaphores. Data moves between devices by JAX's collectives and lax.ppermute only.
A program may use at most 128 MiB of HBM per device.

v0:
```python
import math

import jax
import jax.numpy as jnp
from jax import lax
from jax.sharding import PartitionSpec as P


def body(
    homolog_embedding,
    presence_indicator,
    former_projection_matrix,
    latter_projection_matrix,
    final_projection_matrix,
    offset_vector,
    couple_increment_cotangent,
):
    standard_precision_type = jnp.float32
    reduced_precision_type = jnp.bfloat16
    homolog_total, shard_lines, feature_depth = homolog_embedding.shape
    width = former_projection_matrix.shape[1]
    pair_ch = final_projection_matrix.shape[1]
    collected_source = homolog_embedding.astype(standard_precision_type)
    mean_val = jnp.mean(collected_source, axis=-1, keepdims=True)
    centred = collected_source - mean_val
    var_val = jnp.mean(centred * centred, axis=-1, keepdims=True)
    reciprocal_spread = lax.rsqrt(var_val + 1e-05)
    standardized_source = centred * reciprocal_spread
    standardized_reduced = standardized_source.astype(reduced_precision_type)
    mask_float = presence_indicator.astype(standard_precision_type)
    left_t = (
        jnp.einsum(
            "srm,mc->scr",
            standardized_reduced,
            former_projection_matrix,
            preferred_element_type=standard_precision_type,
        )
        * mask_float[:, None, :]
    ).astype(reduced_precision_type)
    right_t = (
        jnp.einsum(
            "srm,mc->scr",
            standardized_reduced,
            latter_projection_matrix,
            preferred_element_type=standard_precision_type,
        )
        * mask_float[:, None, :]
    ).astype(reduced_precision_type)
    right_all, mask_all = (
        lax.all_gather(right_t, "row", axis=2, tiled=True),
        lax.all_gather(mask_float.astype(reduced_precision_type), "row", axis=1, tiled=True),
    )
    total = right_all.shape[2]
    block = math.gcd(total, 128)
    nblock = total // block

    def column_step(carry, index):
        update_buf, d_acc, left_acc, right_acc = carry
        start = index * block
        cols = lax.dynamic_slice_in_dim(right_all, start, block, 2)
        mask_cols = lax.dynamic_slice_in_dim(mask_all, start, block, 1).astype(
            standard_precision_type
        )
        cnt = jnp.einsum("si,sj->ij", mask_float, mask_cols) + 1.0
        outer_sum = jnp.einsum(
            "sci,sej->ijce", left_t, cols, preferred_element_type=standard_precision_type
        )
        outer = (
            (outer_sum / cnt[:, :, None, None])
            .astype(reduced_precision_type)
            .reshape(shard_lines * block, width * width)
        )
        update = (
            jnp.dot(outer, final_projection_matrix, preferred_element_type=standard_precision_type)
            + offset_vector
        ).astype(reduced_precision_type)
        update_buf = lax.dynamic_update_slice_in_dim(
            update_buf, update.reshape(shard_lines, block, pair_ch), start, 1
        )
        cot = lax.dynamic_slice_in_dim(couple_increment_cotangent, start, block, 1).reshape(
            shard_lines * block, pair_ch
        )
        d_acc = d_acc + jnp.einsum(
            "pk,pz->kz", outer, cot, preferred_element_type=standard_precision_type
        )
        d_o = jnp.einsum(
            "pz,kz->pk",
            cot,
            final_projection_matrix,
            preferred_element_type=standard_precision_type,
        )
        scaled = (d_o.reshape(shard_lines, block, width, width) / cnt[:, :, None, None]).astype(
            reduced_precision_type
        )
        left_acc = left_acc + jnp.einsum(
            "ijce,sej->sci", scaled, cols, preferred_element_type=standard_precision_type
        )
        part = jnp.einsum(
            "ijce,sci->sej", scaled, left_t, preferred_element_type=standard_precision_type
        )
        right_acc = lax.dynamic_update_slice_in_dim(right_acc, part, start, 2)
        return ((update_buf, d_acc, left_acc, right_acc), 0)

    right_shape = (homolog_total, width, total)
    init = (
        jnp.zeros((shard_lines, total, pair_ch), reduced_precision_type),
        jnp.zeros((width * width, pair_ch), standard_precision_type),
        jnp.zeros((homolog_total, width, shard_lines), standard_precision_type),
        jnp.zeros(right_shape, standard_precision_type),
    )
    carry, unused = lax.scan(column_step, init, jnp.arange(nblock, dtype=jnp.int32))
    couple_increment, d_acc, left_acc, right_acc = carry
    right_sum = lax.psum_scatter(right_acc, "row", scatter_dimension=2, tiled=True)
    left_grad = (left_acc * mask_float[:, None, :]).astype(reduced_precision_type)
    right_grad = (right_sum * mask_float[:, None, :]).astype(reduced_precision_type)
    part_left = jnp.einsum(
        "srm,scr->mc",
        standardized_reduced,
        left_grad,
        preferred_element_type=standard_precision_type,
    )
    part_right = jnp.einsum(
        "srm,scr->mc",
        standardized_reduced,
        right_grad,
        preferred_element_type=standard_precision_type,
    )
    part_bias = jnp.sum(couple_increment_cotangent, axis=(0, 1), dtype=standard_precision_type)
    sum_left, sum_right, sum_out, sum_bias = lax.psum(
        (part_left, part_right, d_acc, part_bias), "row"
    )
    standardized_derivative = jnp.einsum(
        "scr,mc->srm",
        left_grad,
        former_projection_matrix,
        preferred_element_type=standard_precision_type,
    )
    standardized_derivative = standardized_derivative + jnp.einsum(
        "scr,mc->srm",
        right_grad,
        latter_projection_matrix,
        preferred_element_type=standard_precision_type,
    )
    former_factor = jnp.mean(standardized_derivative, axis=-1, keepdims=True)
    latter_factor = jnp.mean(standardized_derivative * standardized_source, axis=-1, keepdims=True)
    homolog_embedding_derivative = (
        (standardized_derivative - former_factor - standardized_source * latter_factor)
        * reciprocal_spread
    ).astype(reduced_precision_type)
    return (
        couple_increment,
        homolog_embedding_derivative,
        sum_left / total,
        sum_right / total,
        sum_out / total,
        sum_bias / total,
    )


def solution(mesh):
    return jax.shard_map(
        body,
        mesh=mesh,
        in_specs=(
            P(None, ("grp", "row"), None),
            P(None, ("grp", "row")),
            P(),
            P(),
            P(),
            P(),
            P(("grp", "row"), None, None),
        ),
        out_specs=(
            P(("grp", "row"), None, None),
            P(None, ("grp", "row"), None),
            P("grp", None),
            P("grp", None),
            P("grp", None),
            P("grp"),
        ),
        check_vma=False,
    )
```

profile of v0, /device:TPU:0, one launch (start us, length us, event | category | flops | bytes accessed | tf_op | source)
XLA Modules:
  0.0 314.1 jit_solution(9784661913509772996)
XLA Ops:
  7.3 1.1 convert_reduce_fusion.1
  8.3 1.1 fusion.27
  10.8 1.2 fusion.16
  12.0 26.2 %all_gather.6 = bf16[32,32,128]{1,2,0:T(8,128)(2,1)S(1)} all-gather(bf16[32,32,8]{1,2,0:T(8,128)(2,1)S(1)} %fusion.16), channel_id=1, replica_groups=mesh['grp'=2,'row'=16] {'row'}, dimensions={2}, use_global_device_ids=true | all-gather | bytes 278528 | tf_op jit(solution)/shard_map/all_gather | solution.py:50
  38.2 17.5 %all_gather.7 = bf16[32,128]{0,1:T(8,128)(2,1)S(1)} all-gather(bf16[32,8]{0,1:T(8,128)(2,1)S(1)} %get-tuple-element.35), channel_id=1, replica_groups=mesh['grp'=2,'row'=16] {'row'}, dimensions={1}, use_global_device_ids=true | all-gather | bytes 8704 | tf_op jit(solution)/shard_map/all_gather | solution.py:51
  56.1 2.2 copy.54
  60.2 1.5 fusion.1
  61.8 1.7 divide_convert_fusion
  63.5 1.3 copy-done.2
  64.8 1.5 convolution_bitcast_fusion
  66.2 3.9 %copy.51 = f32[32,32,128]{1,0,2:T(8,128)} copy(f32[32,32,128]{2,0,1:T(8,128)} %convolution_bitcast_fusion) | data formatting | bytes 1048576 | tf_op jit(solution)/shard_map/while/body/eval_jaxpr/ijce,sci->sej/transpose | solution.py:98
  70.2 2.9 copy.47
  73.1 3.8 %convolution_bitcast_fusion.1 = f32[32,8,32]{2,0,1:T(8,128)S(1)} fusion(bf16[8,128,32,32]{1,2,0,3:T(8,128)(2,1)} %copy-done.2, bf16[32,32,128]{0,2,1:T(8,128)(2,1)} %copy.47), kind=kOutput, calls=%fused_computation.13 | convolution fusion | flops 67108864 | bytes 2392064 | tf_op jit(solution)/shard_map/while/body/eval_jaxpr/ijce,sej->sci/dot_general | solution.py:95
  76.9 0.9 convolution_bitcast_fusion.3
  78.8 1.5 fusion.10
  80.3 70.1 %all-reduce.4.cloned.1.call-done = f32[1024,128]{1,0:T(8,128)} async-done(((f32[1024,128]{1,0:T(8,128)}), f32[1024,128]{1,0:T(8,128)}) %all-reduce.4.cloned.1.call-update) | async-done | bytes 524304 | tf_op jit(solution)/shard_map/psum | solution.py:129
  150.4 1.9 broadcast_multiply_fusion
  152.3 63.9 %reduce-scatter.2.cloned.1.call-done = f32[32,32,8]{1,0,2:T(8,128)} async-done(((f32[32,32,128]{1,0,2:T(8,128)}), f32[32,32,8]{1,0,2:T(8,128)}) %reduce-scatter.2.cloned.1.call-update) | async-done | bytes 32784 | tf_op jit(solution)/shard_map/reduce_scatter | solution.py:113
  216.2 1.0 multiply_convert_fusion
  217.3 0.9 convolution_bitcast_fusion.2
  218.5 0.9 fusion.26
  219.3 85.7 %all-reduce.6.cloned.1.call-done = (f32[256,32]{0,1:T(8,128)}, f32[256,32]{0,1:T(8,128)}, f32[128]{0:T(128)}) async-done(((f32[256,32]{0,1:T(8,128)}, f32[256,32]{0,1:T(8,128)}, f32[128]{0:T(128)}), (f32[256,32]{0,1:T(8,128)}, f32[256,32]{0,1:T(8,128)}, f32[128]{0:T(128)})) %all-reduce.6.cloned.1.call-update) | async-done | bytes 66064 | tf_op jit(solution)/shard_map/psum | solution.py:129
  305.0 1.1 broadcast_multiply_fusion.6
  306.2 1.4 broadcast_multiply_fusion.1
  (56 shorter events, 5.0 us)
Async XLA Ops:
  7.2 54.6 %copy-start = (bf16[1024,128]{1,0:T(8,128)(2,1)S(1)}, bf16[1024,128]{1,0:T(8,128)(2,1)}, u32[]{:S(2)}) copy-start(bf16[1024,128]{1,0:T(8,128)(2,1)} %param.11) | copy-start | bytes 786436
  7.2 48.6 %copy-start.1 = (bf16[32,8,256]{2,1,0:T(8,128)(2,1)S(1)}, bf16[32,8,256]{2,1,0:T(8,128)(2,1)}, u32[]{:S(2)}) copy-start(bf16[32,8,256]{2,1,0:T(8,128)(2,1)} %param.7) | copy-start | bytes 393220
  7.2 48.5 %copy-start.14 = (s32[32,8]{0,1:T(8,128)S(1)}, s32[32,8]{0,1:T(8,128)}, u32[]{:S(2)}) copy-start(s32[32,8]{0,1:T(8,128)} %param.8) | copy-start | bytes 3076
  7.2 48.6 %copy-start.15 = (bf16[256,32]{0,1:T(8,128)(2,1)S(1)}, bf16[256,32]{0,1:T(8,128)(2,1)}, u32[]{:S(2)}) copy-start(bf16[256,32]{0,1:T(8,128)(2,1)} %param.9) | copy-start | bytes 49156
  7.2 143.2 %all-reduce.4.cloned.1.call-start = ((), (), s32[]{:S(2)}) async-start(), calls=%async_computation.2 | async-start | bytes 1048576 | tf_op jit(solution)/shard_map/psum | solution.py:129
  9.5 48.9 %copy-start.7 = (f32[32,8]{1,0:T(8,128)}, f32[32,8]{1,0:T(8,128)S(1)}, u32[]{:S(2)}) copy-start(f32[32,8]{1,0:T(8,128)S(1)} %add_rsqrt_fusion) | copy-start | bytes 3076
  10.2 0.6 copy-start.11
  10.8 47.5 %copy-start.9 = (f32[32,8]{1,0:T(8,128)}, f32[32,8]{1,0:T(8,128)S(1)}, u32[]{:S(2)}) copy-start(f32[32,8]{1,0:T(8,128)S(1)} %copy.42) | copy-start | bytes 3076
  55.8 2.7 copy-start.17
  56.1 2.4 copy-start.5
  59.2 1.0 copy-start.3
  61.7 154.6 %reduce-scatter.2.cloned.1.call-start = ((), (), s32[]{:S(2)}) async-start(), calls=%async_computation.1 | async-start | bytes 2228224 | tf_op jit(solution)/shard_map/reduce_scatter | solution.py:113
  61.7 3.0 copy-start.6
  63.5 1.3 copy-start.2
  70.1 234.9 %all-reduce.6.cloned.1.call-start = ((), (), s32[]{:S(2)}) async-start(), calls=%async_computation.3 | async-start | bytes 132096 | tf_op jit(solution)/shard_map/psum | solution.py:129
  73.1 3.8 %copy-start.8 = (f32[32,8]{1,0:T(8,128)S(1)}, f32[32,8]{1,0:T(8,128)}, u32[]{:S(2)}) copy-start(f32[32,8]{1,0:T(8,128)} %copy-done.7) | copy-start | bytes 3076
  73.1 3.8 %copy-start.10 = (f32[32,8]{1,0:T(8,128)S(1)}, f32[32,8]{1,0:T(8,128)}, u32[]{:S(2)}) copy-start(f32[32,8]{1,0:T(8,128)} %copy-done.9) | copy-start | bytes 3076
  73.1 4.7 %copy-start.4 = (bf16[8,128,128]{2,1,0:T(8,128)(2,1)S(1)}, bf16[8,128,128]{2,1,0:T(8,128)(2,1)}, u32[]{:S(2)}) copy-start(bf16[8,128,128]{2,1,0:T(8,128)(2,1)} %param.13) | copy-start | bytes 786436
  73.1 5.4 %copy-start.16 = (bf16[256,32]{0,1:T(8,128)(2,1)S(1)}, bf16[256,32]{0,1:T(8,128)(2,1)}, u32[]{:S(2)}) copy-start(bf16[256,32]{0,1:T(8,128)(2,1)} %param.9) | copy-start | bytes 49156
  73.1 5.6 %copy-start.18 = (f32[128]{0:T(128)S(1)}, f32[128]{0:T(128)}, u32[]{:S(2)}) copy-start(f32[128]{0:T(128)} %param.12) | copy-start | bytes 1540
  78.8 137.5 %copy-start.12 = (f32[32,8]{0,1:T(8,128)S(1)}, f32[32,8]{0,1:T(8,128)}, u32[]{:S(2)}) copy-start(f32[32,8]{0,1:T(8,128)} %copy-done.11) | copy-start | bytes 3076
  78.8 139.4 %copy-start.13 = (bf16[256,32]{0,1:T(8,128)(2,1)S(1)}, bf16[256,32]{0,1:T(8,128)(2,1)}, u32[]{:S(2)}) copy-start(bf16[256,32]{0,1:T(8,128)(2,1)} %param.10) | copy-start | bytes 49156
Sparse Core Ops, SparseCore 0:
  61.8 88.5 all-reduce.3
  154.2 62.0 reduce-scatter.1
  221.1 83.9 all-reduce.5
where the time goes:
time: 316 us; the launch traced here: 314 us
  waiting for transfers between devices  220 us (70%)
  blocking collectives  43.7 us (14%)
  matrix products  14.5 us (5%)
  between operations  14 us (4%)
  local copies, waits for them, and re-layouts  12.1 us (4%)
  other arithmetic  9.8 us (3%)
    psum x2, waiting for transfers between devices, body(): lax.psum((part_left, part_right, d_acc, part_bias), 'row')  156 us
    reduce_scatter x1, waiting for transfers between devices, body(): lax.psum_scatter(right_acc, 'row', scatter_dimension=2, tiled=True)  63.9 us
    all_gather x1, blocking collectives, body(): lax.all_gather(right_t, 'row', axis=2, tiled=True)  26.2 us
    all_gather x1, blocking collectives, body(): lax.all_gather(mask_float.astype(reduced_precision_type), 'row', axis=1,...  17.5 us
  transfers between devices with their start and end apart: 3, of which 3 were waited for; matrix products, arithmetic and copies ran while one was open for 6% of the time, Pallas kernels for 0%

commit v1 on v0

v1 whole, which is shorter than its diff:
```python
import functools

import jax
import jax.numpy as jnp
from jax import lax
from jax.experimental import pallas as pl
from jax.experimental.pallas import tpu as pltpu
from jax.sharding import PartitionSpec as P

F32 = jnp.float32
BF16 = jnp.bfloat16
LANES = 128
EPS = 1e-05
VMEM_LIMIT = 40 * 1024 * 1024


def dot(a, b, ca=1, cb=0):
    return lax.dot_general(a, b, (((ca,), (cb,)), ((), ())), preferred_element_type=F32)


def normalize(msa_ref):
    homologs, lines, depth = msa_ref.shape
    x = msa_ref[...].astype(F32).reshape(homologs * lines, depth)
    centred = x - jnp.mean(x, axis=-1, keepdims=True)
    spread = lax.rsqrt(jnp.mean(centred * centred, axis=-1, keepdims=True) + EPS)
    return centred * spread, spread


def pre_kernel(
    msa_ref, mask_ref, wf_ref, wl_ref, cot_ref,
    pay_ref, left_ref, right_ref, maskb_ref, low_ref,
    norm_scr, cot_scr,
):
    homologs, lines, depth = msa_ref.shape
    width = wf_ref.shape[1]
    rows = homologs * lines
    wide = width * homologs
    total, pair_ch = cot_ref.shape[1:]
    normed, _ = normalize(msa_ref)
    for h in range(depth // LANES):
        norm_scr[h] = normed[:, h * LANES : (h + 1) * LANES]
    low = jnp.concatenate(
        [
            jnp.concatenate(
                [norm_scr[h, pl.ds(k, homologs, stride=lines), :] for k in range(lines)], axis=0
            )
            for h in range(depth // LANES)
        ],
        axis=1,
    ).astype(BF16)
    low_ref[...] = low
    mask = mask_ref[...].astype(F32)
    cols = [jnp.broadcast_to(mask[:, k : k + 1], (homologs, LANES)) for k in range(lines)]
    for k in range(lines):
        maskb_ref[:, k * LANES : (k + 1) * LANES] = cols[k].astype(BF16)
    mask_rows = jnp.concatenate(cols, axis=0)
    left = (dot(low, wf_ref[...]) * mask_rows[:, :width]).astype(BF16)
    right = (dot(low, wl_ref[...]) * mask_rows[:, :width]).astype(BF16)
    left_ref[...] = left
    right_ref[...] = right
    spread_to = (
        lax.broadcasted_iota(jnp.int32, (width, wide), 1) // homologs
        == lax.broadcasted_iota(jnp.int32, (width, wide), 0)
    ).astype(BF16)
    own_tile = (
        lax.broadcasted_iota(jnp.int32, (homologs, LANES), 1) % homologs
        == lax.broadcasted_iota(jnp.int32, (homologs, LANES), 0)
    ).astype(F32)
    own_rows = jnp.concatenate([own_tile] * lines, axis=0)
    own = jnp.concatenate([own_rows] * (wide // LANES), axis=1)
    first = (lax.broadcasted_iota(jnp.int32, (rows, LANES), 1) < homologs).astype(F32)
    fold = (
        lax.broadcasted_iota(jnp.int32, (lines, rows), 1) // homologs
        == lax.broadcasted_iota(jnp.int32, (lines, rows), 0)
    ).astype(BF16)
    parts = [
        dot(fold, (dot(right, spread_to) * own).astype(BF16)),
        dot(fold, (dot(left, spread_to) * own).astype(BF16)),
        dot(fold, (mask_rows * own_rows * first).astype(BF16)),
    ]
    same = jnp.concatenate(parts, axis=1)
    same = jnp.concatenate([same, same], axis=0).astype(BF16)
    base = same.shape[1]
    cot_scr[...] = cot_ref[...].astype(F32).reshape(lines * total, pair_ch)
    for pair in range(total // (2 * lines)):
        at = pl.ds(pair * 2 * lines, 2 * lines)
        pay_ref[at, 0:base] = same
        for k in range(lines):
            block = jnp.concatenate(
                [
                    cot_scr[pl.ds((2 * pair + h) * lines + k, lines, stride=total), :]
                    for h in range(2)
                ],
                axis=0,
            )
            pay_ref[at, base + k * pair_ch : base + (k + 1) * pair_ch] = block.astype(BF16)


def mid_kernel(
    half_ref, got_ref, cot_ref, wout_ref, left_ref, right_ref, maskb_ref, low_ref,
    keep_ref, send_ref, grads_ref, inv_ref, wleft_ref,
    w_scr, p_scr, q_scr, half_scr,
):
    lines, total, pair_ch = cot_ref.shape
    homologs = maskb_ref.shape[0]
    width = left_ref.shape[1]
    wide = width * homologs
    rows = lines * homologs
    base = 2 * wide + LANES
    counts = dot(got_ref[:, 2 * wide : 2 * wide + homologs], maskb_ref[...]) + 1.0
    inv = 1.0 / counts
    inv_ref[...] = inv
    by_col = (got_ref[:, base:].astype(F32) * inv).astype(BF16)
    cot = [cot_ref[k].astype(F32) for k in range(lines)]
    by_row = jnp.concatenate(
        [(cot[k] * inv[:, k * LANES : (k + 1) * LANES]).astype(BF16) for k in range(lines)], axis=1
    )
    bias = functools.reduce(jnp.add, [jnp.sum(c, axis=0, keepdims=True) for c in cot])
    w_scr[...] = wout_ref[...].astype(F32)
    for e in range(width):
        wleft_ref[:, e * pair_ch : (e + 1) * pair_ch] = w_scr[
            pl.ds(e, width, stride=width), :
        ].astype(BF16)
    wright = jnp.concatenate(
        [wout_ref[c * width : (c + 1) * width, :] for c in range(width)], axis=1
    )
    group = LANES // homologs

    def contract(source, other, out):
        for g in range(wide // LANES):
            part = dot(source[:, g * LANES : (g + 1) * LANES], other, 0, 0).astype(BF16)
            for b in range(group):
                c = g * group + b
                for k in range(lines):
                    out[k * homologs : (k + 1) * homologs, c * pair_ch : (c + 1) * pair_ch] = part[
                        b * homologs : (b + 1) * homologs, k * pair_ch : (k + 1) * pair_ch
                    ]

    contract(got_ref[:, wide : 2 * wide], by_col, p_scr)
    contract(got_ref[:, 0:wide], by_row, q_scr)
    mask_rows = jnp.concatenate(
        [maskb_ref[:, k * LANES : k * LANES + width] for k in range(lines)], axis=0
    ).astype(F32)
    right_grad = (dot(p_scr[...], wright, 1, 1) * mask_rows).astype(BF16)
    left_grad = (dot(q_scr[...], wleft_ref[...], 1, 1) * mask_rows).astype(BF16)
    grads_ref[0] = left_grad
    grads_ref[1] = right_grad
    d_out = dot(right_ref[...], p_scr[...], 0, 0)
    part_left = dot(left_grad, low_ref[...], 0, 0)
    part_right = dot(right_grad, low_ref[...], 0, 0)
    half = width // 2
    for h in range(2):
        for c in range(half):
            at = (h * half + c) * pair_ch
            half_scr[h, c * width : (c + 1) * width, :] = d_out[:, at : at + pair_ch]
        at = half * width
        depth = low_ref.shape[1] // 2
        half_scr[h, at : at + width, :] = part_left[:, h * depth : (h + 1) * depth]
        half_scr[h, at + width : at + 2 * width, :] = part_right[:, h * depth : (h + 1) * depth]
        half_scr[h, at + 2 * width :, :] = jnp.broadcast_to(
            bias, (half_scr.shape[1] - at - 2 * width, pair_ch)
        )
    me = half_ref[0]
    keep_ref[...] = half_scr[me]
    send_ref[...] = half_scr[1 - me].astype(BF16)


def update_kernel(got_ref, inv_ref, left_ref, wleft_ref, offset_ref, out_ref, lw_scr):
    lines, total, pair_ch = out_ref.shape
    rows, width = left_ref.shape
    homologs = rows // lines
    wide = width * homologs
    for e in range(width):
        part = dot(left_ref[...], wleft_ref[:, e * pair_ch : (e + 1) * pair_ch]).astype(BF16)
        for k in range(lines):
            lw_scr[e * homologs : (e + 1) * homologs, k * pair_ch : (k + 1) * pair_ch] = part[
                k * homologs : (k + 1) * homologs, :
            ]
    update = dot(got_ref[:, 0:wide], lw_scr[...]) * inv_ref[...]
    for k in range(lines):
        out_ref[k] = (update[:, k * pair_ch : (k + 1) * pair_ch] + offset_ref[...]).astype(BF16)


def msa_kernel(msa_ref, grads_ref, wf_ref, wl_ref, out_ref, scr):
    homologs, lines, depth = msa_ref.shape
    derivative = dot(grads_ref[0], wf_ref[...], 1, 1) + dot(grads_ref[1], wl_ref[...], 1, 1)
    for h in range(depth // LANES):
        for k in range(lines):
            scr[h, pl.ds(k, homologs, stride=lines), :] = derivative[
                k * homologs : (k + 1) * homologs, h * LANES : (h + 1) * LANES
            ]
    derivative = jnp.concatenate([scr[h] for h in range(depth // LANES)], axis=1)
    normed, spread = normalize(msa_ref)
    one = jnp.mean(derivative, axis=-1, keepdims=True)
    two = jnp.mean(derivative * normed, axis=-1, keepdims=True)
    out = (derivative - one - normed * two) * spread
    out_ref[...] = out.reshape(homologs, lines, depth).astype(BF16)


def last_kernel(total, half_ref, own_ref, other_ref, out_ref, former_ref, latter_ref, offset_ref):
    me = half_ref[0]
    scale = 1.0 / total
    width = former_ref.shape[1]
    half = out_ref.shape[0] // 2
    own = own_ref[...].astype(F32) * scale
    other = other_ref[...].astype(F32) * scale
    out_ref[pl.ds(pl.multiple_of(me * half, half), half), :] = own[:half]
    out_ref[pl.ds(pl.multiple_of((1 - me) * half, half), half), :] = other[:half]
    own_part, other_part = own[half : half + 2 * width], other[half : half + 2 * width]
    first = me == 0
    both = jnp.concatenate(
        [
            jnp.where(first, own_part, other_part).T,
            jnp.where(first, other_part, own_part).T,
        ],
        axis=0,
    )
    former_ref[...] = both[:, :width]
    latter_ref[...] = both[:, width:]
    offset_ref[...] = own[half + 2 * width : half + 2 * width + 1]


def call(kernel, outs, scratch=(), smem=0, ins=0, flops=0):
    vmem = pl.BlockSpec(memory_space=pltpu.VMEM)
    return pl.pallas_call(
        kernel,
        out_shape=[jax.ShapeDtypeStruct(shape, kind) for shape, kind in outs],
        in_specs=[pl.BlockSpec(memory_space=pltpu.SMEM)] * smem + [vmem] * ins,
        out_specs=[vmem] * len(outs),
        scratch_shapes=[pltpu.VMEM(shape, kind) for shape, kind in scratch],
        compiler_params=pltpu.CompilerParams(vmem_limit_bytes=VMEM_LIMIT),
        cost_estimate=pl.CostEstimate(flops=flops, bytes_accessed=2 * 1024 * 1024, transcendentals=0),
    )


def body(size, msa, mask, wf, wl, wout, offset, cot):
    homologs, lines, depth = msa.shape
    width = wf.shape[1]
    total, pair_ch = cot.shape[1:]
    wide = width * homologs
    rows = lines * homologs
    span = 2 * wide + LANES + lines * pair_ch
    payload, left, right, maskb, low = call(
        pre_kernel,
        [
            ((total, span), BF16),
            ((rows, width), BF16),
            ((rows, width), BF16),
            ((homologs, lines * LANES), BF16),
            ((rows, depth), BF16),
        ],
        [((depth // LANES, rows, LANES), F32), ((lines * total, pair_ch), F32)],
        ins=5,
    )(msa, mask, wf, wl, cot)
    got = lax.all_to_all(payload.reshape(size, lines, span), "row", 0, 0).reshape(total, span)
    me = (lax.axis_index("row") % 2).astype(jnp.int32).reshape(1)
    length = width * width // 2 + 2 * width + 16
    keep, send, grads, inv, wleft = call(
        mid_kernel,
        [
            ((length, pair_ch), F32),
            ((length, pair_ch), BF16),
            ((2, rows, width), BF16),
            ((total, lines * LANES), F32),
            ((width, width * pair_ch), BF16),
        ],
        [
            ((width * width, pair_ch), F32),
            ((rows, width * pair_ch), BF16),
            ((rows, width * pair_ch), BF16),
            ((2, length, pair_ch), F32),
        ],
        smem=1,
        ins=7,
    )(me, got, cot, wout, left, right, maskb, low)

    def swap(x, step):
        return lax.ppermute(x, "row", [(i, i ^ step) for i in range(size)])

    sums = (keep + swap(send, 1).astype(F32)).astype(BF16)
    step = 2
    while step < size:
        sums = (sums.astype(F32) + swap(sums, step).astype(F32)).astype(BF16)
        step *= 2
    others = swap(sums, 1)
    d_out, d_former, d_latter, d_offset = call(
        functools.partial(last_kernel, total),
        [
            ((width * width, pair_ch), F32),
            ((depth, width), F32),
            ((depth, width), F32),
            ((1, pair_ch), F32),
        ],
        smem=1,
        ins=2,
    )(me, sums, others)
    (update,) = call(
        update_kernel,
        [((lines, total, pair_ch), BF16)],
        [((wide, lines * pair_ch), BF16)],
        ins=5,
        flops=2 * total * wide * lines * pair_ch,
    )(got, inv, left, wleft, offset.reshape(1, pair_ch))
    (d_msa,) = call(
        msa_kernel,
        [((homologs, lines, depth), BF16)],
        [((depth // LANES, rows, LANES), F32)],
        ins=4,
        flops=2 * rows * depth * 2 * width,
    )(msa, grads, wf, wl)
    return update, d_msa, d_former, d_latter, d_out, d_offset.reshape(pair_ch)


def solution(mesh):
    return jax.shard_map(
        functools.partial(body, mesh.shape["row"]),
        mesh=mesh,
        in_specs=(
            P(None, ("grp", "row"), None),
            P(None, ("grp", "row")),
            P(),
            P(),
            P(),
            P(),
            P(("grp", "row"), None, None),
        ),
        out_specs=(
            P(("grp", "row"), None, None),
            P(None, ("grp", "row"), None),
            P("grp", None),
            P("grp", None),
            P("grp", None),
            P("grp"),
        ),
        check_vma=False,
    )
```

time: 316 us -> 64.8 us (0.21)
  waiting for transfers between devices: 220 us -> 35 us
  blocking collectives: 43.7 us -> 0 us
  starting transfers between devices: 0.12 us -> 15 us
  matrix products: 14.5 us -> 0 us
  between operations: 14 us -> 0.72 us
  other arithmetic: 9.8 us -> 0.18 us
  Pallas kernels: 0 us -> 8.89 us
  local copies, waits for them, and re-layouts: 12.1 us -> 4.75 us
    psum x2 -> x0, waiting for transfers between devices: 156 us -> none  [body(): lax.psum((part_left, part_right, d_acc, part_bias), 'row')]
    reduce_scatter x1 -> x0, waiting for transfers between devices: 63.9 us -> none  [body(): lax.psum_scatter(right_acc, 'row', scatter_dimension=2, tiled=True)]
    all_gather x2 -> x0, blocking collectives: 43.7 us -> none  [the longest x1 26.2 us: body(): lax.all_gather(right_t, 'row', axis=2, tiled=True)]
    all_to_all x0 -> x1, waiting for transfers between devices: none -> 19.2 us  [body(): lax.all_to_all(payload.reshape(size, lines, span), 'row', 0, 0)]
    ppermute x0 -> x5, waiting for transfers between devices: none -> 15.7 us  [swap(): return lax.ppermute(x, 'row', [(i, i ^ step) for i in range(size)])]
    dot_general x13 -> x0, matrix products: 14.5 us -> none  [the longest x1 3.76 us: column_step(): jnp.einsum('ijce,sej->sci', scaled, cols, preferred_element_type=standard...]
    pallas_call x0 -> x5, Pallas kernels: none -> 8.89 us  [the longest x1 3.04 us: body(): call(mid_kernel, [((length, pair_ch), F32), ((length, pair_ch), BF16), ((...]
    all_to_all x0 -> x1, starting transfers between devices: none -> 7.49 us  [body(): lax.all_to_all(payload.reshape(size, lines, span), 'row', 0, 0)]
  transfers between devices with their start and end apart: 3 -> 6, of which waited for: 3 -> 5; matrix products, arithmetic and copies ran while one was open for 6% -> 0% of each run, Pallas kernels for 0% -> 4%
where the time goes in v1:
time: 64.8 us; the launch traced here: 64.5 us
  waiting for transfers between devices  35 us (54%)
  starting transfers between devices  15 us (23%)
  Pallas kernels  8.89 us (14%)
  local copies, waits for them, and re-layouts  4.75 us (7%)
  between operations  0.72 us (1%)
    all_to_all x1, waiting for transfers between devices, body(): lax.all_to_all(payload.reshape(size, lines, span), 'row', 0, 0)  19.2 us
    ppermute x5, waiting for transfers between devices, swap(): return lax.ppermute(x, 'row', [(i, i ^ step) for i in range(size)])  15.7 us
    all_to_all x1, starting transfers between devices, body(): lax.all_to_all(payload.reshape(size, lines, span), 'row', 0, 0)  7.49 us
    ppermute x5, starting transfers between devices, swap(): return lax.ppermute(x, 'row', [(i, i ^ step) for i in range(size)])  7.48 us
    unnamed x17, local copies, waits for them, and re-layouts  4.75 us
    pallas_call x1, Pallas kernels, body(): call(mid_kernel, [((length, pair_ch), F32), ((length, pair_ch), BF16), ((...  3.04 us
    pallas_call x1, Pallas kernels, body(): call(pre_kernel, [((total, span), BF16), ((rows, width), BF16), ((rows, w...  2.22 us
    pallas_call x1, Pallas kernels, body(): call(update_kernel, [((lines, total, pair_ch), BF16)], [((wide, lines * p...  1.67 us
  transfers between devices with their start and end apart: 6, of which 5 were waited for; matrix products, arithmetic and copies ran while one was open for 0% of the time, Pallas kernels for 4%

profile of v1, /device:TPU:0, one launch (start us, length us, event | category | flops | bytes accessed | tf_op | source)
XLA Modules:
  0.0 64.5 jit_solution(15769465254669231526)
XLA Ops:
  0.7 0.8 %copy.13.mask_ref = s32[32,8]{1,0:T(8,128)S(1)} copy(s32[32,8]{0,1:T(8,128)} %param.8) | data formatting | bytes 2048 | tf_op args[1]
  1.5 0.1 copy.14.wf_ref
  1.6 0.8 %copy.15.wl_ref = bf16[256,32]{1,0:T(8,128)(2,1)S(1)} copy(bf16[256,32]{0,1:T(8,128)(2,1)} %param.10) | data formatting | bytes 32768 | tf_op args[3]
  2.4 0.0 copy-start
  2.4 0.9 %copy-done = bf16[8,128,128]{2,1,0:T(8,128)(2,1)S(1)} copy-done((bf16[8,128,128]{2,1,0:T(8,128)(2,1)S(1)}, bf16[8,128,128]{2,1,0:T(8,128)(2,1)}, u32[]{:S(2)}) %copy-start) | copy-done | bytes 262168
  3.4 2.2 %shard_map.118 = (bf16[128,3200]{1,0:T(8,128)(2,1)}, bf16[256,32]{1,0:T(8,128)(2,1)S(1)}, bf16[256,32]{1,0:T(8,128)(2,1)S(1)}, bf16[32,1024]{1,0:T(8,128)(2,1)S(1)}, bf16[256,256]{1,0:T(8,128)(2,1)S(1)}) custom-call(bf16[32,8,256]{2,1,0:T(8,128)(2,1)S(1)} %copy-done.2, s32[32,8]{1,0:T(8,128)S(1)} %copy.13.mask_ref, bf16[256,32]{1,0:T(8,128)(2,1)S(1)} %copy.14.wf_ref, ...), custom_call_target="tpu_custom_call" | custom-call | bytes 2097152 | tf_op jit(solution)/shard_map/pallas_call | solution.py:243
  5.6 7.5 %all-to-all-start = ((bf16[16,8,3200]{2,1,0:T(8,128)(2,1)}), bf16[16,8,3200]{2,1,0:T(8,128)(2,1)S(1)}, u32[]{:S(2)}, u32[]{:S(2)}) async-start(bf16[16,8,3200]{2,1,0:T(8,128)(2,1)} %bitcast), calls=%async_computation | async-start | bytes 1638400 | tf_op jit(solution)/shard_map/all_to_all | solution.py:255
  13.1 19.2 %all-to-all-done = bf16[16,8,3200]{2,1,0:T(8,128)(2,1)S(1)} async-done(((bf16[16,8,3200]{2,1,0:T(8,128)(2,1)}), bf16[16,8,3200]{2,1,0:T(8,128)(2,1)S(1)}, u32[]{:S(2)}, u32[]{:S(2)}) %all-to-all-start) | async-done | bytes 819232 | tf_op jit(solution)/shard_map/all_to_all | solution.py:255
  32.3 3.0 %shard_map.119 = (f32[592,128]{1,0:T(8,128)S(1)}, bf16[592,128]{1,0:T(8,128)(2,1)S(1)}, bf16[2,256,32]{2,1,0:T(8,128)(2,1)S(1)}, f32[128,1024]{1,0:T(8,128)S(1)}, bf16[32,4096]{1,0:T(8,128)(2,1)S(1)}) custom-call(s32[1]{0:T(128)} %bitcast.2.half_ref, bf16[128,3200]{1,0:T(8,128)(2,1)S(1)} %bitcast.5, bf16[8,128,128]{2,1,0:T(8,128)(2,1)S(1)} %copy-done.1, ...), custom_call_target="tpu_custom_call" | custom-call | bytes 2097152 | tf_op jit(solution)/shard_map/pallas_call | solution.py:258
  35.4 0.4 collective-permute-start
  35.7 1.1 %collective-permute-done = bf16[592,128]{1,0:T(8,128)(2,1)S(1)} collective-permute-done((bf16[592,128]{1,0:T(8,128)(2,1)S(1)}, bf16[592,128]{1,0:T(8,128)(2,1)S(1)}, u32[]{:S(2)}, u32[]{:S(2)}) %collective-permute-start) | collective-permute-done | bytes 151584 | tf_op jit(solution)/shard_map/ppermute | solution.py:278
  36.9 1.7 %collective-permute-start.1 = (bf16[592,128]{1,0:T(8,128)(2,1)S(1)}, bf16[592,128]{1,0:T(8,128)(2,1)S(1)}, u32[]{:S(2)}, u32[]{:S(2)}) collective-permute-start(bf16[592,128]{1,0:T(8,128)(2,1)S(1)} %add_convert_fusion.3), channel_id=1, source_target_pairs={{0,2},{1,3},{2,0},{3,1},{4,6},{5,7},{6,4},{7,5},{8,10},{9,11},{10,... | collective-permute-start | bytes 454664 | tf_op jit(solution)/shard_map/ppermute | solution.py:278
  38.6 4.5 %collective-permute-done.1 = bf16[592,128]{1,0:T(8,128)(2,1)S(1)} collective-permute-done((bf16[592,128]{1,0:T(8,128)(2,1)S(1)}, bf16[592,128]{1,0:T(8,128)(2,1)S(1)}, u32[]{:S(2)}, u32[]{:S(2)}) %collective-permute-start.1) | collective-permute-done | bytes 151584 | tf_op jit(solution)/shard_map/ppermute | solution.py:278
  43.1 2.8 %collective-permute-start.2 = (bf16[592,128]{1,0:T(8,128)(2,1)S(1)}, bf16[592,128]{1,0:T(8,128)(2,1)S(1)}, u32[]{:S(2)}, u32[]{:S(2)}) collective-permute-start(bf16[592,128]{1,0:T(8,128)(2,1)S(1)} %add_convert_fusion.2), channel_id=1, source_target_pairs={{0,4},{1,5},{2,6},{3,7},{4,0},{5,1},{6,2},{7,3},{8,12},{9,13},{10,... | collective-permute-start | bytes 454664 | tf_op jit(solution)/shard_map/ppermute | solution.py:278
  46.0 3.7 %collective-permute-done.2 = bf16[592,128]{1,0:T(8,128)(2,1)S(1)} collective-permute-done((bf16[592,128]{1,0:T(8,128)(2,1)S(1)}, bf16[592,128]{1,0:T(8,128)(2,1)S(1)}, u32[]{:S(2)}, u32[]{:S(2)}) %collective-permute-start.2) | collective-permute-done | bytes 151584 | tf_op jit(solution)/shard_map/ppermute | solution.py:278
  49.6 2.5 %collective-permute-start.3 = (bf16[592,128]{1,0:T(8,128)(2,1)S(1)}, bf16[592,128]{1,0:T(8,128)(2,1)S(1)}, u32[]{:S(2)}, u32[]{:S(2)}) collective-permute-start(bf16[592,128]{1,0:T(8,128)(2,1)S(1)} %add_convert_fusion.1), channel_id=1, source_target_pairs={{0,8},{1,9},{2,10},{3,11},{4,12},{5,13},{6,14},{7,15},{8,0},{9,1},... | collective-permute-start | bytes 454664 | tf_op jit(solution)/shard_map/ppermute | solution.py:278
  52.2 6.5 %collective-permute-done.3 = bf16[592,128]{1,0:T(8,128)(2,1)S(1)} collective-permute-done((bf16[592,128]{1,0:T(8,128)(2,1)S(1)}, bf16[592,128]{1,0:T(8,128)(2,1)S(1)}, u32[]{:S(2)}, u32[]{:S(2)}) %collective-permute-start.3) | collective-permute-done | bytes 151584 | tf_op jit(solution)/shard_map/ppermute | solution.py:278
  58.7 0.1 collective-permute-start.4
  58.8 1.0 %shard_map.121 = bf16[32,8,256]{2,1,0:T(8,128)(2,1)} custom-call(bf16[32,8,256]{2,1,0:T(8,128)(2,1)S(1)} %copy-done.2, bf16[2,256,32]{2,1,0:T(8,128)(2,1)S(1)} %get-tuple-element.27.grads_ref, bf16[256,32]{1,0:T(8,128)(2,1)S(1)} %copy.14.wf_ref, bf16[256,32]{1,0:T(8,128)(2,1)S(1)} %copy.15.wl_ref), custom_call_target="tpu_custom_call" | custom-call | flops 8388608 | bytes 2097152 | tf_op jit(solution)/shard_map/pallas_call | solution.py:304
  59.8 0.7 %copy-done.4 = f32[128]{0:T(128)S(1)} copy-done((f32[128]{0:T(128)S(1)}, f32[128]{0:T(128)}, u32[]{:S(2)}) %copy-start.4) | copy-done | bytes 536
  60.5 1.7 %shard_map.120 = bf16[8,128,128]{2,1,0:T(8,128)(2,1)} custom-call(bf16[128,3200]{1,0:T(8,128)(2,1)S(1)} %bitcast.6, f32[128,1024]{1,0:T(8,128)S(1)} %get-tuple-element.25.inv_ref, bf16[256,32]{1,0:T(8,128)(2,1)S(1)} %get-tuple-element.21.left_ref, bf16[32,4096]{1,0:T(8,128)(2,1)S(1)} %get-tuple-element.26.wleft_ref, f32[1,128]{1,0:T(1,128)S(1)} %bitcast.7), custom_call_target="tpu_custom_call" | custom-call | flops 268435456 | bytes 2097152 | tf_op jit(solution)/shard_map/pallas_call | solution.py:297
  62.2 0.9 %shard_map.122 = (f32[1024,128]{1,0:T(8,128)}, f32[256,32]{1,0:T(8,128)S(1)}, f32[256,32]{1,0:T(8,128)S(1)}, f32[1,128]{1,0:T(1,128)}) custom-call(s32[1]{0:T(128)} %bitcast.2.half_ref, bf16[592,128]{1,0:T(8,128)(2,1)S(1)} %add_convert_fusion.own_ref, bf16[592,128]{1,0:T(8,128)(2,1)S(1)} %collective-permute-done.4.other_ref), custom_call_target="tpu_custom_call" | custom-call | bytes 2097152 | tf_op jit(solution)/shard_map/pallas_call | solution.py:286
  63.1 0.7 %copy.18 = f32[256,32]{0,1:T(8,128)} copy(f32[256,32]{1,0:T(8,128)S(1)} %get-tuple-element.36) | data formatting | bytes 65536
  63.8 0.7 %copy.19 = f32[256,32]{0,1:T(8,128)} copy(f32[256,32]{1,0:T(8,128)S(1)} %get-tuple-element.37) | data formatting | bytes 65536
  (14 shorter events, 0.2 us)
Async XLA Ops:
  0.6 0.8 %copy-start.5 = (bf16[256,32]{0,1:T(8,128)(2,1)S(1)}, bf16[256,32]{0,1:T(8,128)(2,1)}, u32[]{:S(2)}) copy-start(bf16[256,32]{0,1:T(8,128)(2,1)} %param.9) | copy-start | bytes 49156
  0.6 1.8 %copy-start.2 = (bf16[32,8,256]{2,1,0:T(8,128)(2,1)S(1)}, bf16[32,8,256]{2,1,0:T(8,128)(2,1)}, u32[]{:S(2)}) copy-start(bf16[32,8,256]{2,1,0:T(8,128)(2,1)} %msa_ref.3) | copy-start | bytes 393220
  2.4 1.0 %copy-start = (bf16[8,128,128]{2,1,0:T(8,128)(2,1)S(1)}, bf16[8,128,128]{2,1,0:T(8,128)(2,1)}, u32[]{:S(2)}) copy-start(bf16[8,128,128]{2,1,0:T(8,128)(2,1)} %cot_ref.3) | copy-start | bytes 786436
  5.6 26.7 %copy-start.1 = (bf16[8,128,128]{2,1,0:T(8,128)(2,1)S(1)}, bf16[8,128,128]{2,1,0:T(8,128)(2,1)}, u32[]{:S(2)}) copy-start(bf16[8,128,128]{2,1,0:T(8,128)(2,1)} %cot_ref.3) | copy-start | bytes 786436
  5.6 26.7 %copy-start.3 = (bf16[1024,128]{1,0:T(8,128)(2,1)S(1)}, bf16[1024,128]{1,0:T(8,128)(2,1)}, u32[]{:S(2)}) copy-start(bf16[1024,128]{1,0:T(8,128)(2,1)} %wout_ref.1) | copy-start | bytes 786436
  5.6 26.7 %all-to-all-start = ((bf16[16,8,3200]{2,1,0:T(8,128)(2,1)}), bf16[16,8,3200]{2,1,0:T(8,128)(2,1)S(1)}, u32[]{:S(2)}, u32[]{:S(2)}) async-start(bf16[16,8,3200]{2,1,0:T(8,128)(2,1)} %bitcast), calls=%async_computation | async-start | bytes 1638400 | tf_op jit(solution)/shard_map/all_to_all | solution.py:255
  35.4 1.4 %collective-permute-start = (bf16[592,128]{1,0:T(8,128)(2,1)S(1)}, bf16[592,128]{1,0:T(8,128)(2,1)S(1)}, u32[]{:S(2)}, u32[]{:S(2)}) collective-permute-start(bf16[592,128]{1,0:T(8,128)(2,1)S(1)} %get-tuple-element.29), channel_id=1, source_target_pairs={{0,1},{1,0},{2,3},{3,2},{4,5},{5,4},{6,7},{7,6},{8,9},{9,8},{10,11... | collective-permute-start | bytes 454664 | tf_op jit(solution)/shard_map/ppermute | solution.py:278
  36.9 6.2 %collective-permute-start.1 = (bf16[592,128]{1,0:T(8,128)(2,1)S(1)}, bf16[592,128]{1,0:T(8,128)(2,1)S(1)}, u32[]{:S(2)}, u32[]{:S(2)}) collective-permute-start(bf16[592,128]{1,0:T(8,128)(2,1)S(1)} %add_convert_fusion.3), channel_id=1, source_target_pairs={{0,2},{1,3},{2,0},{3,1},{4,6},{5,7},{6,4},{7,5},{8,10},{9,11},{10,... | collective-permute-start | bytes 454664 | tf_op jit(solution)/shard_map/ppermute | solution.py:278
  43.1 6.5 %collective-permute-start.2 = (bf16[592,128]{1,0:T(8,128)(2,1)S(1)}, bf16[592,128]{1,0:T(8,128)(2,1)S(1)}, u32[]{:S(2)}, u32[]{:S(2)}) collective-permute-start(bf16[592,128]{1,0:T(8,128)(2,1)S(1)} %add_convert_fusion.2), channel_id=1, source_target_pairs={{0,4},{1,5},{2,6},{3,7},{4,0},{5,1},{6,2},{7,3},{8,12},{9,13},{10,... | collective-permute-start | bytes 454664 | tf_op jit(solution)/shard_map/ppermute | solution.py:278
  49.6 9.0 %collective-permute-start.3 = (bf16[592,128]{1,0:T(8,128)(2,1)S(1)}, bf16[592,128]{1,0:T(8,128)(2,1)S(1)}, u32[]{:S(2)}, u32[]{:S(2)}) collective-permute-start(bf16[592,128]{1,0:T(8,128)(2,1)S(1)} %add_convert_fusion.1), channel_id=1, source_target_pairs={{0,8},{1,9},{2,10},{3,11},{4,12},{5,13},{6,14},{7,15},{8,0},{9,1},... | collective-permute-start | bytes 454664 | tf_op jit(solution)/shard_map/ppermute | solution.py:278
  58.7 3.4 %collective-permute-start.4 = (bf16[592,128]{1,0:T(8,128)(2,1)S(1)}, bf16[592,128]{1,0:T(8,128)(2,1)S(1)}, u32[]{:S(2)}, u32[]{:S(2)}) collective-permute-start(bf16[592,128]{1,0:T(8,128)(2,1)S(1)} %add_convert_fusion.own_ref), channel_id=1, source_target_pairs={{0,1},{1,0},{2,3},{3,2},{4,5},{5,4},{6,7},{7,6},{8,9},{9,8},{10,11... | collective-permute-start | bytes 454664 | tf_op jit(solution)/shard_map/ppermute | solution.py:278
  59.8 0.7 %copy-start.4 = (f32[128]{0:T(128)S(1)}, f32[128]{0:T(128)}, u32[]{:S(2)}) copy-start(f32[128]{0:T(128)} %param.12) | copy-start | bytes 1540

commit v2 on v1

--- a/solution.py
+++ b/solution.py
@@ -27,15 +27,31 @@
 
 
 def pre_kernel(
-    msa_ref, mask_ref, wf_ref, wl_ref, cot_ref,
-    pay_ref, left_ref, right_ref, maskb_ref, low_ref,
-    norm_scr, cot_scr,
+    half_ref, msa_hbm, mask_hbm, wf_hbm, wl_hbm, cot_hbm,
+    pay_ref, cot_out_ref, left_ref, right_ref, maskb_ref, low_ref,
+    msa_ref, mask_ref, wf_ref, wl_ref, cot_ref, norm_scr, cot_scr, sems,
 ):
+    copies = [
+        pltpu.make_async_copy(source, target, sems.at[n])
+        for n, (source, target) in enumerate(
+            [
+                (msa_hbm, msa_ref),
+                (wf_hbm, wf_ref),
+                (wl_hbm, wl_ref),
+                (mask_hbm, mask_ref),
+                (cot_hbm, cot_ref),
+            ]
+        )
+    ]
+    for copy in copies:
+        copy.start()
     homologs, lines, depth = msa_ref.shape
-    width = wf_ref.shape[1]
+    width = wf_ref.shape[0]
     rows = homologs * lines
     wide = width * homologs
     total, pair_ch = cot_ref.shape[1:]
+    even = half_ref[0] == 0
+    copies[0].wait()
     normed, _ = normalize(msa_ref)
     for h in range(depth // LANES):
         norm_scr[h] = normed[:, h * LANES : (h + 1) * LANES]
@@ -49,13 +65,15 @@
         axis=1,
     ).astype(BF16)
     low_ref[...] = low
-    mask = mask_ref[...].astype(F32)
+    for copy in copies[1:4]:
+        copy.wait()
+    mask = mask_ref[...].astype(F32).T
     cols = [jnp.broadcast_to(mask[:, k : k + 1], (homologs, LANES)) for k in range(lines)]
     for k in range(lines):
         maskb_ref[:, k * LANES : (k + 1) * LANES] = cols[k].astype(BF16)
     mask_rows = jnp.concatenate(cols, axis=0)
-    left = (dot(low, wf_ref[...]) * mask_rows[:, :width]).astype(BF16)
-    right = (dot(low, wl_ref[...]) * mask_rows[:, :width]).astype(BF16)
+    left = (dot(low, wf_ref[...], 1, 1) * mask_rows[:, :width]).astype(BF16)
+    right = (dot(low, wl_ref[...], 1, 1) * mask_rows[:, :width]).astype(BF16)
     left_ref[...] = left
     right_ref[...] = right
     spread_to = (
@@ -73,31 +91,47 @@
         lax.broadcasted_iota(jnp.int32, (lines, rows), 1) // homologs
         == lax.broadcasted_iota(jnp.int32, (lines, rows), 0)
     ).astype(BF16)
-    parts = [
-        dot(fold, (dot(right, spread_to) * own).astype(BF16)),
-        dot(fold, (dot(left, spread_to) * own).astype(BF16)),
-        dot(fold, (mask_rows * own_rows * first).astype(BF16)),
-    ]
-    same = jnp.concatenate(parts, axis=1)
+    same = jnp.concatenate(
+        [
+            dot(fold, (dot(right, spread_to) * own).astype(BF16)),
+            dot(fold, (dot(left, spread_to) * own).astype(BF16)),
+            dot(fold, (mask_rows * own_rows * first).astype(BF16)),
+        ],
+        axis=1,
+    )
     same = jnp.concatenate([same, same], axis=0).astype(BF16)
     base = same.shape[1]
+    cols = lines * pair_ch
+    copies[4].wait()
     cot_scr[...] = cot_ref[...].astype(F32).reshape(lines * total, pair_ch)
-    for pair in range(total // (2 * lines)):
-        at = pl.ds(pair * 2 * lines, 2 * lines)
-        pay_ref[at, 0:base] = same
+    peers = total // (2 * lines)
+    for q in range(0, peers, 2):
+        at = pl.ds(q * lines, 2 * lines)
+        pay_ref[at, cols : cols + base] = same
         for k in range(lines):
-            block = jnp.concatenate(
+            block = [
                 [
-                    cot_scr[pl.ds((2 * pair + h) * lines + k, lines, stride=total), :]
-                    for h in range(2)
-                ],
-                axis=0,
-            )
-            pay_ref[at, base + k * pair_ch : base + (k + 1) * pair_ch] = block.astype(BF16)
+                    cot_scr[pl.ds((2 * (q + h) + core) * lines + k, lines, stride=total), :]
+                    for core in range(2)
+                ]
+                for h in range(2)
+            ]
+            mine = jnp.concatenate([jnp.where(even, b[0], b[1]) for b in block], axis=0)
+            yours = jnp.concatenate([jnp.where(even, b[1], b[0]) for b in block], axis=0)
+            pay_ref[at, k * pair_ch : (k + 1) * pair_ch] = mine.astype(BF16)
+            to = cols + base + k * pair_ch
+            pay_ref[at, to : to + pair_ch] = yours.astype(BF16)
+    for k in range(lines):
+        tiles = [
+            cot_scr[k * total + n * lines : k * total + (n + 1) * lines, :] for n in range(2 * peers)
+        ]
+        mine = [jnp.where(even, tiles[2 * q], tiles[2 * q + 1]) for q in range(peers)]
+        yours = [jnp.where(even, tiles[2 * q + 1], tiles[2 * q]) for q in range(peers)]
+        cot_out_ref[k] = jnp.concatenate(mine + yours, axis=0).astype(BF16)
 
 
 def mid_kernel(
-    half_ref, got_ref, cot_ref, wout_ref, left_ref, right_ref, maskb_ref, low_ref,
+    half_ref, near_ref, far_ref, cot_ref, wout_ref, left_ref, right_ref, maskb_ref, low_ref,
     keep_ref, send_ref, grads_ref, inv_ref, wleft_ref,
     w_scr, p_scr, q_scr, half_scr,
 ):
@@ -106,11 +140,19 @@
     width = left_ref.shape[1]
     wide = width * homologs
     rows = lines * homologs
-    base = 2 * wide + LANES
-    counts = dot(got_ref[:, 2 * wide : 2 * wide + homologs], maskb_ref[...]) + 1.0
+    cols = lines * pair_ch
+    base = cols + 2 * wide + LANES
+
+    def both(start, size):
+        return jnp.concatenate(
+            [near_ref[:, start : start + size], far_ref[:, start : start + size]], axis=0
+        )
+
+    counts = dot(both(cols + 2 * wide, LANES)[:, :homologs], maskb_ref[...]) + 1.0
     inv = 1.0 / counts
     inv_ref[...] = inv
-    by_col = (got_ref[:, base:].astype(F32) * inv).astype(BF16)
+    by_col = jnp.concatenate([near_ref[:, :cols], far_ref[:, base:]], axis=0)
+    by_col = (by_col.astype(F32) * inv).astype(BF16)
     cot = [cot_ref[k].astype(F32) for k in range(lines)]
     by_row = jnp.concatenate(
         [(cot[k] * inv[:, k * LANES : (k + 1) * LANES]).astype(BF16) for k in range(lines)], axis=1
@@ -136,8 +178,8 @@
                         b * homologs : (b + 1) * homologs, k * pair_ch : (k + 1) * pair_ch
                     ]
 
-    contract(got_ref[:, wide : 2 * wide], by_col, p_scr)
-    contract(got_ref[:, 0:wide], by_row, q_scr)
+    contract(both(cols + wide, wide), by_col, p_scr)
+    contract(both(cols, wide), by_row, q_scr)
     mask_rows = jnp.concatenate(
         [maskb_ref[:, k * LANES : k * LANES + width] for k in range(lines)], axis=0
     ).astype(F32)
@@ -165,8 +207,12 @@
     send_ref[...] = half_scr[1 - me].astype(BF16)
 
 
-def update_kernel(got_ref, inv_ref, left_ref, wleft_ref, offset_ref, out_ref, lw_scr):
+def update_kernel(
+    half_ref, near_ref, far_ref, inv_ref, left_ref, wleft_ref, offset_ref, out_ref, lw_scr
+):
     lines, total, pair_ch = out_ref.shape
+    cols = lines * pair_ch
+    even = half_ref[0] == 0
     rows, width = left_ref.shape
     homologs = rows // lines
     wide = width * homologs
@@ -176,14 +222,23 @@
             lw_scr[e * homologs : (e + 1) * homologs, k * pair_ch : (k + 1) * pair_ch] = part[
                 k * homologs : (k + 1) * homologs, :
             ]
-    update = dot(got_ref[:, 0:wide], lw_scr[...]) * inv_ref[...]
+    right = jnp.concatenate(
+        [near_ref[:, cols : cols + wide], far_ref[:, cols : cols + wide]], axis=0
+    )
+    update = dot(right, lw_scr[...]) * inv_ref[...]
     for k in range(lines):
-        out_ref[k] = (update[:, k * pair_ch : (k + 1) * pair_ch] + offset_ref[...]).astype(BF16)
+        line = update[:, k * pair_ch : (k + 1) * pair_ch] + offset_ref[...]
+        tiles = [line[n * lines : (n + 1) * lines] for n in range(total // lines)]
+        near, far = tiles[: len(tiles) // 2], tiles[len(tiles) // 2 :]
+        order = []
+        for a, b in zip(near, far):
+            order += [jnp.where(even, a, b), jnp.where(even, b, a)]
+        out_ref[k] = jnp.concatenate(order, axis=0).astype(BF16)
 
 
 def msa_kernel(msa_ref, grads_ref, wf_ref, wl_ref, out_ref, scr):
     homologs, lines, depth = msa_ref.shape
-    derivative = dot(grads_ref[0], wf_ref[...], 1, 1) + dot(grads_ref[1], wl_ref[...], 1, 1)
+    derivative = dot(grads_ref[0], wf_ref[...]) + dot(grads_ref[1], wl_ref[...])
     for h in range(depth // LANES):
         for k in range(lines):
             scr[h, pl.ds(k, homologs, stride=lines), :] = derivative[
@@ -200,7 +255,7 @@
 def last_kernel(total, half_ref, own_ref, other_ref, out_ref, former_ref, latter_ref, offset_ref):
     me = half_ref[0]
     scale = 1.0 / total
-    width = former_ref.shape[1]
+    width = former_ref.shape[0]
     half = out_ref.shape[0] // 2
     own = own_ref[...].astype(F32) * scale
     other = other_ref[...].astype(F32) * scale
@@ -209,26 +264,25 @@
     own_part, other_part = own[half : half + 2 * width], other[half : half + 2 * width]
     first = me == 0
     both = jnp.concatenate(
-        [
-            jnp.where(first, own_part, other_part).T,
-            jnp.where(first, other_part, own_part).T,
-        ],
-        axis=0,
-    )
-    former_ref[...] = both[:, :width]
-    latter_ref[...] = both[:, width:]
+        [jnp.where(first, own_part, other_part), jnp.where(first, other_part, own_part)], axis=1
+    )
+    former_ref[...] = both[:width]
+    latter_ref[...] = both[width:]
     offset_ref[...] = own[half + 2 * width : half + 2 * width + 1]
 
 
-def call(kernel, outs, scratch=(), smem=0, ins=0, flops=0):
+def call(kernel, outs, scratch=(), smem=0, ins=0, flops=0, away=0, limit=VMEM_LIMIT):
     vmem = pl.BlockSpec(memory_space=pltpu.VMEM)
     return pl.pallas_call(
         kernel,
         out_shape=[jax.ShapeDtypeStruct(shape, kind) for shape, kind in outs],
-        in_specs=[pl.BlockSpec(memory_space=pltpu.SMEM)] * smem + [vmem] * ins,
+        in_specs=[pl.BlockSpec(memory_space=pltpu.SMEM)] * smem
+        + [pl.BlockSpec(memory_space=pltpu.HBM)] * away
+        + [vmem] * ins,
         out_specs=[vmem] * len(outs),
-        scratch_shapes=[pltpu.VMEM(shape, kind) for shape, kind in scratch],
-        compiler_params=pltpu.CompilerParams(vmem_limit_bytes=VMEM_LIMIT),
+        scratch_shapes=[pltpu.VMEM(shape, kind) for shape, kind in scratch]
+        + [pltpu.SemaphoreType.DMA((away,))] * (away > 0),
+        compiler_params=pltpu.CompilerParams(vmem_limit_bytes=limit),
         cost_estimate=pl.CostEstimate(flops=flops, bytes_accessed=2 * 1024 * 1024, transcendentals=0),
     )
 
@@ -239,21 +293,39 @@
     total, pair_ch = cot.shape[1:]
     wide = width * homologs
     rows = lines * homologs
-    span = 2 * wide + LANES + lines * pair_ch
-    payload, left, right, maskb, low = call(
+    cols = lines * pair_ch
+    span = 2 * wide + LANES + 2 * cols
+    wf, wl = wf.T, wl.T
+    me = (lax.axis_index("row") % 2).astype(jnp.int32).reshape(1)
+    given = [msa, mask.T, wf, wl, cot]
+    payload, cot, left, right, maskb, low = call(
         pre_kernel,
         [
-            ((total, span), BF16),
+            ((total // 2, span), BF16),
+            ((lines, total, pair_ch), BF16),
             ((rows, width), BF16),
             ((rows, width), BF16),
             ((homologs, lines * LANES), BF16),
             ((rows, depth), BF16),
         ],
-        [((depth // LANES, rows, LANES), F32), ((lines * total, pair_ch), F32)],
-        ins=5,
-    )(msa, mask, wf, wl, cot)
-    got = lax.all_to_all(payload.reshape(size, lines, span), "row", 0, 0).reshape(total, span)
-    me = (lax.axis_index("row") % 2).astype(jnp.int32).reshape(1)
+        [(x.shape, x.dtype) for x in given]
+        + [((depth // LANES, rows, LANES), F32), ((lines * total, pair_ch), F32)],
+        smem=1,
+        away=len(given),
+        limit=None,
+    )(me, *given)
+
+    def swap(x, step):
+        return lax.ppermute(x, "row", [(i, i ^ step) for i in range(size)])
+
+    near = lax.all_to_all(
+        payload.reshape(size // 2, lines, span),
+        "row",
+        0,
+        0,
+        axis_index_groups=[list(range(core, size, 2)) for core in range(2)],
+    ).reshape(total // 2, span)
+    far = swap(near, 1)
     length = width * width // 2 + 2 * width + 16
     keep, send, grads, inv, wleft = call(
         mid_kernel,
@@ -271,44 +343,60 @@
             ((2, length, pair_ch), F32),
         ],
         smem=1,
-        ins=7,
-    )(me, got, cot, wout, left, right, maskb, low)
-
-    def swap(x, step):
-        return lax.ppermute(x, "row", [(i, i ^ step) for i in range(size)])
-
-    sums = (keep + swap(send, 1).astype(F32)).astype(BF16)
+        ins=8,
+    )(me, near, far, cot, wout, left, right, maskb, low)
+
+    def add(x, y):
+        return (x.astype(F32) + y.astype(F32)).astype(BF16)
+
+    def make_update():
+        (out,) = call(
+            update_kernel,
+            [((lines, total, pair_ch), BF16)],
+            [((wide, cols), BF16)],
+            smem=1,
+            ins=6,
+            flops=2 * total * wide * cols,
+        )(me, near, far, inv, left, wleft, offset.reshape(1, pair_ch))
+        return out
+
+    def make_d_msa():
+        (out,) = call(
+            msa_kernel,
+            [((homologs, lines, depth), BF16)],
+            [((depth // LANES, rows, LANES), F32)],
+            ins=4,
+            flops=2 * rows * depth * 2 * width,
+        )(msa, grads, wf, wl)
+        return out
+
+    work = [make_d_msa, make_update]
+    done = []
+    sums = add(keep, swap(send, 1))
     step = 2
     while step < size:
-        sums = (sums.astype(F32) + swap(sums, step).astype(F32)).astype(BF16)
+        got = swap(sums, step)
+        if work:
+            out = work.pop(0)()
+            got, out = lax.optimization_barrier((got, out))
+            done.append(out)
+        sums = add(sums, got)
         step *= 2
+    done += [make() for make in work]
+    d_msa, update = done
     others = swap(sums, 1)
     d_out, d_former, d_latter, d_offset = call(
         functools.partial(last_kernel, total),
         [
             ((width * width, pair_ch), F32),
-            ((depth, width), F32),
-            ((depth, width), F32),
+            ((width, depth), F32),
+            ((width, depth), F32),
             ((1, pair_ch), F32),
         ],
         smem=1,
         ins=2,
     )(me, sums, others)
-    (update,) = call(
-        update_kernel,
-        [((lines, total, pair_ch), BF16)],
-        [((wide, lines * pair_ch), BF16)],
-        ins=5,
-        flops=2 * total * wide * lines * pair_ch,
-    )(got, inv, left, wleft, offset.reshape(1, pair_ch))
-    (d_msa,) = call(
-        msa_kernel,
-        [((homologs, lines, depth), BF16)],
-        [((depth // LANES, rows, LANES), F32)],
-        ins=4,
-        flops=2 * rows * depth * 2 * width,
-    )(msa, grads, wf, wl)
-    return update, d_msa, d_former, d_latter, d_out, d_offset.reshape(pair_ch)
+    return update, d_msa, d_former.T, d_latter.T, d_out, d_offset.reshape(pair_ch)
 
 
 def solution(mesh):

time: 64.8 us -> 55.8 us (0.86)
  blocking collectives: 0 us -> 23.1 us
  waiting for transfers between devices: 35 us -> 18.6 us
  starting transfers between devices: 15 us -> 2.26 us
  local copies, waits for them, and re-layouts: 4.75 us -> 0.85 us
  Pallas kernels: 8.89 us -> 9.84 us
    all_to_all x0 -> x1, blocking collectives: none -> 23.1 us  [body(): lax.all_to_all(payload.reshape(size // 2, lines, span), 'row', 0, 0, axis...]
    all_to_all x1 -> x0, waiting for transfers between devices: 19.2 us -> none  [body(): lax.all_to_all(payload.reshape(size, lines, span), 'row', 0, 0)]
    all_to_all x1 -> x0, starting transfers between devices: 7.49 us -> none  [body(): lax.all_to_all(payload.reshape(size, lines, span), 'row', 0, 0)]
    ppermute x5 -> x6, starting transfers between devices: 7.48 us -> 2.26 us  [swap(): return lax.ppermute(x, 'row', [(i, i ^ step) for i in range(size)])]
    unnamed x17 -> x20, local copies, waits for them, and re-layouts: 4.75 us -> 0.85 us
    ppermute x5 -> x6, waiting for transfers between devices: 15.7 us -> 18.6 us  [swap(): return lax.ppermute(x, 'row', [(i, i ^ step) for i in range(size)])]
    pallas_call x3, Pallas kernels: 4.93 us -> 5.93 us  [the longest x1 3.24 us: body(): call(pre_kernel, [((total // 2, span), BF16), ((lines, total, pair_ch), B...]
  transfers between devices with their start and end apart: 6 -> 6, of which waited for: 5 -> 6; matrix products, arithmetic and copies ran while one was open for 0% -> 0% of each run, Pallas kernels for 4% -> 5%
where the time goes in v2:
time: 55.8 us; the launch traced here: 55.6 us
  blocking collectives  23.1 us (41%)
  waiting for transfers between devices  18.6 us (33%)
  Pallas kernels  9.84 us (18%)
  starting transfers between devices  2.26 us (4%)
  local copies, waits for them, and re-layouts  0.85 us (2%)
  between operations  0.77 us (1%)
    all_to_all x1, blocking collectives, body(): lax.all_to_all(payload.reshape(size // 2, lines, span), 'row', 0, 0, axis...  23.1 us
    ppermute x6, waiting for transfers between devices, swap(): return lax.ppermute(x, 'row', [(i, i ^ step) for i in range(size)])  18.6 us
    pallas_call x1, Pallas kernels, body(): call(pre_kernel, [((total // 2, span), BF16), ((lines, total, pair_ch), B...  3.24 us
    pallas_call x1, Pallas kernels, body(): call(mid_kernel, [((length, pair_ch), F32), ((length, pair_ch), BF16), ((...  3.08 us
    ppermute x6, starting transfers between devices, swap(): return lax.ppermute(x, 'row', [(i, i ^ step) for i in range(size)])  2.26 us
    pallas_call x1, Pallas kernels, make_update(): call(update_kernel, [((lines, total, pair_ch), BF16)], [((wide, cols), BF...  1.67 us
  transfers between devices with their start and end apart: 6, of which 6 were waited for; matrix products, arithmetic and copies ran while one was open for 0% of the time, Pallas kernels for 5%

profile of v2, /device:TPU:0, one launch (start us, length us, event | category | flops | bytes accessed | tf_op | source)
XLA Modules:
  0.0 55.6 jit_solution(3317083572986067720)
XLA Ops:
  0.6 3.2 %shard_map.118 = (bf16[64,4224]{1,0:T(8,128)(2,1)}, bf16[8,128,128]{2,1,0:T(8,128)(2,1)}, bf16[256,32]{1,0:T(8,128)(2,1)}, bf16[256,32]{1,0:T(8,128)(2,1)}, bf16...) custom-call(s32[1]{0:T(128)} %bitcast.half_ref, bf16[32,8,256]{2,1,0:T(8,128)(2,1)} %msa_ref.1, s32[8,32]{1,0:T(8,128)} %bitcast.19, ...), custom_call_target="tpu_custom_call" | custom-call | bytes 2097152 | tf_op jit(solution)/shard_map/pallas_call | solution.py:301
  3.9 0.0 copy-start.1
  3.9 0.0 copy-start.2
  3.9 0.0 copy-start.3
  3.9 0.0 copy-start.4
  4.0 23.1 %all_to_all.5 = bf16[8,8,4224]{2,1,0:T(8,128)(2,1)S(1)} all-to-all(bf16[8,8,4224]{2,1,0:T(8,128)(2,1)} %bitcast.18), channel_id=1, replica_groups={{0,2,4,6,8,10,12,14},{1,3,5,7,9,11,13,15},{16,18,20,22,24,26,28,30},{17..., dimensions={0} | all-to-all | bytes 1081344 | tf_op jit(solution)/shard_map/all_to_all | solution.py:321
  27.1 0.0 collective-permute-start
  27.1 1.9 %collective-permute-done.far_ref = bf16[64,4224]{1,0:T(8,128)(2,1)S(1)} collective-permute-done((bf16[64,4224]{1,0:T(8,128)(2,1)S(1)}, bf16[64,4224]{1,0:T(8,128)(2,1)S(1)}, u32[]{:S(2)}, u32[]{:S(2)}) %collective-permute-start) | collective-permute-done | bytes 540704 | tf_op jit(solution)/shard_map/ppermute | solution.py:319
  29.0 3.1 %shard_map.119 = (f32[592,128]{1,0:T(8,128)S(1)}, bf16[592,128]{1,0:T(8,128)(2,1)S(1)}, bf16[2,256,32]{2,1,0:T(8,128)(2,1)S(1)}, f32[128,1024]{1,0:T(8,128)S(1)}, bf16[32,4096]{1,0:T(8,128)(2,1)S(1)}) custom-call(s32[1]{0:T(128)} %bitcast.half_ref, bf16[64,4224]{1,0:T(8,128)(2,1)S(1)} %bitcast.11, bf16[64,4224]{1,0:T(8,128)(2,1)S(1)} %collective-permute-done.far_ref, ...), custom_call_target="tpu_custom_call" | custom-call | bytes 2097152 | tf_op jit(solution)/shard_map/pallas_call | solution.py:330
  32.1 0.2 collective-permute-start.1
  32.3 1.3 %collective-permute-done.1 = bf16[592,128]{1,0:T(8,128)(2,1)S(1)} collective-permute-done((bf16[592,128]{1,0:T(8,128)(2,1)S(1)}, bf16[592,128]{1,0:T(8,128)(2,1)S(1)}, u32[]{:S(2)}, u32[]{:S(2)}) %collective-permute-start.1) | collective-permute-done | bytes 151584 | tf_op jit(solution)/shard_map/ppermute | solution.py:319
  33.6 0.7 %collective-permute-start.2 = (bf16[592,128]{1,0:T(8,128)(2,1)S(1)}, bf16[592,128]{1,0:T(8,128)(2,1)S(1)}, u32[]{:S(2)}, u32[]{:S(2)}) collective-permute-start(bf16[592,128]{1,0:T(8,128)(2,1)S(1)} %add_convert_fusion.3), channel_id=1, source_target_pairs={{0,2},{1,3},{2,0},{3,1},{4,6},{5,7},{6,4},{7,5},{8,10},{9,11},{10,... | collective-permute-start | bytes 454664 | tf_op jit(solution)/shard_map/ppermute | solution.py:319
  34.3 0.2 copy-done
  34.5 1.0 %shard_map.120 = bf16[32,8,256]{2,1,0:T(8,128)(2,1)} custom-call(bf16[32,8,256]{2,1,0:T(8,128)(2,1)S(1)} %copy-done, bf16[2,256,32]{2,1,0:T(8,128)(2,1)S(1)} %get-tuple-element.33.grads_ref, bf16[32,256]{1,0:T(8,128)(2,1)S(1)} %bitcast.14, bf16[32,256]{1,0:T(8,128)(2,1)S(1)} %bitcast.16), custom_call_target="tpu_custom_call" | custom-call | flops 8388608 | bytes 2097152 | tf_op jit(solution)/shard_map/pallas_call | solution.py:364
  35.5 4.2 %collective-permute-done.2 = bf16[592,128]{1,0:T(8,128)(2,1)S(1)} collective-permute-done((bf16[592,128]{1,0:T(8,128)(2,1)S(1)}, bf16[592,128]{1,0:T(8,128)(2,1)S(1)}, u32[]{:S(2)}, u32[]{:S(2)}) %collective-permute-start.2) | collective-permute-done | bytes 151584 | tf_op jit(solution)/shard_map/ppermute | solution.py:319
  39.7 0.7 %collective-permute-start.3 = (bf16[592,128]{1,0:T(8,128)(2,1)S(1)}, bf16[592,128]{1,0:T(8,128)(2,1)S(1)}, u32[]{:S(2)}, u32[]{:S(2)}) collective-permute-start(bf16[592,128]{1,0:T(8,128)(2,1)S(1)} %add_convert_fusion.2), channel_id=1, source_target_pairs={{0,4},{1,5},{2,6},{3,7},{4,0},{5,1},{6,2},{7,3},{8,12},{9,13},{10,... | collective-permute-start | bytes 454664 | tf_op jit(solution)/shard_map/ppermute | solution.py:319
  40.4 0.7 %copy-done.9 = f32[128]{0:T(128)S(1)} copy-done((f32[128]{0:T(128)S(1)}, f32[128]{0:T(128)}, u32[]{:S(2)}) %copy-start.9) | copy-done | bytes 536
  41.1 1.7 %shard_map.121 = bf16[8,128,128]{2,1,0:T(8,128)(2,1)} custom-call(s32[1]{0:T(128)} %bitcast.half_ref, bf16[64,4224]{1,0:T(8,128)(2,1)S(1)} %bitcast.12, bf16[64,4224]{1,0:T(8,128)(2,1)S(1)} %collective-permute-done.far_ref, f32[128,1024]{1,0:T(8,128)S(1)} %get-tuple-element.35.inv_ref, bf16[256,32]{1,0:T(8,128)(2,1)S(1)} %copy-done.1, ...), custom_call_target="tpu_custom_call" | custom-call | flops 268435456 | bytes 2097152 | tf_op jit(solution)/shard_map/pallas_call | solution.py:353
  42.7 2.2 %collective-permute-done.3 = bf16[592,128]{1,0:T(8,128)(2,1)S(1)} collective-permute-done((bf16[592,128]{1,0:T(8,128)(2,1)S(1)}, bf16[592,128]{1,0:T(8,128)(2,1)S(1)}, u32[]{:S(2)}, u32[]{:S(2)}) %collective-permute-start.3) | collective-permute-done | bytes 151584 | tf_op jit(solution)/shard_map/ppermute | solution.py:319
  45.0 0.6 %collective-permute-start.4 = (bf16[592,128]{1,0:T(8,128)(2,1)S(1)}, bf16[592,128]{1,0:T(8,128)(2,1)S(1)}, u32[]{:S(2)}, u32[]{:S(2)}) collective-permute-start(bf16[592,128]{1,0:T(8,128)(2,1)S(1)} %add_convert_fusion.1), channel_id=1, source_target_pairs={{0,8},{1,9},{2,10},{3,11},{4,12},{5,13},{6,14},{7,15},{8,0},{9,1},... | collective-permute-start | bytes 454664 | tf_op jit(solution)/shard_map/ppermute | solution.py:319
  45.7 7.6 %collective-permute-done.4 = bf16[592,128]{1,0:T(8,128)(2,1)S(1)} collective-permute-done((bf16[592,128]{1,0:T(8,128)(2,1)S(1)}, bf16[592,128]{1,0:T(8,128)(2,1)S(1)}, u32[]{:S(2)}, u32[]{:S(2)}) %collective-permute-start.4) | collective-permute-done | bytes 151584 | tf_op jit(solution)/shard_map/ppermute | solution.py:319
  53.3 0.1 collective-permute-start.5
  53.4 1.4 %collective-permute-done.5.other_ref = bf16[592,128]{1,0:T(8,128)(2,1)S(1)} collective-permute-done((bf16[592,128]{1,0:T(8,128)(2,1)S(1)}, bf16[592,128]{1,0:T(8,128)(2,1)S(1)}, u32[]{:S(2)}, u32[]{:S(2)}) %collective-permute-start.5) | collective-permute-done | bytes 151584 | tf_op jit(solution)/shard_map/ppermute | solution.py:319
  54.7 0.8 %shard_map.122 = (f32[1024,128]{1,0:T(8,128)}, f32[32,256]{1,0:T(8,128)}, f32[32,256]{1,0:T(8,128)}, f32[1,128]{1,0:T(1,128)}) custom-call(s32[1]{0:T(128)} %bitcast.half_ref, bf16[592,128]{1,0:T(8,128)(2,1)S(1)} %add_convert_fusion.own_ref, bf16[592,128]{1,0:T(8,128)(2,1)S(1)} %collective-permute-done.5.other_ref), custom_call_target="tpu_custom_call" | custom-call | bytes 2097152 | tf_op jit(solution)/shard_map/pallas_call | solution.py:388
  (18 shorter events, 0.2 us)
Async XLA Ops:
  3.9 25.1 %copy-start.1 = (bf16[256,32]{1,0:T(8,128)(2,1)S(1)}, bf16[256,32]{1,0:T(8,128)(2,1)}, u32[]{:S(2)}) copy-start(bf16[256,32]{1,0:T(8,128)(2,1)} %get-tuple-element.27.left_ref) | copy-start | bytes 49156
  3.9 25.1 %copy-start.2 = (bf16[1024,128]{1,0:T(8,128)(2,1)S(1)}, bf16[1024,128]{1,0:T(8,128)(2,1)}, u32[]{:S(2)}) copy-start(bf16[1024,128]{1,0:T(8,128)(2,1)} %wout_ref.1) | copy-start | bytes 786436
  3.9 25.1 %copy-start.3 = (bf16[8,128,128]{2,1,0:T(8,128)(2,1)S(1)}, bf16[8,128,128]{2,1,0:T(8,128)(2,1)}, u32[]{:S(2)}) copy-start(bf16[8,128,128]{2,1,0:T(8,128)(2,1)} %get-tuple-element.26.cot_ref) | copy-start | bytes 786436
  3.9 25.1 %copy-start.4 = (bf16[256,256]{1,0:T(8,128)(2,1)S(1)}, bf16[256,256]{1,0:T(8,128)(2,1)}, u32[]{:S(2)}) copy-start(bf16[256,256]{1,0:T(8,128)(2,1)} %get-tuple-element.30.low_ref) | copy-start | bytes 393220
  3.9 25.1 %copy-start.5 = (bf16[256,32]{1,0:T(8,128)(2,1)S(1)}, bf16[256,32]{1,0:T(8,128)(2,1)}, u32[]{:S(2)}) copy-start(bf16[256,32]{1,0:T(8,128)(2,1)} %get-tuple-element.28.right_ref) | copy-start | bytes 49156
  3.9 25.1 %copy-start.6 = (bf16[32,1024]{1,0:T(8,128)(2,1)S(1)}, bf16[32,1024]{1,0:T(8,128)(2,1)}, u32[]{:S(2)}) copy-start(bf16[32,1024]{1,0:T(8,128)(2,1)} %get-tuple-element.29.maskb_ref) | copy-start | bytes 196612
  27.1 1.9 %collective-permute-start = (bf16[64,4224]{1,0:T(8,128)(2,1)S(1)}, bf16[64,4224]{1,0:T(8,128)(2,1)S(1)}, u32[]{:S(2)}, u32[]{:S(2)}) collective-permute-start(bf16[64,4224]{1,0:T(8,128)(2,1)S(1)} %bitcast.10), channel_id=1, source_target_pairs={{0,1},{1,0},{2,3},{3,2},{4,5},{5,4},{6,7},{7,6},{8,9},{9,8},{10,11... | collective-permute-start | bytes 1622024 | tf_op jit(solution)/shard_map/ppermute | solution.py:319
  32.1 1.4 %collective-permute-start.1 = (bf16[592,128]{1,0:T(8,128)(2,1)S(1)}, bf16[592,128]{1,0:T(8,128)(2,1)S(1)}, u32[]{:S(2)}, u32[]{:S(2)}) collective-permute-start(bf16[592,128]{1,0:T(8,128)(2,1)S(1)} %get-tuple-element.32), channel_id=1, source_target_pairs={{0,1},{1,0},{2,3},{3,2},{4,5},{5,4},{6,7},{7,6},{8,9},{9,8},{10,11... | collective-permute-start | bytes 454664 | tf_op jit(solution)/shard_map/ppermute | solution.py:319
  33.6 0.9 %copy-start = (bf16[32,8,256]{2,1,0:T(8,128)(2,1)S(1)}, bf16[32,8,256]{2,1,0:T(8,128)(2,1)}, u32[]{:S(2)}) copy-start(bf16[32,8,256]{2,1,0:T(8,128)(2,1)} %msa_ref.1) | copy-start | bytes 393220
  33.6 0.9 %copy-start.7 = (bf16[256,32]{0,1:T(8,128)(2,1)S(1)}, bf16[256,32]{0,1:T(8,128)(2,1)}, u32[]{:S(2)}) copy-start(bf16[256,32]{0,1:T(8,128)(2,1)} %param.9) | copy-start | bytes 49156
  33.6 0.9 %copy-start.8 = (bf16[256,32]{0,1:T(8,128)(2,1)S(1)}, bf16[256,32]{0,1:T(8,128)(2,1)}, u32[]{:S(2)}) copy-start(bf16[256,32]{0,1:T(8,128)(2,1)} %param.10) | copy-start | bytes 49156
  33.6 6.1 %collective-permute-start.2 = (bf16[592,128]{1,0:T(8,128)(2,1)S(1)}, bf16[592,128]{1,0:T(8,128)(2,1)S(1)}, u32[]{:S(2)}, u32[]{:S(2)}) collective-permute-start(bf16[592,128]{1,0:T(8,128)(2,1)S(1)} %add_convert_fusion.3), channel_id=1, source_target_pairs={{0,2},{1,3},{2,0},{3,1},{4,6},{5,7},{6,4},{7,5},{8,10},{9,11},{10,... | collective-permute-start | bytes 454664 | tf_op jit(solution)/shard_map/ppermute | solution.py:319
  39.7 5.3 %collective-permute-start.3 = (bf16[592,128]{1,0:T(8,128)(2,1)S(1)}, bf16[592,128]{1,0:T(8,128)(2,1)S(1)}, u32[]{:S(2)}, u32[]{:S(2)}) collective-permute-start(bf16[592,128]{1,0:T(8,128)(2,1)S(1)} %add_convert_fusion.2), channel_id=1, source_target_pairs={{0,4},{1,5},{2,6},{3,7},{4,0},{5,1},{6,2},{7,3},{8,12},{9,13},{10,... | collective-permute-start | bytes 454664 | tf_op jit(solution)/shard_map/ppermute | solution.py:319
  40.4 0.7 %copy-start.9 = (f32[128]{0:T(128)S(1)}, f32[128]{0:T(128)}, u32[]{:S(2)}) copy-start(f32[128]{0:T(128)} %param.12) | copy-start | bytes 1540
  45.0 8.2 %collective-permute-start.4 = (bf16[592,128]{1,0:T(8,128)(2,1)S(1)}, bf16[592,128]{1,0:T(8,128)(2,1)S(1)}, u32[]{:S(2)}, u32[]{:S(2)}) collective-permute-start(bf16[592,128]{1,0:T(8,128)(2,1)S(1)} %add_convert_fusion.1), channel_id=1, source_target_pairs={{0,8},{1,9},{2,10},{3,11},{4,12},{5,13},{6,14},{7,15},{8,0},{9,1},... | collective-permute-start | bytes 454664 | tf_op jit(solution)/shard_map/ppermute | solution.py:319
  53.3 1.4 %collective-permute-start.5 = (bf16[592,128]{1,0:T(8,128)(2,1)S(1)}, bf16[592,128]{1,0:T(8,128)(2,1)S(1)}, u32[]{:S(2)}, u32[]{:S(2)}) collective-permute-start(bf16[592,128]{1,0:T(8,128)(2,1)S(1)} %add_convert_fusion.own_ref), channel_id=1, source_target_pairs={{0,1},{1,0},{2,3},{3,2},{4,5},{5,4},{6,7},{7,6},{8,9},{9,8},{10,11... | collective-permute-start | bytes 454664 | tf_op jit(solution)/shard_map/ppermute | solution.py:319

commit v3 on v2

--- a/solution.py
+++ b/solution.py
@@ -132,7 +132,7 @@
 
 def mid_kernel(
     half_ref, near_ref, far_ref, cot_ref, wout_ref, left_ref, right_ref, maskb_ref, low_ref,
-    keep_ref, send_ref, grads_ref, inv_ref, wleft_ref,
+    keep_a_ref, keep_b_ref, send_a_ref, send_b_ref, grads_ref, inv_ref, wleft_ref,
     w_scr, p_scr, q_scr, half_scr,
 ):
     lines, total, pair_ch = cot_ref.shape
@@ -203,8 +203,11 @@
             bias, (half_scr.shape[1] - at - 2 * width, pair_ch)
         )
     me = half_ref[0]
-    keep_ref[...] = half_scr[me]
-    send_ref[...] = half_scr[1 - me].astype(BF16)
+    cut = keep_a_ref.shape[0]
+    keep_a_ref[...] = half_scr[me, :cut]
+    keep_b_ref[...] = half_scr[me, cut:]
+    send_a_ref[...] = half_scr[1 - me, :cut].astype(BF16)
+    send_b_ref[...] = half_scr[1 - me, cut:].astype(BF16)
 
 
 def update_kernel(
@@ -252,13 +255,16 @@
     out_ref[...] = out.reshape(homologs, lines, depth).astype(BF16)
 
 
-def last_kernel(total, half_ref, own_ref, other_ref, out_ref, former_ref, latter_ref, offset_ref):
+def last_kernel(
+    total, half_ref, own_a_ref, own_b_ref, other_a_ref, other_b_ref,
+    out_ref, former_ref, latter_ref, offset_ref,
+):
     me = half_ref[0]
     scale = 1.0 / total
     width = former_ref.shape[0]
     half = out_ref.shape[0] // 2
-    own = own_ref[...].astype(F32) * scale
-    other = other_ref[...].astype(F32) * scale
+    own = jnp.concatenate([own_a_ref[...], own_b_ref[...]], axis=0).astype(F32) * scale
+    other = jnp.concatenate([other_a_ref[...], other_b_ref[...]], axis=0).astype(F32) * scale
     out_ref[pl.ds(pl.multiple_of(me * half, half), half), :] = own[:half]
     out_ref[pl.ds(pl.multiple_of((1 - me) * half, half), half), :] = other[:half]
     own_part, other_part = own[half : half + 2 * width], other[half : half + 2 * width]
@@ -326,12 +332,14 @@
         axis_index_groups=[list(range(core, size, 2)) for core in range(2)],
     ).reshape(total // 2, span)
     far = swap(near, 1)
-    length = width * width // 2 + 2 * width + 16
-    keep, send, grads, inv, wleft = call(
+    length = width * width // 2 + 2 * width + 32
+    keep_a, keep_b, send_a, send_b, grads, inv, wleft = call(
         mid_kernel,
         [
-            ((length, pair_ch), F32),
-            ((length, pair_ch), BF16),
+            ((length // 2, pair_ch), F32),
+            ((length // 2, pair_ch), F32),
+            ((length // 2, pair_ch), BF16),
+            ((length // 2, pair_ch), BF16),
             ((2, rows, width), BF16),
             ((total, lines * LANES), F32),
             ((width, width * pair_ch), BF16),
@@ -372,19 +380,17 @@
 
     work = [make_d_msa, make_update]
     done = []
-    sums = add(keep, swap(send, 1))
-    step = 2
-    while step < size:
-        got = swap(sums, step)
+    steps = [1 << n for n in range(1, size.bit_length() - 1)]
+    sums_a, sums_b = add(keep_a, swap(send_a, 1)), add(keep_b, swap(send_b, 1))
+    for step_a, step_b in zip(steps, steps[1:] + steps[:1]):
+        got_a, got_b = swap(sums_a, step_a), swap(sums_b, step_b)
         if work:
             out = work.pop(0)()
-            got, out = lax.optimization_barrier((got, out))
+            got_a, got_b, out = lax.optimization_barrier((got_a, got_b, out))
             done.append(out)
-        sums = add(sums, got)
-        step *= 2
+        sums_a, sums_b = add(sums_a, got_a), add(sums_b, got_b)
     done += [make() for make in work]
     d_msa, update = done
-    others = swap(sums, 1)
     d_out, d_former, d_latter, d_offset = call(
         functools.partial(last_kernel, total),
         [
@@ -394,8 +400,8 @@
             ((1, pair_ch), F32),
         ],
         smem=1,
-        ins=2,
-    )(me, sums, others)
+        ins=4,
+    )(me, sums_a, sums_b, swap(sums_a, 1), swap(sums_b, 1))
     return update, d_msa, d_former.T, d_latter.T, d_out, d_offset.reshape(pair_ch)
 
 

time: 55.8 us -> 53.6 us (0.961)
  waiting for transfers between devices: 18.6 us -> 11 us
  starting transfers between devices: 2.26 us -> 7.37 us
    ppermute x6 -> x11, waiting for transfers between devices: 18.6 us -> 11 us  [swap(): return lax.ppermute(x, 'row', [(i, i ^ step) for i in range(size)])]
    ppermute x6 -> x11, starting transfers between devices: 2.26 us -> 7.37 us  [swap(): return lax.ppermute(x, 'row', [(i, i ^ step) for i in range(size)])]
  transfers between devices with their start and end apart: 6 -> 11, of which waited for: 6 -> 8; matrix products, arithmetic and copies ran while one was open for 0% -> 0% of each run, Pallas kernels for 5% -> 5%
where the time goes in v3:
time: 53.6 us; the launch traced here: 53.3 us
  blocking collectives  23.1 us (43%)
  waiting for transfers between devices  11 us (21%)
  Pallas kernels  9.89 us (18%)
  starting transfers between devices  7.37 us (14%)
  local copies, waits for them, and re-layouts  0.98 us (2%)
  between operations  0.81 us (2%)
    all_to_all x1, blocking collectives, body(): lax.all_to_all(payload.reshape(size // 2, lines, span), 'row', 0, 0, axis...  23.1 us
    ppermute x11, waiting for transfers between devices, swap(): return lax.ppermute(x, 'row', [(i, i ^ step) for i in range(size)])  11 us
    ppermute x11, starting transfers between devices, swap(): return lax.ppermute(x, 'row', [(i, i ^ step) for i in range(size)])  7.37 us
    pallas_call x1, Pallas kernels, body(): call(pre_kernel, [((total // 2, span), BF16), ((lines, total, pair_ch), B...  3.25 us
    pallas_call x1, Pallas kernels, body(): call(mid_kernel, [((length // 2, pair_ch), F32), ((length // 2, pair_ch),...  3.08 us
    pallas_call x1, Pallas kernels, make_update(): call(update_kernel, [((lines, total, pair_ch), BF16)], [((wide, cols), BF...  1.7 us
  transfers between devices with their start and end apart: 11, of which 8 were waited for; matrix products, arithmetic and copies ran while one was open for 0% of the time, Pallas kernels for 5%

profile of v3, /device:TPU:0, one launch (start us, length us, event | category | flops | bytes accessed | tf_op | source)
XLA Modules:
  0.0 53.3 jit_solution(14384939021763027699)
XLA Ops:
  0.6 3.2 %shard_map.118 = (bf16[64,4224]{1,0:T(8,128)(2,1)}, bf16[8,128,128]{2,1,0:T(8,128)(2,1)}, bf16[256,32]{1,0:T(8,128)(2,1)}, bf16[256,32]{1,0:T(8,128)(2,1)}, bf16...) custom-call(s32[1]{0:T(128)} %bitcast.half_ref, bf16[32,8,256]{2,1,0:T(8,128)(2,1)} %msa_ref.1, s32[8,32]{1,0:T(8,128)} %bitcast.19, ...), custom_call_target="tpu_custom_call" | custom-call | bytes 2097152 | tf_op jit(solution)/shard_map/pallas_call | solution.py:307
  4.0 23.1 %all_to_all.5 = bf16[8,8,4224]{2,1,0:T(8,128)(2,1)S(1)} all-to-all(bf16[8,8,4224]{2,1,0:T(8,128)(2,1)} %bitcast.18), channel_id=1, replica_groups={{0,2,4,6,8,10,12,14},{1,3,5,7,9,11,13,15},{16,18,20,22,24,26,28,30},{17..., dimensions={0} | all-to-all | bytes 1081344 | tf_op jit(solution)/shard_map/all_to_all | solution.py:327
  27.1 1.9 %collective-permute-done.far_ref = bf16[64,4224]{1,0:T(8,128)(2,1)S(1)} collective-permute-done((bf16[64,4224]{1,0:T(8,128)(2,1)S(1)}, bf16[64,4224]{1,0:T(8,128)(2,1)S(1)}, u32[]{:S(2)}, u32[]{:S(2)}) %collective-permute-start) | collective-permute-done | bytes 540704 | tf_op jit(solution)/shard_map/ppermute | solution.py:325
  29.1 3.1 %shard_map.119 = (f32[304,128]{1,0:T(8,128)S(1)}, f32[304,128]{1,0:T(8,128)S(1)}, bf16[304,128]{1,0:T(8,128)(2,1)S(1)}, bf16[304,128]{1,0:T(8,128)(2,1)S(1)}, bf...) custom-call(s32[1]{0:T(128)} %bitcast.half_ref, ...), custom_call_target="tpu_custom_call" | custom-call | bytes 2097152 | tf_op jit(solution)/shard_map/pallas_call | solution.py:336
  32.3 0.4 collective-permute-start.3
  32.7 0.8 %collective-permute-done.1 = bf16[304,128]{1,0:T(8,128)(2,1)S(1)} collective-permute-done((bf16[304,128]{1,0:T(8,128)(2,1)S(1)}, bf16[304,128]{1,0:T(8,128)(2,1)S(1)}, u32[]{:S(2)}, u32[]{:S(2)}) %collective-permute-start.1) | collective-permute-done | bytes 77856 | tf_op jit(solution)/shard_map/ppermute | solution.py:325
  33.5 0.7 %collective-permute-start.2 = (bf16[304,128]{1,0:T(8,128)(2,1)S(1)}, bf16[304,128]{1,0:T(8,128)(2,1)S(1)}, u32[]{:S(2)}, u32[]{:S(2)}) collective-permute-start(bf16[304,128]{1,0:T(8,128)(2,1)S(1)} %add_convert_fusion.7), channel_id=1, source_target_pairs={{0,2},{1,3},{2,0},{3,1},{4,6},{5,7},{6,4},{7,5},{8,10},{9,11},{10,... | collective-permute-start | bytes 233480 | tf_op jit(solution)/shard_map/ppermute | solution.py:325
  34.2 0.6 %collective-permute-start.4 = (bf16[304,128]{1,0:T(8,128)(2,1)S(1)}, bf16[304,128]{1,0:T(8,128)(2,1)S(1)}, u32[]{:S(2)}, u32[]{:S(2)}) collective-permute-start(bf16[304,128]{1,0:T(8,128)(2,1)S(1)} %add_convert_fusion.6), channel_id=1, source_target_pairs={{0,4},{1,5},{2,6},{3,7},{4,0},{5,1},{6,2},{7,3},{8,12},{9,13},{10,... | collective-permute-start | bytes 233480 | tf_op jit(solution)/shard_map/ppermute | solution.py:325
  34.8 0.3 copy-done
  35.1 1.0 %shard_map.120 = bf16[32,8,256]{2,1,0:T(8,128)(2,1)} custom-call(bf16[32,8,256]{2,1,0:T(8,128)(2,1)S(1)} %copy-done, bf16[2,256,32]{2,1,0:T(8,128)(2,1)S(1)} %get-tuple-element.39.grads_ref, bf16[32,256]{1,0:T(8,128)(2,1)S(1)} %bitcast.14, bf16[32,256]{1,0:T(8,128)(2,1)S(1)} %bitcast.16), custom_call_target="tpu_custom_call" | custom-call | flops 8388608 | bytes 2097152 | tf_op jit(solution)/shard_map/pallas_call | solution.py:372
  36.1 1.9 %collective-permute-done.2 = bf16[304,128]{1,0:T(8,128)(2,1)S(1)} collective-permute-done((bf16[304,128]{1,0:T(8,128)(2,1)S(1)}, bf16[304,128]{1,0:T(8,128)(2,1)S(1)}, u32[]{:S(2)}, u32[]{:S(2)}) %collective-permute-start.2) | collective-permute-done | bytes 77856 | tf_op jit(solution)/shard_map/ppermute | solution.py:325
  38.0 0.7 %collective-permute-done.4 = bf16[304,128]{1,0:T(8,128)(2,1)S(1)} collective-permute-done((bf16[304,128]{1,0:T(8,128)(2,1)S(1)}, bf16[304,128]{1,0:T(8,128)(2,1)S(1)}, u32[]{:S(2)}, u32[]{:S(2)}) %collective-permute-start.4) | collective-permute-done | bytes 77856 | tf_op jit(solution)/shard_map/ppermute | solution.py:325
  38.8 0.5 %collective-permute-start.6 = (bf16[304,128]{1,0:T(8,128)(2,1)S(1)}, bf16[304,128]{1,0:T(8,128)(2,1)S(1)}, u32[]{:S(2)}, u32[]{:S(2)}) collective-permute-start(bf16[304,128]{1,0:T(8,128)(2,1)S(1)} %add_convert_fusion.4), channel_id=1, source_target_pairs={{0,8},{1,9},{2,10},{3,11},{4,12},{5,13},{6,14},{7,15},{8,0},{9,1},... | collective-permute-start | bytes 233480 | tf_op jit(solution)/shard_map/ppermute | solution.py:325
  39.3 1.5 %collective-permute-start.5 = (bf16[304,128]{1,0:T(8,128)(2,1)S(1)}, bf16[304,128]{1,0:T(8,128)(2,1)S(1)}, u32[]{:S(2)}, u32[]{:S(2)}) collective-permute-start(bf16[304,128]{1,0:T(8,128)(2,1)S(1)} %add_convert_fusion.5), channel_id=1, source_target_pairs={{0,4},{1,5},{2,6},{3,7},{4,0},{5,1},{6,2},{7,3},{8,12},{9,13},{10,... | collective-permute-start | bytes 233480 | tf_op jit(solution)/shard_map/ppermute | solution.py:325
  40.8 0.7 %copy-done.9 = f32[128]{0:T(128)S(1)} copy-done((f32[128]{0:T(128)S(1)}, f32[128]{0:T(128)}, u32[]{:S(2)}) %copy-start.9) | copy-done | bytes 536
  41.5 1.7 %shard_map.121 = bf16[8,128,128]{2,1,0:T(8,128)(2,1)} custom-call(s32[1]{0:T(128)} %bitcast.half_ref, bf16[64,4224]{1,0:T(8,128)(2,1)S(1)} %bitcast.12, bf16[64,4224]{1,0:T(8,128)(2,1)S(1)} %collective-permute-done.far_ref, f32[128,1024]{1,0:T(8,128)S(1)} %get-tuple-element.42.inv_ref, bf16[256,32]{1,0:T(8,128)(2,1)S(1)} %copy-done.1, ...), custom_call_target="tpu_custom_call" | custom-call | flops 268435456 | bytes 2097152 | tf_op jit(solution)/shard_map/pallas_call | solution.py:361
  43.2 1.8 %collective-permute-done.6 = bf16[304,128]{1,0:T(8,128)(2,1)S(1)} collective-permute-done((bf16[304,128]{1,0:T(8,128)(2,1)S(1)}, bf16[304,128]{1,0:T(8,128)(2,1)S(1)}, u32[]{:S(2)}, u32[]{:S(2)}) %collective-permute-start.6) | collective-permute-done | bytes 77856 | tf_op jit(solution)/shard_map/ppermute | solution.py:325
  45.0 1.3 %collective-permute-start.7 = (bf16[304,128]{1,0:T(8,128)(2,1)S(1)}, bf16[304,128]{1,0:T(8,128)(2,1)S(1)}, u32[]{:S(2)}, u32[]{:S(2)}) collective-permute-start(bf16[304,128]{1,0:T(8,128)(2,1)S(1)} %add_convert_fusion.3), channel_id=1, source_target_pairs={{0,8},{1,9},{2,10},{3,11},{4,12},{5,13},{6,14},{7,15},{8,0},{9,1},... | collective-permute-start | bytes 233480 | tf_op jit(solution)/shard_map/ppermute | solution.py:325
  46.3 1.6 %collective-permute-start.8 = (bf16[304,128]{1,0:T(8,128)(2,1)S(1)}, bf16[304,128]{1,0:T(8,128)(2,1)S(1)}, u32[]{:S(2)}, u32[]{:S(2)}) collective-permute-start(bf16[304,128]{1,0:T(8,128)(2,1)S(1)} %add_convert_fusion.1), channel_id=1, source_target_pairs={{0,2},{1,3},{2,0},{3,1},{4,6},{5,7},{6,4},{7,5},{8,10},{9,11},{10,... | collective-permute-start | bytes 233480 | tf_op jit(solution)/shard_map/ppermute | solution.py:325
  47.8 3.0 %collective-permute-done.7 = bf16[304,128]{1,0:T(8,128)(2,1)S(1)} collective-permute-done((bf16[304,128]{1,0:T(8,128)(2,1)S(1)}, bf16[304,128]{1,0:T(8,128)(2,1)S(1)}, u32[]{:S(2)}, u32[]{:S(2)}) %collective-permute-start.7) | collective-permute-done | bytes 77856 | tf_op jit(solution)/shard_map/ppermute | solution.py:325
  51.0 0.6 %collective-permute-start.10 = (bf16[304,128]{1,0:T(8,128)(2,1)S(1)}, bf16[304,128]{1,0:T(8,128)(2,1)S(1)}, u32[]{:S(2)}, u32[]{:S(2)}) collective-permute-start(bf16[304,128]{1,0:T(8,128)(2,1)S(1)} %add_convert_fusion.own_b_ref), channel_id=1, source_target_pairs={{0,1},{1,0},{2,3},{3,2},{4,5},{5,4},{6,7},{7,6},{8,9},{9,8},{10,11... | collective-permute-start | bytes 233480 | tf_op jit(solution)/shard_map/ppermute | solution.py:325
  51.6 0.7 %collective-permute-done.9.other_a_ref = bf16[304,128]{1,0:T(8,128)(2,1)S(1)} collective-permute-done((bf16[304,128]{1,0:T(8,128)(2,1)S(1)}, bf16[304,128]{1,0:T(8,128)(2,1)S(1)}, u32[]{:S(2)}, u32[]{:S(2)}) %collective-permute-start.9) | collective-permute-done | bytes 77856 | tf_op jit(solution)/shard_map/ppermute | solution.py:325
  52.2 0.3 collective-permute-done.10.other_b_ref
  52.5 0.8 %shard_map.122 = (f32[1024,128]{1,0:T(8,128)}, f32[32,256]{1,0:T(8,128)}, f32[32,256]{1,0:T(8,128)}, f32[1,128]{1,0:T(1,128)}) custom-call(s32[1]{0:T(128)} %bitcast.half_ref, bf16[304,128]{1,0:T(8,128)(2,1)S(1)} %add_convert_fusion.2.own_a_ref, bf16[304,128]{1,0:T(8,128)(2,1)S(1)} %add_convert_fusion.own_b_ref, ...), custom_call_target="tpu_custom_call" | custom-call | bytes 2097152 | tf_op jit(solution)/shard_map/pallas_call | solution.py:394
  (32 shorter events, 0.5 us)
Async XLA Ops:
  3.9 25.1 %copy-start.1 = (bf16[256,32]{1,0:T(8,128)(2,1)S(1)}, bf16[256,32]{1,0:T(8,128)(2,1)}, u32[]{:S(2)}) copy-start(bf16[256,32]{1,0:T(8,128)(2,1)} %get-tuple-element.31.left_ref) | copy-start | bytes 49156
  3.9 25.1 %copy-start.2 = (bf16[1024,128]{1,0:T(8,128)(2,1)S(1)}, bf16[1024,128]{1,0:T(8,128)(2,1)}, u32[]{:S(2)}) copy-start(bf16[1024,128]{1,0:T(8,128)(2,1)} %wout_ref.1) | copy-start | bytes 786436
  3.9 25.1 %copy-start.3 = (bf16[8,128,128]{2,1,0:T(8,128)(2,1)S(1)}, bf16[8,128,128]{2,1,0:T(8,128)(2,1)}, u32[]{:S(2)}) copy-start(bf16[8,128,128]{2,1,0:T(8,128)(2,1)} %get-tuple-element.30.cot_ref) | copy-start | bytes 786436
  3.9 25.1 %copy-start.4 = (bf16[256,256]{1,0:T(8,128)(2,1)S(1)}, bf16[256,256]{1,0:T(8,128)(2,1)}, u32[]{:S(2)}) copy-start(bf16[256,256]{1,0:T(8,128)(2,1)} %get-tuple-element.34.low_ref) | copy-start | bytes 393220
  3.9 25.1 %copy-start.5 = (bf16[256,32]{1,0:T(8,128)(2,1)S(1)}, bf16[256,32]{1,0:T(8,128)(2,1)}, u32[]{:S(2)}) copy-start(bf16[256,32]{1,0:T(8,128)(2,1)} %get-tuple-element.32.right_ref) | copy-start | bytes 49156
  4.0 25.1 %copy-start.6 = (bf16[32,1024]{1,0:T(8,128)(2,1)S(1)}, bf16[32,1024]{1,0:T(8,128)(2,1)}, u32[]{:S(2)}) copy-start(bf16[32,1024]{1,0:T(8,128)(2,1)} %get-tuple-element.33.maskb_ref) | copy-start | bytes 196612
  27.1 1.9 %collective-permute-start = (bf16[64,4224]{1,0:T(8,128)(2,1)S(1)}, bf16[64,4224]{1,0:T(8,128)(2,1)S(1)}, u32[]{:S(2)}, u32[]{:S(2)}) collective-permute-start(bf16[64,4224]{1,0:T(8,128)(2,1)S(1)} %bitcast.10), channel_id=1, source_target_pairs={{0,1},{1,0},{2,3},{3,2},{4,5},{5,4},{6,7},{7,6},{8,9},{9,8},{10,11... | collective-permute-start | bytes 1622024 | tf_op jit(solution)/shard_map/ppermute | solution.py:325
  32.1 1.3 %collective-permute-start.1 = (bf16[304,128]{1,0:T(8,128)(2,1)S(1)}, bf16[304,128]{1,0:T(8,128)(2,1)S(1)}, u32[]{:S(2)}, u32[]{:S(2)}) collective-permute-start(bf16[304,128]{1,0:T(8,128)(2,1)S(1)} %get-tuple-element.36), channel_id=1, source_target_pairs={{0,1},{1,0},{2,3},{3,2},{4,5},{5,4},{6,7},{7,6},{8,9},{9,8},{10,11... | collective-permute-start | bytes 233480 | tf_op jit(solution)/shard_map/ppermute | solution.py:325
  32.3 1.9 %collective-permute-start.3 = (bf16[304,128]{1,0:T(8,128)(2,1)S(1)}, bf16[304,128]{1,0:T(8,128)(2,1)S(1)}, u32[]{:S(2)}, u32[]{:S(2)}) collective-permute-start(bf16[304,128]{1,0:T(8,128)(2,1)S(1)} %get-tuple-element.38), channel_id=1, source_target_pairs={{0,1},{1,0},{2,3},{3,2},{4,5},{5,4},{6,7},{7,6},{8,9},{9,8},{10,11... | collective-permute-start | bytes 233480 | tf_op jit(solution)/shard_map/ppermute | solution.py:325
  33.5 4.5 %collective-permute-start.2 = (bf16[304,128]{1,0:T(8,128)(2,1)S(1)}, bf16[304,128]{1,0:T(8,128)(2,1)S(1)}, u32[]{:S(2)}, u32[]{:S(2)}) collective-permute-start(bf16[304,128]{1,0:T(8,128)(2,1)S(1)} %add_convert_fusion.7), channel_id=1, source_target_pairs={{0,2},{1,3},{2,0},{3,1},{4,6},{5,7},{6,4},{7,5},{8,10},{9,11},{10,... | collective-permute-start | bytes 233480 | tf_op jit(solution)/shard_map/ppermute | solution.py:325
  34.2 0.9 %copy-start = (bf16[32,8,256]{2,1,0:T(8,128)(2,1)S(1)}, bf16[32,8,256]{2,1,0:T(8,128)(2,1)}, u32[]{:S(2)}) copy-start(bf16[32,8,256]{2,1,0:T(8,128)(2,1)} %msa_ref.1) | copy-start | bytes 393220
  34.2 0.9 %copy-start.7 = (bf16[256,32]{0,1:T(8,128)(2,1)S(1)}, bf16[256,32]{0,1:T(8,128)(2,1)}, u32[]{:S(2)}) copy-start(bf16[256,32]{0,1:T(8,128)(2,1)} %param.9) | copy-start | bytes 49156
  34.2 0.9 %copy-start.8 = (bf16[256,32]{0,1:T(8,128)(2,1)S(1)}, bf16[256,32]{0,1:T(8,128)(2,1)}, u32[]{:S(2)}) copy-start(bf16[256,32]{0,1:T(8,128)(2,1)} %param.10) | copy-start | bytes 49156
  34.2 4.5 %collective-permute-start.4 = (bf16[304,128]{1,0:T(8,128)(2,1)S(1)}, bf16[304,128]{1,0:T(8,128)(2,1)S(1)}, u32[]{:S(2)}, u32[]{:S(2)}) collective-permute-start(bf16[304,128]{1,0:T(8,128)(2,1)S(1)} %add_convert_fusion.6), channel_id=1, source_target_pairs={{0,4},{1,5},{2,6},{3,7},{4,0},{5,1},{6,2},{7,3},{8,12},{9,13},{10,... | collective-permute-start | bytes 233480 | tf_op jit(solution)/shard_map/ppermute | solution.py:325
  38.8 6.2 %collective-permute-start.6 = (bf16[304,128]{1,0:T(8,128)(2,1)S(1)}, bf16[304,128]{1,0:T(8,128)(2,1)S(1)}, u32[]{:S(2)}, u32[]{:S(2)}) collective-permute-start(bf16[304,128]{1,0:T(8,128)(2,1)S(1)} %add_convert_fusion.4), channel_id=1, source_target_pairs={{0,8},{1,9},{2,10},{3,11},{4,12},{5,13},{6,14},{7,15},{8,0},{9,1},... | collective-permute-start | bytes 233480 | tf_op jit(solution)/shard_map/ppermute | solution.py:325
  39.3 5.6 %collective-permute-start.5 = (bf16[304,128]{1,0:T(8,128)(2,1)S(1)}, bf16[304,128]{1,0:T(8,128)(2,1)S(1)}, u32[]{:S(2)}, u32[]{:S(2)}) collective-permute-start(bf16[304,128]{1,0:T(8,128)(2,1)S(1)} %add_convert_fusion.5), channel_id=1, source_target_pairs={{0,4},{1,5},{2,6},{3,7},{4,0},{5,1},{6,2},{7,3},{8,12},{9,13},{10,... | collective-permute-start | bytes 233480 | tf_op jit(solution)/shard_map/ppermute | solution.py:325
  40.8 0.7 %copy-start.9 = (f32[128]{0:T(128)S(1)}, f32[128]{0:T(128)}, u32[]{:S(2)}) copy-start(f32[128]{0:T(128)} %param.12) | copy-start | bytes 1540
  45.0 5.9 %collective-permute-start.7 = (bf16[304,128]{1,0:T(8,128)(2,1)S(1)}, bf16[304,128]{1,0:T(8,128)(2,1)S(1)}, u32[]{:S(2)}, u32[]{:S(2)}) collective-permute-start(bf16[304,128]{1,0:T(8,128)(2,1)S(1)} %add_convert_fusion.3), channel_id=1, source_target_pairs={{0,8},{1,9},{2,10},{3,11},{4,12},{5,13},{6,14},{7,15},{8,0},{9,1},... | collective-permute-start | bytes 233480 | tf_op jit(solution)/shard_map/ppermute | solution.py:325
  46.3 4.7 %collective-permute-start.8 = (bf16[304,128]{1,0:T(8,128)(2,1)S(1)}, bf16[304,128]{1,0:T(8,128)(2,1)S(1)}, u32[]{:S(2)}, u32[]{:S(2)}) collective-permute-start(bf16[304,128]{1,0:T(8,128)(2,1)S(1)} %add_convert_fusion.1), channel_id=1, source_target_pairs={{0,2},{1,3},{2,0},{3,1},{4,6},{5,7},{6,4},{7,5},{8,10},{9,11},{10,... | collective-permute-start | bytes 233480 | tf_op jit(solution)/shard_map/ppermute | solution.py:325
  50.9 1.3 %collective-permute-start.9 = (bf16[304,128]{1,0:T(8,128)(2,1)S(1)}, bf16[304,128]{1,0:T(8,128)(2,1)S(1)}, u32[]{:S(2)}, u32[]{:S(2)}) collective-permute-start(bf16[304,128]{1,0:T(8,128)(2,1)S(1)} %add_convert_fusion.2.own_a_ref), channel_id=1, source_target_pairs={{0,1},{1,0},{2,3},{3,2},{4,5},{5,4},{6,7},{7,6},{8,9},{9,8},{10,11... | collective-permute-start | bytes 233480 | tf_op jit(solution)/shard_map/ppermute | solution.py:325
  51.0 1.5 %collective-permute-start.10 = (bf16[304,128]{1,0:T(8,128)(2,1)S(1)}, bf16[304,128]{1,0:T(8,128)(2,1)S(1)}, u32[]{:S(2)}, u32[]{:S(2)}) collective-permute-start(bf16[304,128]{1,0:T(8,128)(2,1)S(1)} %add_convert_fusion.own_b_ref), channel_id=1, source_target_pairs={{0,1},{1,0},{2,3},{3,2},{4,5},{5,4},{6,7},{7,6},{8,9},{9,8},{10,11... | collective-permute-start | bytes 233480 | tf_op jit(solution)/shard_map/ppermute | solution.py:325

commit v4 on v3

v4 whole, which is shorter than its diff:
```python
import functools

import jax
import jax.numpy as jnp
from jax import lax
from jax.experimental import pallas as pl
from jax.experimental.pallas import tpu as pltpu
from jax.sharding import Mesh
from jax.sharding import PartitionSpec as P

F32 = jnp.float32
BF16 = jnp.bfloat16
LANES = 128
EPS = 1e-05
VMEM_LIMIT = 40 * 1024 * 1024
PAIR = 2
DIRECT = 8


def dot(a, b, ca=1, cb=0):
    return lax.dot_general(a, b, (((ca,), (cb,)), ((), ())), preferred_element_type=F32)


def normalize(msa_ref):
    homologs, lines, depth = msa_ref.shape
    x = msa_ref[...].astype(F32).reshape(homologs * lines, depth)
    centred = x - jnp.mean(x, axis=-1, keepdims=True)
    spread = lax.rsqrt(jnp.mean(centred * centred, axis=-1, keepdims=True) + EPS)
    return centred * spread, spread


def pre_kernel(
    pos_ref, msa_hbm, mask_hbm, wf_hbm, wl_hbm, cot_hbm,
    left_ref, right_ref, maskb_ref, low_ref, *refs
):
    slots = refs[:-8]
    msa_ref, mask_ref, wf_ref, wl_ref, cot_ref, norm_scr, cot_scr, sems = refs[-8:]
    copies = [
        pltpu.make_async_copy(source, target, sems.at[n])
        for n, (source, target) in enumerate(
            [
                (msa_hbm, msa_ref),
                (wf_hbm, wf_ref),
                (wl_hbm, wl_ref),
                (mask_hbm, mask_ref),
                (cot_hbm, cot_ref),
            ]
        )
    ]
    for copy in copies:
        copy.start()
    homologs, lines, depth = msa_ref.shape
    width = wf_ref.shape[0]
    rows = homologs * lines
    wide = width * homologs
    total, pair_ch = cot_ref.shape[1:]
    chip, core = pos_ref[0] // 2, pos_ref[0] % 2
    copies[0].wait()
    normed, _ = normalize(msa_ref)
    for h in range(depth // LANES):
        norm_scr[h] = normed[:, h * LANES : (h + 1) * LANES]
    low = jnp.concatenate(
        [
            jnp.concatenate(
                [norm_scr[h, pl.ds(k, homologs, stride=lines), :] for k in range(lines)], axis=0
            )
            for h in range(depth // LANES)
        ],
        axis=1,
    ).astype(BF16)
    low_ref[...] = low
    for copy in copies[1:4]:
        copy.wait()
    mask = mask_ref[...].astype(F32).T
    cols = [jnp.broadcast_to(mask[:, k : k + 1], (homologs, LANES)) for k in range(lines)]
    for k in range(lines):
        maskb_ref[:, k * LANES : (k + 1) * LANES] = cols[k].astype(BF16)
    mask_rows = jnp.concatenate(cols, axis=0)
    left = (dot(low, wf_ref[...], 1, 1) * mask_rows[:, :width]).astype(BF16)
    right = (dot(low, wl_ref[...], 1, 1) * mask_rows[:, :width]).astype(BF16)
    left_ref[...] = left
    right_ref[...] = right
    spread_to = (
        lax.broadcasted_iota(jnp.int32, (width, wide), 1) // homologs
        == lax.broadcasted_iota(jnp.int32, (width, wide), 0)
    ).astype(BF16)
    own_tile = (
        lax.broadcasted_iota(jnp.int32, (homologs, LANES), 1) % homologs
        == lax.broadcasted_iota(jnp.int32, (homologs, LANES), 0)
    ).astype(F32)
    own_rows = jnp.concatenate([own_tile] * lines, axis=0)
    own = jnp.concatenate([own_rows] * (wide // LANES), axis=1)
    first = (lax.broadcasted_iota(jnp.int32, (rows, LANES), 1) < homologs).astype(F32)
    fold = (
        lax.broadcasted_iota(jnp.int32, (lines, rows), 1) // homologs
        == lax.broadcasted_iota(jnp.int32, (lines, rows), 0)
    ).astype(BF16)
    same = jnp.concatenate(
        [
            dot(fold, (dot(right, spread_to) * own).astype(BF16)),
            dot(fold, (dot(left, spread_to) * own).astype(BF16)),
            dot(fold, (mask_rows * own_rows * first).astype(BF16)),
        ],
        axis=1,
    )
    same = same.astype(BF16)
    base = same.shape[1]
    cols = lines * pair_ch
    copies[4].wait()
    cot_scr[...] = cot_ref[...].astype(F32).reshape(lines * total, pair_ch)
    for m, slot in enumerate(slots):
        slot[:, cols : cols + base] = same
        for begin, to in ((0, core), (cols + base, 1 - core)):
            first = (2 * (chip ^ m) + to) * lines
            for k in range(lines):
                slot[:, begin + k * pair_ch : begin + (k + 1) * pair_ch] = cot_scr[
                    pl.ds(first + k, lines, stride=total), :
                ].astype(BF16)


def weight_kernel(wout_ref, wleft_ref, w_scr):
    width, pair_ch = wleft_ref.shape[0], wout_ref.shape[1]
    w_scr[...] = wout_ref[...].astype(F32)
    for e in range(width):
        wleft_ref[:, e * pair_ch : (e + 1) * pair_ch] = w_scr[
            pl.ds(e, width, stride=width), :
        ].astype(BF16)


def half_kernel(offsets, pos_ref, mask_a_ref, mask_b_ref, right_a_ref, right_b_ref, *refs):
    early_ref, late_ref, right_ref, left_ref, by_col_ref, inv_ref, got_scr, p_scr = refs[-8:]
    slots = refs[:-8]
    near, far = slots[: len(slots) // 2], slots[len(slots) // 2 :]
    rows, width = right_a_ref.shape
    homologs, cols = mask_a_ref.shape
    wide = width * homologs
    lines = rows // homologs
    pair_ch = cols // lines
    span = wide // PAIR
    base = cols + 2 * wide + LANES
    chip, core = pos_ref[0] // 2, pos_ref[0] % 2
    for m, a_ref, b_ref in zip(offsets, near, far):
        tile = 2 * (chip ^ m)
        got_scr[tile + core] = a_ref[...]
        got_scr[tile + 1 - core, :, cols:base] = b_ref[:, cols:base]
        got_scr[tile + 1 - core, :, :cols] = b_ref[:, base:]
        got_scr[tile + 1 - core, :, base:] = b_ref[:, :cols]

    def load(start, size):
        return got_scr[:, :, pl.ds(start, size)].astype(F32).reshape(-1, size)

    right_ref[...] = load(cols, wide).astype(BF16)
    left_ref[...] = load(cols + wide, wide).astype(BF16)
    left = left_ref[:, pl.ds(pl.multiple_of(core * span, span), span)]
    masks = load(cols + 2 * wide, LANES).astype(BF16)
    group = LANES // homologs
    for m, (mask_ref, start) in enumerate(((mask_a_ref, 0), (mask_b_ref, base))):
        inv = 1.0 / (dot(masks[:, :homologs], mask_ref[...]) + 1.0)
        cot = (load(start, cols) * inv).astype(BF16)
        if m == 0:
            inv_ref[...] = inv
            by_col_ref[...] = cot
        for g in range(span // LANES):
            part = dot(left[:, g * LANES : (g + 1) * LANES], cot, 0, 0).astype(BF16)
            for b in range(group):
                c = g * group + b
                for k in range(lines):
                    to = m * rows + k * homologs
                    p_scr[to : to + homologs, c * pair_ch : (c + 1) * pair_ch] = part[
                        b * homologs : (b + 1) * homologs, k * pair_ch : (k + 1) * pair_ch
                    ]
    right = jnp.concatenate([right_a_ref[...], right_b_ref[...]], axis=0)
    out = dot(right, p_scr[...], 0, 0).astype(BF16)
    cut = early_ref.shape[0] // width
    for c in range(width // PAIR):
        line = out[:, c * pair_ch : (c + 1) * pair_ch]
        if c < cut:
            early_ref[c * width : (c + 1) * width, :] = line
        else:
            late_ref[(c - cut) * width : (c - cut + 1) * width, :] = line


def grads_kernel(
    right_ref, left_ref, by_col_ref, inv_ref, cot_ref, wout_ref, wleft_ref, maskb_ref, low_ref, late_ref,
    parts_ref, grads_ref,
    pq_scr,
):
    lines, total, pair_ch = cot_ref.shape
    homologs = maskb_ref.shape[0]
    width = wleft_ref.shape[0]
    wide = width * homologs
    rows = lines * homologs
    bias = 0.0
    by_row = []
    for k in range(lines):
        line = cot_ref[k].astype(F32)
        bias = bias + jnp.sum(line, axis=0, keepdims=True)
        by_row.append((line * inv_ref[:, k * LANES : (k + 1) * LANES]).astype(BF16))
    by_row = jnp.concatenate(by_row, axis=1)
    group = LANES // homologs
    for first, source, other in (
        (0, left_ref, by_col_ref[...]),
        (rows, right_ref, by_row),
    ):
        for g in range(wide // LANES):
            part = dot(source[:, g * LANES : (g + 1) * LANES], other, 0, 0).astype(BF16)
            for b in range(group):
                c = g * group + b
                for k in range(lines):
                    at = first + k * homologs
                    pq_scr[at : at + homologs, c * pair_ch : (c + 1) * pair_ch] = part[
                        b * homologs : (b + 1) * homologs, k * pair_ch : (k + 1) * pair_ch
                    ]
    wright = jnp.concatenate(
        [wout_ref[c * width : (c + 1) * width, :] for c in range(width)], axis=1
    )
    mask_rows = jnp.concatenate(
        [maskb_ref[:, k * LANES : k * LANES + width] for k in range(lines)], axis=0
    ).astype(F32)
    right_grad = (dot(pq_scr[:rows], wright, 1, 1) * mask_rows).astype(BF16)
    left_grad = (dot(pq_scr[rows:], wleft_ref[...], 1, 1) * mask_rows).astype(BF16)
    grads_ref[0] = left_grad
    grads_ref[1] = right_grad
    part_left = dot(left_grad, low_ref[...], 0, 0)
    part_right = dot(right_grad, low_ref[...], 0, 0)
    begin = late_ref.shape[0]
    parts_ref[:begin, :] = late_ref[...]
    for h in range(2):
        lanes = slice(h * pair_ch, (h + 1) * pair_ch)
        at = begin + 2 * h * width
        parts_ref[at : at + width, :] = part_left[:, lanes].astype(BF16)
        parts_ref[at + width : at + 2 * width, :] = part_right[:, lanes].astype(BF16)
    at = begin + 4 * width
    parts_ref[at:, :] = jnp.broadcast_to(bias, (parts_ref.shape[0] - at, pair_ch)).astype(BF16)


def update_kernel(right_ref, inv_ref, left_ref, wleft_ref, offset_ref, out_ref, lw_scr):
    lines, total, pair_ch = out_ref.shape
    rows, width = left_ref.shape
    homologs = rows // lines
    for e in range(width):
        part = dot(left_ref[...], wleft_ref[:, e * pair_ch : (e + 1) * pair_ch]).astype(BF16)
        for k in range(lines):
            lw_scr[e * homologs : (e + 1) * homologs, k * pair_ch : (k + 1) * pair_ch] = part[
                k * homologs : (k + 1) * homologs, :
            ]
    update = dot(right_ref[...], lw_scr[...]) * inv_ref[...]
    for k in range(lines):
        out_ref[k] = (update[:, k * pair_ch : (k + 1) * pair_ch] + offset_ref[...]).astype(BF16)


def msa_kernel(msa_ref, grads_ref, wf_ref, wl_ref, out_ref, scr):
    homologs, lines, depth = msa_ref.shape
    derivative = dot(grads_ref[0], wf_ref[...]) + dot(grads_ref[1], wl_ref[...])
    for h in range(depth // LANES):
        for k in range(lines):
            scr[h, pl.ds(k, homologs, stride=lines), :] = derivative[
                k * homologs : (k + 1) * homologs, h * LANES : (h + 1) * LANES
            ]
    derivative = jnp.concatenate([scr[h] for h in range(depth // LANES)], axis=1)
    normed, spread = normalize(msa_ref)
    one = jnp.mean(derivative, axis=-1, keepdims=True)
    two = jnp.mean(derivative * normed, axis=-1, keepdims=True)
    out = (derivative - one - normed * two) * spread
    out_ref[...] = out.reshape(homologs, lines, depth).astype(BF16)


def last_kernel(
    total, pos_ref, own_a_ref, other_a_ref, own_b_ref, other_b_ref,
    out_ref, former_ref, latter_ref, offset_ref,
):
    scale = 1.0 / total
    width = former_ref.shape[0]
    half = out_ref.shape[0] // PAIR
    early = own_a_ref.shape[0]
    late = half - early
    me = pos_ref[0] % PAIR
    for core, a_ref, b_ref in ((me, own_a_ref, own_b_ref), (1 - me, other_a_ref, other_b_ref)):
        at = core * half
        out_ref[pl.ds(pl.multiple_of(at, half), early), :] = a_ref[...].astype(F32) * scale
        out_ref[pl.ds(pl.multiple_of(at + early, width), late), :] = (
            b_ref[:late, :].astype(F32) * scale
        )
    parts = (own_b_ref[late:, :].astype(F32) + other_b_ref[late:, :].astype(F32)) * scale
    both = jnp.concatenate([parts[: 2 * width], parts[2 * width : 4 * width]], axis=1)
    former_ref[...] = both[:width]
    latter_ref[...] = both[width:]
    offset_ref[...] = parts[4 * width : 4 * width + 1]


def call(kernel, outs, scratch=(), smem=0, ins=0, flops=0, away=0, limit=VMEM_LIMIT):
    vmem = pl.BlockSpec(memory_space=pltpu.VMEM)
    return pl.pallas_call(
        kernel,
        out_shape=[jax.ShapeDtypeStruct(shape, kind) for shape, kind in outs],
        in_specs=[pl.BlockSpec(memory_space=pltpu.SMEM)] * smem
        + [pl.BlockSpec(memory_space=pltpu.HBM)] * away
        + [vmem] * ins,
        out_specs=[vmem] * len(outs),
        scratch_shapes=[pltpu.VMEM(shape, kind) for shape, kind in scratch]
        + [pltpu.SemaphoreType.DMA((away,))] * (away > 0),
        compiler_params=pltpu.CompilerParams(vmem_limit_bytes=limit),
        cost_estimate=pl.CostEstimate(flops=flops, bytes_accessed=0, transcendentals=0),
    )


def body(size, msa, mask, wf, wl, wout, offset, cot):
    homologs, lines, depth = msa.shape
    width = wf.shape[1]
    total, pair_ch = cot.shape[1:]
    wide = width * homologs
    rows = lines * homologs
    cols = lines * pair_ch
    span = 2 * wide + LANES + 2 * cols
    wf, wl = wf.T, wl.T
    pos = lax.axis_index(("chip", "core")).astype(jnp.int32).reshape(1)
    given = [msa, mask.T, wf, wl, cot]
    chips = size // 2
    left, right, maskb, low, *slots = call(
        pre_kernel,
        [
            ((rows, width), BF16),
            ((rows, width), BF16),
            ((homologs, lines * LANES), BF16),
            ((rows, depth), BF16),
        ]
        + [((lines, span), BF16)] * chips,
        [(x.shape, x.dtype) for x in given]
        + [((depth // LANES, rows, LANES), F32), ((lines * total, pair_ch), F32)],
        smem=1,
        away=len(given),
        limit=None,
    )(pos, *given)

    def swap(x, step):
        return lax.ppermute(x, ("chip", "core"), [(i, i ^ step) for i in range(size)])

    def add(x, y):
        return (x.astype(F32) + y.astype(F32)).astype(BF16)

    offsets = sorted(range(chips), key=lambda m: (-(m // 4), -(m // 2), m))
    if chips <= DIRECT:
        near = [swap(slots[m], 2 * m) if m else slots[0] for m in offsets]
    else:
        order = (pos[0] // 2) ^ jnp.arange(chips)
        near = lax.all_to_all(jnp.stack(slots)[order], "chip", 0, 0)[order]
        near = [near[m] for m in offsets]
    far = [swap(slot, 1) for slot in near]
    other_right, other_maskb = swap(right, 1), swap(maskb, 1)
    (wleft,) = call(
        weight_kernel,
        [((width, width * pair_ch), BF16)],
        [((width * width, pair_ch), F32)],
        ins=1,
    )(wout)
    near, wleft = lax.optimization_barrier((near, wleft))
    half = width * width // PAIR
    early = half * 7 // 8
    sums, late, all_right, all_left, by_col, inv = call(
        functools.partial(half_kernel, offsets),
        [
            ((early, pair_ch), BF16),
            ((half - early, pair_ch), BF16),
            ((total, wide), BF16),
            ((total, wide), BF16),
            ((total, cols), BF16),
            ((total, cols), F32),
        ],
        [((size, lines, span), BF16), ((PAIR * rows, width * pair_ch // PAIR), BF16)],
        smem=1,
        ins=4 + 2 * chips,
    )(pos, maskb, other_maskb, right, other_right, *near, *far)
    parts, grads = call(
        grads_kernel,
        [
            ((half - early + 4 * width + 16, pair_ch), BF16),
            ((2, rows, width), BF16),
        ],
        [((2 * rows, width * pair_ch), BF16)],
        ins=10,
    )(all_right, all_left, by_col, inv, cot, wout, wleft, maskb, low, late)

    def make_update():
        (out,) = call(
            update_kernel,
            [((lines, total, pair_ch), BF16)],
            [((wide, cols), BF16)],
            ins=5,
            flops=2 * total * wide * cols,
        )(all_right, inv, left, wleft, offset.reshape(1, pair_ch))
        return out

    def make_d_msa():
        (out,) = call(
            msa_kernel,
            [((homologs, lines, depth), BF16)],
            [((depth // LANES, rows, LANES), F32)],
            ins=4,
            flops=2 * rows * depth * 2 * width,
        )(msa, grads, wf, wl)
        return out

    steps = [1 << n for n in range(1, size.bit_length() - 1)]
    work = [make_d_msa, make_update]
    done = []
    for step_a, step_b in zip(steps, steps[1:] + steps[:1]):
        sums = add(sums, swap(sums, step_a))
        got = swap(parts, step_b)
        if work:
            out = work.pop(0)()
            got, out = lax.optimization_barrier((got, out))
            done.append(out)
        parts = add(parts, got)
    d_msa, update = done
    d_out, d_former, d_latter, d_offset = call(
        functools.partial(last_kernel, total),
        [
            ((width * width, pair_ch), F32),
            ((width, depth), F32),
            ((width, depth), F32),
            ((1, pair_ch), F32),
        ],
        smem=1,
        ins=4,
    )(pos, sums, swap(sums, 1), parts, swap(parts, 1))
    return update, d_msa, d_former.T, d_latter.T, d_out, d_offset.reshape(pair_ch)


def solution(mesh):
    size = mesh.shape["row"]
    split = Mesh(mesh.devices.reshape(-1, size // 2, 2), ("grp", "chip", "core"))
    whole = ("grp", "chip", "core")
    return jax.shard_map(
        functools.partial(body, size),
        mesh=split,
        in_specs=(P(None, whole, None), P(None, whole), P(), P(), P(), P(), P(whole, None, None)),
        out_specs=(
            P(whole, None, None),
            P(None, whole, None),
            P("grp", None),
            P("grp", None),
            P("grp", None),
            P("grp"),
        ),
        check_vma=False,
    )
```

time: 53.6 us -> 50.1 us (0.935)
  blocking collectives: 23.1 us -> 0 us
  starting transfers between devices: 7.37 us -> 25.5 us
  Pallas kernels: 9.89 us -> 11.5 us
    all_to_all x1 -> x0, blocking collectives: 23.1 us -> none  [body(): lax.all_to_all(payload.reshape(size // 2, lines, span), 'row', 0, 0, axis...]
    ppermute x11 -> x25, starting transfers between devices: 7.37 us -> 25.5 us  [swap(): lax.ppermute(x, ('chip', 'core'), [(i, i ^ step) for i in range(size)])]
    pallas_call x2 -> x4, Pallas kernels: 6.33 us -> 7.95 us  [the longest x1 3.2 us: body(): call(pre_kernel, [((rows, width), BF16), ((rows, width), BF16), ((homolog...]
    ppermute x11 -> x25, waiting for transfers between devices: 11 us -> 11.4 us  [swap(): lax.ppermute(x, ('chip', 'core'), [(i, i ^ step) for i in range(size)])]
  transfers between devices with their start and end apart: 11 -> 25, of which waited for: 8 -> 12; matrix products, arithmetic and copies ran while one was open for 0% -> 0% of each run, Pallas kernels for 5% -> 12%
where the time goes in v4:
time: 50.1 us; the launch traced here: 50 us
  starting transfers between devices  25.5 us (51%)
  Pallas kernels  11.5 us (23%)
  waiting for transfers between devices  11.4 us (23%)
  between operations  0.79 us (2%)
  local copies, waits for them, and re-layouts  0.7 us (1%)
    ppermute x25, starting transfers between devices, swap(): lax.ppermute(x, ('chip', 'core'), [(i, i ^ step) for i in range(size)])  25.5 us
    ppermute x25, waiting for transfers between devices, swap(): lax.ppermute(x, ('chip', 'core'), [(i, i ^ step) for i in range(size)])  11.4 us
    pallas_call x1, Pallas kernels, body(): call(pre_kernel, [((rows, width), BF16), ((rows, width), BF16), ((homolog...  3.2 us
    pallas_call x1, Pallas kernels, body(): call(grads_kernel, [((half - early + 4 * width + 16, pair_ch), BF16), ((2...  2.77 us
    pallas_call x1, Pallas kernels, make_update(): call(update_kernel, [((lines, total, pair_ch), BF16)], [((wide, cols), BF...  1.68 us
    pallas_call x1, Pallas kernels, body(): call(functools.partial(half_kernel, offsets), [((early, pair_ch), BF16),...  1.63 us
    pallas_call x1, Pallas kernels, make_d_msa(): call(msa_kernel, [((homologs, lines, depth), BF16)], [((depth // LANES, r...  1.01 us
  transfers between devices with their start and end apart: 25, of which 12 were waited for; matrix products, arithmetic and copies ran while one was open for 0% of the time, Pallas kernels for 12%

profile of v4, /device:TPU:0, one launch (start us, length us, event | category | flops | bytes accessed | tf_op | source)
XLA Modules:
  0.0 50.0 jit_solution(17805227464066510722)
XLA Ops:
  0.6 3.2 %shard_map.118 = (bf16[256,32]{1,0:T(8,128)(2,1)}, bf16[256,32]{1,0:T(8,128)(2,1)}, bf16[32,1024]{1,0:T(8,128)(2,1)}, bf16[256,256]{1,0:T(8,128)(2,1)}, bf16[8,4...) custom-call(s32[1]{0:T(128)} %bitcast.pos_ref, ...), custom_call_target="tpu_custom_call" | custom-call | tf_op jit(solution)/shard_map/pallas_call | solution.py:319
  4.5 5.0 %collective-permute-start.2 = (bf16[8,4224]{1,0:T(8,128)(2,1)}, bf16[8,4224]{1,0:T(8,128)(2,1)S(1)}, u32[]{:S(2)}, u32[]{:S(2)}) collective-permute-start(bf16[8,4224]{1,0:T(8,128)(2,1)} %get-tuple-element.45), channel_id=1, source_target_pairs={{0,12},{1,13},{2,14},{3,15},{4,8},{5,9},{6,10},{7,11},{8,4},{9,5},... | collective-permute-start | bytes 202760 | tf_op jit(solution)/shard_map/ppermute | solution.py:336
  9.5 1.2 %collective-permute-start.3 = (bf16[8,4224]{1,0:T(8,128)(2,1)}, bf16[8,4224]{1,0:T(8,128)(2,1)S(1)}, u32[]{:S(2)}, u32[]{:S(2)}) collective-permute-start(bf16[8,4224]{1,0:T(8,128)(2,1)} %get-tuple-element.46), channel_id=1, source_target_pairs={{0,14},{1,15},{2,12},{3,13},{4,10},{5,11},{6,8},{7,9},{8,6},{9,7},... | collective-permute-start | bytes 202760 | tf_op jit(solution)/shard_map/ppermute | solution.py:336
  10.6 0.8 %collective-permute-start.4 = (bf16[8,4224]{1,0:T(8,128)(2,1)}, bf16[8,4224]{1,0:T(8,128)(2,1)S(1)}, u32[]{:S(2)}, u32[]{:S(2)}) collective-permute-start(bf16[8,4224]{1,0:T(8,128)(2,1)} %get-tuple-element.47), channel_id=1, source_target_pairs={{0,8},{1,9},{2,10},{3,11},{4,12},{5,13},{6,14},{7,15},{8,0},{9,1},... | collective-permute-start | bytes 202760 | tf_op jit(solution)/shard_map/ppermute | solution.py:336
  11.4 1.9 %collective-permute-start.5 = (bf16[8,4224]{1,0:T(8,128)(2,1)}, bf16[8,4224]{1,0:T(8,128)(2,1)S(1)}, u32[]{:S(2)}, u32[]{:S(2)}) collective-permute-start(bf16[8,4224]{1,0:T(8,128)(2,1)} %get-tuple-element.48), channel_id=1, source_target_pairs={{0,10},{1,11},{2,8},{3,9},{4,14},{5,15},{6,12},{7,13},{8,2},{9,3},... | collective-permute-start | bytes 202760 | tf_op jit(solution)/shard_map/ppermute | solution.py:336
  13.3 1.5 %collective-permute-start.6 = (bf16[8,4224]{1,0:T(8,128)(2,1)}, bf16[8,4224]{1,0:T(8,128)(2,1)S(1)}, u32[]{:S(2)}, u32[]{:S(2)}) collective-permute-start(bf16[8,4224]{1,0:T(8,128)(2,1)} %get-tuple-element.49), channel_id=1, source_target_pairs={{0,4},{1,5},{2,6},{3,7},{4,0},{5,1},{6,2},{7,3},{8,12},{9,13},{10,... | collective-permute-start | bytes 202760 | tf_op jit(solution)/shard_map/ppermute | solution.py:336
  14.9 1.6 %collective-permute-start.7 = (bf16[8,4224]{1,0:T(8,128)(2,1)}, bf16[8,4224]{1,0:T(8,128)(2,1)S(1)}, u32[]{:S(2)}, u32[]{:S(2)}) collective-permute-start(bf16[8,4224]{1,0:T(8,128)(2,1)} %get-tuple-element.50), channel_id=1, source_target_pairs={{0,6},{1,7},{2,4},{3,5},{4,2},{5,3},{6,0},{7,1},{8,14},{9,15},{10,... | collective-permute-start | bytes 202760 | tf_op jit(solution)/shard_map/ppermute | solution.py:336
  17.2 1.4 %collective-permute-start.8 = (bf16[8,4224]{1,0:T(8,128)(2,1)}, bf16[8,4224]{1,0:T(8,128)(2,1)S(1)}, u32[]{:S(2)}, u32[]{:S(2)}) collective-permute-start(bf16[8,4224]{1,0:T(8,128)(2,1)} %get-tuple-element.52), channel_id=1, source_target_pairs={{0,2},{1,3},{2,0},{3,1},{4,6},{5,7},{6,4},{7,5},{8,10},{9,11},{10,... | collective-permute-start | bytes 202760 | tf_op jit(solution)/shard_map/ppermute | solution.py:336
  18.5 2.2 %collective-permute-done.4.refs_2_ = bf16[8,4224]{1,0:T(8,128)(2,1)S(1)} collective-permute-done((bf16[8,4224]{1,0:T(8,128)(2,1)}, bf16[8,4224]{1,0:T(8,128)(2,1)S(1)}, u32[]{:S(2)}, u32[]{:S(2)}) %collective-permute-start.4) | collective-permute-done | bytes 67616 | tf_op jit(solution)/shard_map/ppermute | solution.py:336
  20.8 1.7 %collective-permute-done.5.refs_3_ = bf16[8,4224]{1,0:T(8,128)(2,1)S(1)} collective-permute-done((bf16[8,4224]{1,0:T(8,128)(2,1)}, bf16[8,4224]{1,0:T(8,128)(2,1)S(1)}, u32[]{:S(2)}, u32[]{:S(2)}) %collective-permute-start.5) | collective-permute-done | bytes 67616 | tf_op jit(solution)/shard_map/ppermute | solution.py:336
  25.3 1.6 %shard_map.120 = (bf16[448,128]{1,0:T(8,128)(2,1)S(1)}, bf16[64,128]{1,0:T(8,128)(2,1)S(1)}, bf16[128,1024]{1,0:T(8,128)(2,1)S(1)}, bf16[128,1024]{1,0:T(8,128)(...) custom-call(s32[1]{0:T(128)} %bitcast.pos_ref, bf16[32,1024]{1,0:T(8,128)(2,1)S(1)} %copy-done.3, ...), custom_call_target="tpu_custom_call" | custom-call | tf_op jit(solution)/shard_map/pallas_call | solution.py:359
  27.6 2.8 %shard_map.121 = (bf16[208,128]{1,0:T(8,128)(2,1)S(1)}, bf16[2,256,32]{2,1,0:T(8,128)(2,1)S(1)}) custom-call(bf16[128,1024]{1,0:T(8,128)(2,1)S(1)} %get-tuple-element.61.right_ref, bf16[128,1024]{1,0:T(8,128)(2,1)S(1)} %get-tuple-element.62.left_ref, bf16[128,1024]{1,0:T(8,128)(2,1)S(1)} %get-tuple-element.63.by_col_ref, ...), custom_call_target="tpu_custom_call" | custom-call | tf_op jit(solution)/shard_map/pallas_call | solution.py:373
  30.4 1.1 %collective-permute-start.17 = (bf16[208,128]{1,0:T(8,128)(2,1)S(1)}, bf16[208,128]{1,0:T(8,128)(2,1)S(1)}, u32[]{:S(2)}, u32[]{:S(2)}) collective-permute-start(bf16[208,128]{1,0:T(8,128)(2,1)S(1)} %get-tuple-element.68), channel_id=1, source_target_pairs={{0,4},{1,5},{2,6},{3,7},{4,0},{5,1},{6,2},{7,3},{8,12},{9,13},{10,... | collective-permute-start | bytes 159752 | tf_op jit(solution)/shard_map/ppermute | solution.py:336
  31.4 1.0 %shard_map.122 = bf16[32,8,256]{2,1,0:T(8,128)(2,1)} custom-call(bf16[32,8,256]{2,1,0:T(8,128)(2,1)S(1)} %copy-done.2, bf16[2,256,32]{2,1,0:T(8,128)(2,1)S(1)} %get-tuple-element.69.grads_ref, bf16[32,256]{1,0:T(8,128)(2,1)S(1)} %bitcast.9, bf16[32,256]{1,0:T(8,128)(2,1)S(1)} %bitcast.11), custom_call_target="tpu_custom_call" | custom-call | flops 8388608 | tf_op jit(solution)/shard_map/pallas_call | solution.py:394
  32.5 2.0 %collective-permute-done.17 = bf16[208,128]{1,0:T(8,128)(2,1)S(1)} collective-permute-done((bf16[208,128]{1,0:T(8,128)(2,1)S(1)}, bf16[208,128]{1,0:T(8,128)(2,1)S(1)}, u32[]{:S(2)}, u32[]{:S(2)}) %collective-permute-start.17) | collective-permute-done | bytes 53280 | tf_op jit(solution)/shard_map/ppermute | solution.py:336
  34.6 1.1 %collective-permute-start.20 = (bf16[448,128]{1,0:T(8,128)(2,1)S(1)}, bf16[448,128]{1,0:T(8,128)(2,1)S(1)}, u32[]{:S(2)}, u32[]{:S(2)}) collective-permute-start(bf16[448,128]{1,0:T(8,128)(2,1)S(1)} %add_convert_fusion.2), channel_id=1, source_target_pairs={{0,4},{1,5},{2,6},{3,7},{4,0},{5,1},{6,2},{7,3},{8,12},{9,13},{10,... | collective-permute-start | bytes 344072 | tf_op jit(solution)/shard_map/ppermute | solution.py:336
  35.7 2.6 %collective-permute-start.18 = (bf16[208,128]{1,0:T(8,128)(2,1)S(1)}, bf16[208,128]{1,0:T(8,128)(2,1)S(1)}, u32[]{:S(2)}, u32[]{:S(2)}) collective-permute-start(bf16[208,128]{1,0:T(8,128)(2,1)S(1)} %add_convert_fusion.5), channel_id=1, source_target_pairs={{0,8},{1,9},{2,10},{3,11},{4,12},{5,13},{6,14},{7,15},{8,0},{9,1},... | collective-permute-start | bytes 159752 | tf_op jit(solution)/shard_map/ppermute | solution.py:336
  39.0 1.7 %shard_map.123 = bf16[8,128,128]{2,1,0:T(8,128)(2,1)} custom-call(bf16[128,1024]{1,0:T(8,128)(2,1)S(1)} %get-tuple-element.61.right_ref, f32[128,1024]{1,0:T(8,128)S(1)} %get-tuple-element.64.inv_ref, bf16[256,32]{1,0:T(8,128)(2,1)S(1)} %copy-done.6, bf16[32,4096]{1,0:T(8,128)(2,1)S(1)} %shard_map.119.wleft_ref, f32[1,128]{1,0:T(1,128)S(1)} %bitcast.12), custom_call_target="tpu_custom_call" | custom-call | flops 268435456 | tf_op jit(solution)/shard_map/pallas_call | solution.py:384
  40.9 2.7 %collective-permute-start.21 = (bf16[448,128]{1,0:T(8,128)(2,1)S(1)}, bf16[448,128]{1,0:T(8,128)(2,1)S(1)}, u32[]{:S(2)}, u32[]{:S(2)}) collective-permute-start(bf16[448,128]{1,0:T(8,128)(2,1)S(1)} %add_convert_fusion.1), channel_id=1, source_target_pairs={{0,8},{1,9},{2,10},{3,11},{4,12},{5,13},{6,14},{7,15},{8,0},{9,1},... | collective-permute-start | bytes 344072 | tf_op jit(solution)/shard_map/ppermute | solution.py:336
  43.6 1.5 %collective-permute-start.23 = (bf16[208,128]{1,0:T(8,128)(2,1)S(1)}, bf16[208,128]{1,0:T(8,128)(2,1)S(1)}, u32[]{:S(2)}, u32[]{:S(2)}) collective-permute-start(bf16[208,128]{1,0:T(8,128)(2,1)S(1)} %add_convert_fusion.4), channel_id=1, source_target_pairs={{0,2},{1,3},{2,0},{3,1},{4,6},{5,7},{6,4},{7,5},{8,10},{9,11},{10,... | collective-permute-start | bytes 159752 | tf_op jit(solution)/shard_map/ppermute | solution.py:336
  45.1 1.5 %collective-permute-done.21 = bf16[448,128]{1,0:T(8,128)(2,1)S(1)} collective-permute-done((bf16[448,128]{1,0:T(8,128)(2,1)S(1)}, bf16[448,128]{1,0:T(8,128)(2,1)S(1)}, u32[]{:S(2)}, u32[]{:S(2)}) %collective-permute-start.21) | collective-permute-done | bytes 114720 | tf_op jit(solution)/shard_map/ppermute | solution.py:336
  46.7 1.1 %collective-permute-done.23 = bf16[208,128]{1,0:T(8,128)(2,1)S(1)} collective-permute-done((bf16[208,128]{1,0:T(8,128)(2,1)S(1)}, bf16[208,128]{1,0:T(8,128)(2,1)S(1)}, u32[]{:S(2)}, u32[]{:S(2)}) %collective-permute-start.23) | collective-permute-done | bytes 53280 | tf_op jit(solution)/shard_map/ppermute | solution.py:336
  47.9 1.2 %collective-permute-done.24.other_b_ref = bf16[208,128]{1,0:T(8,128)(2,1)S(1)} collective-permute-done((bf16[208,128]{1,0:T(8,128)(2,1)S(1)}, bf16[208,128]{1,0:T(8,128)(2,1)S(1)}, u32[]{:S(2)}, u32[]{:S(2)}) %collective-permute-start.24) | collective-permute-done | bytes 53280 | tf_op jit(solution)/shard_map/ppermute | solution.py:336
  49.1 0.8 %shard_map.124 = (f32[1024,128]{1,0:T(8,128)}, f32[32,256]{1,0:T(8,128)}, f32[32,256]{1,0:T(8,128)}, f32[1,128]{1,0:T(1,128)}) custom-call(s32[1]{0:T(128)} %bitcast.pos_ref, bf16[448,128]{1,0:T(8,128)(2,1)S(1)} %add_convert_fusion.own_a_ref, bf16[448,128]{1,0:T(8,128)(2,1)S(1)} %collective-permute-done.22.other_a_ref, ...), custom_call_target="tpu_custom_call" | custom-call | tf_op jit(solution)/shard_map/pallas_call | solution.py:415
  (61 shorter events, 5.8 us)
Async XLA Ops:
  3.9 9.5 %collective-permute-start = (bf16[32,1024]{1,0:T(8,128)(2,1)}, bf16[32,1024]{1,0:T(8,128)(2,1)S(1)}, u32[]{:S(2)}, u32[]{:S(2)}) collective-permute-start(bf16[32,1024]{1,0:T(8,128)(2,1)} %get-tuple-element.43.mask_a_ref.maskb_ref), channel_id=1, source_target_pairs={{0,1},{1,0},{2,3},{3,2},{4,5},{5,4},{6,7},{7,6},{8,9},{9,8},{10,11... | collective-permute-start | bytes 196616 | tf_op jit(solution)/shard_map/ppermute | solution.py:336
  4.4 7.0 %collective-permute-start.1 = (bf16[256,32]{1,0:T(8,128)(2,1)}, bf16[256,32]{1,0:T(8,128)(2,1)S(1)}, u32[]{:S(2)}, u32[]{:S(2)}) collective-permute-start(bf16[256,32]{1,0:T(8,128)(2,1)} %get-tuple-element.44.right_a_ref), channel_id=1, source_target_pairs={{0,1},{1,0},{2,3},{3,2},{4,5},{5,4},{6,7},{7,6},{8,9},{9,8},{10,11... | collective-permute-start | bytes 49160 | tf_op jit(solution)/shard_map/ppermute | solution.py:336
  4.5 10.4 %collective-permute-start.2 = (bf16[8,4224]{1,0:T(8,128)(2,1)}, bf16[8,4224]{1,0:T(8,128)(2,1)S(1)}, u32[]{:S(2)}, u32[]{:S(2)}) collective-permute-start(bf16[8,4224]{1,0:T(8,128)(2,1)} %get-tuple-element.45), channel_id=1, source_target_pairs={{0,12},{1,13},{2,14},{3,15},{4,8},{5,9},{6,10},{7,11},{8,4},{9,5},... | collective-permute-start | bytes 202760 | tf_op jit(solution)/shard_map/ppermute | solution.py:336
  9.5 7.7 %collective-permute-start.3 = (bf16[8,4224]{1,0:T(8,128)(2,1)}, bf16[8,4224]{1,0:T(8,128)(2,1)S(1)}, u32[]{:S(2)}, u32[]{:S(2)}) collective-permute-start(bf16[8,4224]{1,0:T(8,128)(2,1)} %get-tuple-element.46), channel_id=1, source_target_pairs={{0,14},{1,15},{2,12},{3,13},{4,10},{5,11},{6,8},{7,9},{8,6},{9,7},... | collective-permute-start | bytes 202760 | tf_op jit(solution)/shard_map/ppermute | solution.py:336
  10.6 10.1 %collective-permute-start.4 = (bf16[8,4224]{1,0:T(8,128)(2,1)}, bf16[8,4224]{1,0:T(8,128)(2,1)S(1)}, u32[]{:S(2)}, u32[]{:S(2)}) collective-permute-start(bf16[8,4224]{1,0:T(8,128)(2,1)} %get-tuple-element.47), channel_id=1, source_target_pairs={{0,8},{1,9},{2,10},{3,11},{4,12},{5,13},{6,14},{7,15},{8,0},{9,1},... | collective-permute-start | bytes 202760 | tf_op jit(solution)/shard_map/ppermute | solution.py:336
  11.4 11.0 %collective-permute-start.5 = (bf16[8,4224]{1,0:T(8,128)(2,1)}, bf16[8,4224]{1,0:T(8,128)(2,1)S(1)}, u32[]{:S(2)}, u32[]{:S(2)}) collective-permute-start(bf16[8,4224]{1,0:T(8,128)(2,1)} %get-tuple-element.48), channel_id=1, source_target_pairs={{0,10},{1,11},{2,8},{3,9},{4,14},{5,15},{6,12},{7,13},{8,2},{9,3},... | collective-permute-start | bytes 202760 | tf_op jit(solution)/shard_map/ppermute | solution.py:336
  13.3 9.1 %collective-permute-start.6 = (bf16[8,4224]{1,0:T(8,128)(2,1)}, bf16[8,4224]{1,0:T(8,128)(2,1)S(1)}, u32[]{:S(2)}, u32[]{:S(2)}) collective-permute-start(bf16[8,4224]{1,0:T(8,128)(2,1)} %get-tuple-element.49), channel_id=1, source_target_pairs={{0,4},{1,5},{2,6},{3,7},{4,0},{5,1},{6,2},{7,3},{8,12},{9,13},{10,... | collective-permute-start | bytes 202760 | tf_op jit(solution)/shard_map/ppermute | solution.py:336
  14.9 8.1 %collective-permute-start.7 = (bf16[8,4224]{1,0:T(8,128)(2,1)}, bf16[8,4224]{1,0:T(8,128)(2,1)S(1)}, u32[]{:S(2)}, u32[]{:S(2)}) collective-permute-start(bf16[8,4224]{1,0:T(8,128)(2,1)} %get-tuple-element.50), channel_id=1, source_target_pairs={{0,6},{1,7},{2,4},{3,5},{4,2},{5,3},{6,0},{7,1},{8,14},{9,15},{10,... | collective-permute-start | bytes 202760 | tf_op jit(solution)/shard_map/ppermute | solution.py:336
  17.2 5.9 %collective-permute-start.8 = (bf16[8,4224]{1,0:T(8,128)(2,1)}, bf16[8,4224]{1,0:T(8,128)(2,1)S(1)}, u32[]{:S(2)}, u32[]{:S(2)}) collective-permute-start(bf16[8,4224]{1,0:T(8,128)(2,1)} %get-tuple-element.52), channel_id=1, source_target_pairs={{0,2},{1,3},{2,0},{3,1},{4,6},{5,7},{6,4},{7,5},{8,10},{9,11},{10,... | collective-permute-start | bytes 202760 | tf_op jit(solution)/shard_map/ppermute | solution.py:336
  20.8 2.7 %collective-permute-start.15 = (bf16[8,4224]{1,0:T(8,128)(2,1)}, bf16[8,4224]{1,0:T(8,128)(2,1)S(1)}, u32[]{:S(2)}, u32[]{:S(2)}) collective-permute-start(bf16[8,4224]{1,0:T(8,128)(2,1)} %get-tuple-element.59.refs_6_), channel_id=1, source_target_pairs={{0,1},{1,0},{2,3},{3,2},{4,5},{5,4},{6,7},{7,6},{8,9},{9,8},{10,11... | collective-permute-start | bytes 202760 | tf_op jit(solution)/shard_map/ppermute | solution.py:336
  22.5 1.5 %collective-permute-start.10 = (bf16[8,4224]{1,0:T(8,128)(2,1)S(1)}, bf16[8,4224]{1,0:T(8,128)(2,1)S(1)}, u32[]{:S(2)}, u32[]{:S(2)}) collective-permute-start(bf16[8,4224]{1,0:T(8,128)(2,1)S(1)} %collective-permute-done.3.refs_1_), channel_id=1, source_target_pairs={{0,1},{1,0},{2,3},{3,2},{4,5},{5,4},{6,7},{7,6},{8,9},{9,8},{10,11... | collective-permute-start | bytes 202760 | tf_op jit(solution)/shard_map/ppermute | solution.py:336
  23.0 1.6 %collective-permute-start.11 = (bf16[8,4224]{1,0:T(8,128)(2,1)S(1)}, bf16[8,4224]{1,0:T(8,128)(2,1)S(1)}, u32[]{:S(2)}, u32[]{:S(2)}) collective-permute-start(bf16[8,4224]{1,0:T(8,128)(2,1)S(1)} %collective-permute-done.4.refs_2_), channel_id=1, source_target_pairs={{0,1},{1,0},{2,3},{3,2},{4,5},{5,4},{6,7},{7,6},{8,9},{9,8},{10,11... | collective-permute-start | bytes 202760 | tf_op jit(solution)/shard_map/ppermute | solution.py:336
  23.1 1.6 %collective-permute-start.12 = (bf16[8,4224]{1,0:T(8,128)(2,1)S(1)}, bf16[8,4224]{1,0:T(8,128)(2,1)S(1)}, u32[]{:S(2)}, u32[]{:S(2)}) collective-permute-start(bf16[8,4224]{1,0:T(8,128)(2,1)S(1)} %collective-permute-done.5.refs_3_), channel_id=1, source_target_pairs={{0,1},{1,0},{2,3},{3,2},{4,5},{5,4},{6,7},{7,6},{8,9},{9,8},{10,11... | collective-permute-start | bytes 202760 | tf_op jit(solution)/shard_map/ppermute | solution.py:336
  23.5 1.3 %collective-permute-start.13 = (bf16[8,4224]{1,0:T(8,128)(2,1)S(1)}, bf16[8,4224]{1,0:T(8,128)(2,1)S(1)}, u32[]{:S(2)}, u32[]{:S(2)}) collective-permute-start(bf16[8,4224]{1,0:T(8,128)(2,1)S(1)} %collective-permute-done.6.refs_4_), channel_id=1, source_target_pairs={{0,1},{1,0},{2,3},{3,2},{4,5},{5,4},{6,7},{7,6},{8,9},{9,8},{10,11... | collective-permute-start | bytes 202760 | tf_op jit(solution)/shard_map/ppermute | solution.py:336
  23.7 1.3 %collective-permute-start.14 = (bf16[8,4224]{1,0:T(8,128)(2,1)S(1)}, bf16[8,4224]{1,0:T(8,128)(2,1)S(1)}, u32[]{:S(2)}, u32[]{:S(2)}) collective-permute-start(bf16[8,4224]{1,0:T(8,128)(2,1)S(1)} %collective-permute-done.7.refs_5_), channel_id=1, source_target_pairs={{0,1},{1,0},{2,3},{3,2},{4,5},{5,4},{6,7},{7,6},{8,9},{9,8},{10,11... | collective-permute-start | bytes 202760 | tf_op jit(solution)/shard_map/ppermute | solution.py:336
  24.0 1.3 %collective-permute-start.16 = (bf16[8,4224]{1,0:T(8,128)(2,1)S(1)}, bf16[8,4224]{1,0:T(8,128)(2,1)S(1)}, u32[]{:S(2)}, u32[]{:S(2)}) collective-permute-start(bf16[8,4224]{1,0:T(8,128)(2,1)S(1)} %collective-permute-done.8.refs_7_), channel_id=1, source_target_pairs={{0,1},{1,0},{2,3},{3,2},{4,5},{5,4},{6,7},{7,6},{8,9},{9,8},{10,11... | collective-permute-start | bytes 202760 | tf_op jit(solution)/shard_map/ppermute | solution.py:336
  26.9 7.6 %collective-permute-start.19 = (bf16[448,128]{1,0:T(8,128)(2,1)S(1)}, bf16[448,128]{1,0:T(8,128)(2,1)S(1)}, u32[]{:S(2)}, u32[]{:S(2)}) collective-permute-start(bf16[448,128]{1,0:T(8,128)(2,1)S(1)} %get-tuple-element.74), channel_id=1, source_target_pairs={{0,2},{1,3},{2,0},{3,1},{4,6},{5,7},{6,4},{7,5},{8,10},{9,11},{10,... | collective-permute-start | bytes 344072 | tf_op jit(solution)/shard_map/ppermute | solution.py:336
  30.4 4.2 %collective-permute-start.17 = (bf16[208,128]{1,0:T(8,128)(2,1)S(1)}, bf16[208,128]{1,0:T(8,128)(2,1)S(1)}, u32[]{:S(2)}, u32[]{:S(2)}) collective-permute-start(bf16[208,128]{1,0:T(8,128)(2,1)S(1)} %get-tuple-element.68), channel_id=1, source_target_pairs={{0,4},{1,5},{2,6},{3,7},{4,0},{5,1},{6,2},{7,3},{8,12},{9,13},{10,... | collective-permute-start | bytes 159752 | tf_op jit(solution)/shard_map/ppermute | solution.py:336
  34.6 6.3 %collective-permute-start.20 = (bf16[448,128]{1,0:T(8,128)(2,1)S(1)}, bf16[448,128]{1,0:T(8,128)(2,1)S(1)}, u32[]{:S(2)}, u32[]{:S(2)}) collective-permute-start(bf16[448,128]{1,0:T(8,128)(2,1)S(1)} %add_convert_fusion.2), channel_id=1, source_target_pairs={{0,4},{1,5},{2,6},{3,7},{4,0},{5,1},{6,2},{7,3},{8,12},{9,13},{10,... | collective-permute-start | bytes 344072 | tf_op jit(solution)/shard_map/ppermute | solution.py:336
  35.7 5.1 %collective-permute-start.18 = (bf16[208,128]{1,0:T(8,128)(2,1)S(1)}, bf16[208,128]{1,0:T(8,128)(2,1)S(1)}, u32[]{:S(2)}, u32[]{:S(2)}) collective-permute-start(bf16[208,128]{1,0:T(8,128)(2,1)S(1)} %add_convert_fusion.5), channel_id=1, source_target_pairs={{0,8},{1,9},{2,10},{3,11},{4,12},{5,13},{6,14},{7,15},{8,0},{9,1},... | collective-permute-start | bytes 159752 | tf_op jit(solution)/shard_map/ppermute | solution.py:336
  40.9 5.8 %collective-permute-start.21 = (bf16[448,128]{1,0:T(8,128)(2,1)S(1)}, bf16[448,128]{1,0:T(8,128)(2,1)S(1)}, u32[]{:S(2)}, u32[]{:S(2)}) collective-permute-start(bf16[448,128]{1,0:T(8,128)(2,1)S(1)} %add_convert_fusion.1), channel_id=1, source_target_pairs={{0,8},{1,9},{2,10},{3,11},{4,12},{5,13},{6,14},{7,15},{8,0},{9,1},... | collective-permute-start | bytes 344072 | tf_op jit(solution)/shard_map/ppermute | solution.py:336
  43.6 4.2 %collective-permute-start.23 = (bf16[208,128]{1,0:T(8,128)(2,1)S(1)}, bf16[208,128]{1,0:T(8,128)(2,1)S(1)}, u32[]{:S(2)}, u32[]{:S(2)}) collective-permute-start(bf16[208,128]{1,0:T(8,128)(2,1)S(1)} %add_convert_fusion.4), channel_id=1, source_target_pairs={{0,2},{1,3},{2,0},{3,1},{4,6},{5,7},{6,4},{7,5},{8,10},{9,11},{10,... | collective-permute-start | bytes 159752 | tf_op jit(solution)/shard_map/ppermute | solution.py:336
  46.6 2.5 %collective-permute-start.22 = (bf16[448,128]{1,0:T(8,128)(2,1)S(1)}, bf16[448,128]{1,0:T(8,128)(2,1)S(1)}, u32[]{:S(2)}, u32[]{:S(2)}) collective-permute-start(bf16[448,128]{1,0:T(8,128)(2,1)S(1)} %add_convert_fusion.own_a_ref), channel_id=1, source_target_pairs={{0,1},{1,0},{2,3},{3,2},{4,5},{5,4},{6,7},{7,6},{8,9},{9,8},{10,11... | collective-permute-start | bytes 344072 | tf_op jit(solution)/shard_map/ppermute | solution.py:336
  47.8 1.3 %collective-permute-start.24 = (bf16[208,128]{1,0:T(8,128)(2,1)S(1)}, bf16[208,128]{1,0:T(8,128)(2,1)S(1)}, u32[]{:S(2)}, u32[]{:S(2)}) collective-permute-start(bf16[208,128]{1,0:T(8,128)(2,1)S(1)} %add_convert_fusion.3.own_b_ref), channel_id=1, source_target_pairs={{0,1},{1,0},{2,3},{3,2},{4,5},{5,4},{6,7},{7,6},{8,9},{9,8},{10,11... | collective-permute-start | bytes 159752 | tf_op jit(solution)/shard_map/ppermute | solution.py:336
  (12 other events, 60.5 us)

commit v5 on v4

--- a/solution.py
+++ b/solution.py
@@ -33,8 +33,15 @@
     pos_ref, msa_hbm, mask_hbm, wf_hbm, wl_hbm, cot_hbm,
     left_ref, right_ref, maskb_ref, low_ref, *refs
 ):
-    slots = refs[:-8]
-    msa_ref, mask_ref, wf_ref, wl_ref, cot_ref, norm_scr, cot_scr, sems = refs[-8:]
+    slots, refs = refs[:-13], refs[-13:]
+    msa_ref, mask_ref, wf_ref, wl_ref, cot_ref, norm_scr, cot_scr = refs[:7]
+    left_scr, right_scr, maskb_scr, low_scr, slot_scr, sems = refs[7:]
+    sent = []
+
+    def send(source, target):
+        sent.append(pltpu.make_async_copy(source, target, sems.at[len(copies) + len(sent)]))
+        sent[-1].start()
+
     copies = [
         pltpu.make_async_copy(source, target, sems.at[n])
         for n, (source, target) in enumerate(
@@ -68,18 +75,22 @@
         ],
         axis=1,
     ).astype(BF16)
-    low_ref[...] = low
+    low_scr[...] = low
+    send(low_scr, low_ref)
     for copy in copies[1:4]:
         copy.wait()
     mask = mask_ref[...].astype(F32).T
     cols = [jnp.broadcast_to(mask[:, k : k + 1], (homologs, LANES)) for k in range(lines)]
     for k in range(lines):
-        maskb_ref[:, k * LANES : (k + 1) * LANES] = cols[k].astype(BF16)
+        maskb_scr[:, k * LANES : (k + 1) * LANES] = cols[k].astype(BF16)
+    send(maskb_scr, maskb_ref)
     mask_rows = jnp.concatenate(cols, axis=0)
     left = (dot(low, wf_ref[...], 1, 1) * mask_rows[:, :width]).astype(BF16)
     right = (dot(low, wl_ref[...], 1, 1) * mask_rows[:, :width]).astype(BF16)
-    left_ref[...] = left
-    right_ref[...] = right
+    left_scr[...] = left
+    right_scr[...] = right
+    send(left_scr, left_ref)
+    send(right_scr, right_ref)
     spread_to = (
         lax.broadcasted_iota(jnp.int32, (width, wide), 1) // homologs
         == lax.broadcasted_iota(jnp.int32, (width, wide), 0)
@@ -109,13 +120,16 @@
     copies[4].wait()
     cot_scr[...] = cot_ref[...].astype(F32).reshape(lines * total, pair_ch)
     for m, slot in enumerate(slots):
-        slot[:, cols : cols + base] = same
+        slot_scr[m, :, cols : cols + base] = same
         for begin, to in ((0, core), (cols + base, 1 - core)):
             first = (2 * (chip ^ m) + to) * lines
             for k in range(lines):
-                slot[:, begin + k * pair_ch : begin + (k + 1) * pair_ch] = cot_scr[
+                slot_scr[m, :, begin + k * pair_ch : begin + (k + 1) * pair_ch] = cot_scr[
                     pl.ds(first + k, lines, stride=total), :
                 ].astype(BF16)
+        send(slot_scr.at[m], slot)
+    for copy in sent:
+        copy.wait()
 
 
 def weight_kernel(wout_ref, wleft_ref, w_scr):
@@ -127,9 +141,9 @@
         ].astype(BF16)
 
 
-def half_kernel(offsets, pos_ref, mask_a_ref, mask_b_ref, right_a_ref, right_b_ref, *refs):
-    early_ref, late_ref, right_ref, left_ref, by_col_ref, inv_ref, got_scr, p_scr = refs[-8:]
-    slots = refs[:-8]
+def half_kernel(offsets, pos_ref, *refs):
+    early_ref, late_ref, right_ref, left_ref, by_col_ref, inv_ref, p_ref, got_scr, p_scr = refs[-9:]
+    slots, (mask_a_ref, mask_b_ref, right_a_ref, right_b_ref) = refs[:-13], refs[-13:-9]
     near, far = slots[: len(slots) // 2], slots[len(slots) // 2 :]
     rows, width = right_a_ref.shape
     homologs, cols = mask_a_ref.shape
@@ -154,7 +168,9 @@
     left = left_ref[:, pl.ds(pl.multiple_of(core * span, span), span)]
     masks = load(cols + 2 * wide, LANES).astype(BF16)
     group = LANES // homologs
-    for m, (mask_ref, start) in enumerate(((mask_a_ref, 0), (mask_b_ref, base))):
+    sides = (mask_a_ref, right_a_ref, 0, p_ref), (mask_b_ref, right_b_ref, base, p_scr)
+    out = 0.0
+    for m, (mask_ref, side_ref, start, to_ref) in enumerate(sides):
         inv = 1.0 / (dot(masks[:, :homologs], mask_ref[...]) + 1.0)
         cot = (load(start, cols) * inv).astype(BF16)
         if m == 0:
@@ -165,12 +181,12 @@
             for b in range(group):
                 c = g * group + b
                 for k in range(lines):
-                    to = m * rows + k * homologs
-                    p_scr[to : to + homologs, c * pair_ch : (c + 1) * pair_ch] = part[
+                    to = k * homologs
+                    to_ref[to : to + homologs, c * pair_ch : (c + 1) * pair_ch] = part[
                         b * homologs : (b + 1) * homologs, k * pair_ch : (k + 1) * pair_ch
                     ]
-    right = jnp.concatenate([right_a_ref[...], right_b_ref[...]], axis=0)
-    out = dot(right, p_scr[...], 0, 0).astype(BF16)
+        out = out + dot(side_ref[...], to_ref[...], 0, 0)
+    out = out.astype(BF16)
     cut = early_ref.shape[0] // width
     for c in range(width // PAIR):
         line = out[:, c * pair_ch : (c + 1) * pair_ch]
@@ -181,9 +197,9 @@
 
 
 def grads_kernel(
-    right_ref, left_ref, by_col_ref, inv_ref, cot_ref, wout_ref, wleft_ref, maskb_ref, low_ref, late_ref,
+    pos_ref, p_ref, right_ref, left_ref, by_col_ref, inv_ref, cot_ref, wout_ref, wleft_ref, maskb_ref, low_ref, late_ref,
     parts_ref, grads_ref,
-    pq_scr,
+    p_scr, q_scr,
 ):
     lines, total, pair_ch = cot_ref.shape
     homologs = maskb_ref.shape[0]
@@ -198,27 +214,35 @@
         by_row.append((line * inv_ref[:, k * LANES : (k + 1) * LANES]).astype(BF16))
     by_row = jnp.concatenate(by_row, axis=1)
     group = LANES // homologs
-    for first, source, other in (
-        (0, left_ref, by_col_ref[...]),
-        (rows, right_ref, by_row),
+    span = wide // PAIR
+    core = pos_ref[0] % PAIR
+    for out_ref, source, other in (
+        (p_scr, left_ref[:, pl.ds(pl.multiple_of((1 - core) * span, span), span)], by_col_ref[...]),
+        (q_scr, right_ref[...], by_row),
     ):
-        for g in range(wide // LANES):
+        for g in range(source.shape[1] // LANES):
             part = dot(source[:, g * LANES : (g + 1) * LANES], other, 0, 0).astype(BF16)
             for b in range(group):
                 c = g * group + b
                 for k in range(lines):
-                    at = first + k * homologs
-                    pq_scr[at : at + homologs, c * pair_ch : (c + 1) * pair_ch] = part[
+                    at = k * homologs
+                    out_ref[at : at + homologs, c * pair_ch : (c + 1) * pair_ch] = part[
                         b * homologs : (b + 1) * homologs, k * pair_ch : (k + 1) * pair_ch
                     ]
-    wright = jnp.concatenate(
-        [wout_ref[c * width : (c + 1) * width, :] for c in range(width)], axis=1
-    )
+
+    def weights(half):
+        size = wout_ref.shape[0] // PAIR
+        block = wout_ref[pl.ds(pl.multiple_of(half * size, size), size), :]
+        return jnp.concatenate(
+            [block[c * width : (c + 1) * width] for c in range(width // PAIR)], axis=1
+        )
+
     mask_rows = jnp.concatenate(
         [maskb_ref[:, k * LANES : k * LANES + width] for k in range(lines)], axis=0
     ).astype(F32)
-    right_grad = (dot(pq_scr[:rows], wright, 1, 1) * mask_rows).astype(BF16)
-    left_grad = (dot(pq_scr[rows:], wleft_ref[...], 1, 1) * mask_rows).astype(BF16)
+    right_sum = dot(p_ref[...], weights(core), 1, 1) + dot(p_scr[...], weights(1 - core), 1, 1)
+    right_grad = (right_sum * mask_rows).astype(BF16)
+    left_grad = (dot(q_scr[...], wleft_ref[...], 1, 1) * mask_rows).astype(BF16)
     grads_ref[0] = left_grad
     grads_ref[1] = right_grad
     part_left = dot(left_grad, low_ref[...], 0, 0)
@@ -296,9 +320,9 @@
         in_specs=[pl.BlockSpec(memory_space=pltpu.SMEM)] * smem
         + [pl.BlockSpec(memory_space=pltpu.HBM)] * away
         + [vmem] * ins,
-        out_specs=[vmem] * len(outs),
+        out_specs=[pl.BlockSpec(memory_space=pl.ANY) if away else vmem] * len(outs),
         scratch_shapes=[pltpu.VMEM(shape, kind) for shape, kind in scratch]
-        + [pltpu.SemaphoreType.DMA((away,))] * (away > 0),
+        + [pltpu.SemaphoreType.DMA((away + len(outs),))] * (away > 0),
         compiler_params=pltpu.CompilerParams(vmem_limit_bytes=limit),
         cost_estimate=pl.CostEstimate(flops=flops, bytes_accessed=0, transcendentals=0),
     )
@@ -326,7 +350,15 @@
         ]
         + [((lines, span), BF16)] * chips,
         [(x.shape, x.dtype) for x in given]
-        + [((depth // LANES, rows, LANES), F32), ((lines * total, pair_ch), F32)],
+        + [
+            ((depth // LANES, rows, LANES), F32),
+            ((lines * total, pair_ch), F32),
+            ((rows, width), BF16),
+            ((rows, width), BF16),
+            ((homologs, lines * LANES), BF16),
+            ((rows, depth), BF16),
+            ((chips, lines, span), BF16),
+        ],
         smem=1,
         away=len(given),
         limit=None,
@@ -355,8 +387,8 @@
     )(wout)
     near, wleft = lax.optimization_barrier((near, wleft))
     half = width * width // PAIR
-    early = half * 7 // 8
-    sums, late, all_right, all_left, by_col, inv = call(
+    early = half * 15 // 16
+    sums, late, all_right, all_left, by_col, inv, own_p = call(
         functools.partial(half_kernel, offsets),
         [
             ((early, pair_ch), BF16),
@@ -365,20 +397,22 @@
             ((total, wide), BF16),
             ((total, cols), BF16),
             ((total, cols), F32),
-        ],
-        [((size, lines, span), BF16), ((PAIR * rows, width * pair_ch // PAIR), BF16)],
+            ((rows, width * pair_ch // PAIR), BF16),
+        ],
+        [((size, lines, span), BF16), ((rows, width * pair_ch // PAIR), BF16)],
         smem=1,
         ins=4 + 2 * chips,
-    )(pos, maskb, other_maskb, right, other_right, *near, *far)
+    )(pos, *near, *far, maskb, other_maskb, right, other_right)
     parts, grads = call(
         grads_kernel,
         [
             ((half - early + 4 * width + 16, pair_ch), BF16),
             ((2, rows, width), BF16),
         ],
-        [((2 * rows, width * pair_ch), BF16)],
-        ins=10,
-    )(all_right, all_left, by_col, inv, cot, wout, wleft, maskb, low, late)
+        [((rows, width * pair_ch // PAIR), BF16), ((rows, width * pair_ch), BF16)],
+        smem=1,
+        ins=11,
+    )(pos, own_p, all_right, all_left, by_col, inv, cot, wout, wleft, maskb, low, late)
 
     def make_update():
         (out,) = call(

time: 50.1 us -> 49.5 us (0.988)
  transfers between devices with their start and end apart: 25 -> 25, of which waited for: 12 -> 12; matrix products, arithmetic and copies ran while one was open for 0% -> 0% of each run, Pallas kernels for 12% -> 11%
where the time goes in v5:
time: 49.5 us; the launch traced here: 49.4 us
  starting transfers between devices  25.5 us (52%)
  Pallas kernels  11.1 us (22%)
  waiting for transfers between devices  11.1 us (22%)
  between operations  0.8 us (2%)
  local copies, waits for them, and re-layouts  0.7 us (1%)
    ppermute x25, starting transfers between devices, swap(): lax.ppermute(x, ('chip', 'core'), [(i, i ^ step) for i in range(size)])  25.5 us
    ppermute x25, waiting for transfers between devices, swap(): lax.ppermute(x, ('chip', 'core'), [(i, i ^ step) for i in range(size)])  11.1 us
    pallas_call x1, Pallas kernels, body(): call(pre_kernel, [((rows, width), BF16), ((rows, width), BF16), ((homolog...  3.16 us
    pallas_call x1, Pallas kernels, body(): call(grads_kernel, [((half - early + 4 * width + 16, pair_ch), BF16), ((2...  2.45 us
    pallas_call x1, Pallas kernels, make_update(): call(update_kernel, [((lines, total, pair_ch), BF16)], [((wide, cols), BF...  1.68 us
    pallas_call x1, Pallas kernels, body(): call(functools.partial(half_kernel, offsets), [((early, pair_ch), BF16),...  1.61 us
    pallas_call x1, Pallas kernels, make_d_msa(): call(msa_kernel, [((homologs, lines, depth), BF16)], [((depth // LANES, r...  1.02 us
  transfers between devices with their start and end apart: 25, of which 12 were waited for; matrix products, arithmetic and copies ran while one was open for 0% of the time, Pallas kernels for 11%

profile of v5, /device:TPU:0, one launch (start us, length us, event | category | flops | bytes accessed | tf_op | source)
XLA Modules:
  0.0 49.4 jit_solution(4064691165898245213)
XLA Ops:
  0.6 3.2 %shard_map.118 = (bf16[256,32]{1,0:T(8,128)(2,1)}, bf16[256,32]{1,0:T(8,128)(2,1)}, bf16[32,1024]{1,0:T(8,128)(2,1)}, bf16[256,256]{1,0:T(8,128)(2,1)}, bf16[8,4...) custom-call(s32[1]{0:T(128)} %bitcast.pos_ref, ...), custom_call_target="tpu_custom_call" | custom-call | tf_op jit(solution)/shard_map/pallas_call | solution.py:343
  4.4 5.0 %collective-permute-start = (bf16[8,4224]{1,0:T(8,128)(2,1)}, bf16[8,4224]{1,0:T(8,128)(2,1)S(1)}, u32[]{:S(2)}, u32[]{:S(2)}) collective-permute-start(bf16[8,4224]{1,0:T(8,128)(2,1)} %get-tuple-element.44), channel_id=1, source_target_pairs={{0,12},{1,13},{2,14},{3,15},{4,8},{5,9},{6,10},{7,11},{8,4},{9,5},... | collective-permute-start | bytes 202760 | tf_op jit(solution)/shard_map/ppermute | solution.py:368
  9.5 1.1 %collective-permute-start.1 = (bf16[8,4224]{1,0:T(8,128)(2,1)}, bf16[8,4224]{1,0:T(8,128)(2,1)S(1)}, u32[]{:S(2)}, u32[]{:S(2)}) collective-permute-start(bf16[8,4224]{1,0:T(8,128)(2,1)} %get-tuple-element.45), channel_id=1, source_target_pairs={{0,14},{1,15},{2,12},{3,13},{4,10},{5,11},{6,8},{7,9},{8,6},{9,7},... | collective-permute-start | bytes 202760 | tf_op jit(solution)/shard_map/ppermute | solution.py:368
  10.6 0.8 %collective-permute-start.2 = (bf16[8,4224]{1,0:T(8,128)(2,1)}, bf16[8,4224]{1,0:T(8,128)(2,1)S(1)}, u32[]{:S(2)}, u32[]{:S(2)}) collective-permute-start(bf16[8,4224]{1,0:T(8,128)(2,1)} %get-tuple-element.46), channel_id=1, source_target_pairs={{0,8},{1,9},{2,10},{3,11},{4,12},{5,13},{6,14},{7,15},{8,0},{9,1},... | collective-permute-start | bytes 202760 | tf_op jit(solution)/shard_map/ppermute | solution.py:368
  11.4 1.9 %collective-permute-start.3 = (bf16[8,4224]{1,0:T(8,128)(2,1)}, bf16[8,4224]{1,0:T(8,128)(2,1)S(1)}, u32[]{:S(2)}, u32[]{:S(2)}) collective-permute-start(bf16[8,4224]{1,0:T(8,128)(2,1)} %get-tuple-element.47), channel_id=1, source_target_pairs={{0,10},{1,11},{2,8},{3,9},{4,14},{5,15},{6,12},{7,13},{8,2},{9,3},... | collective-permute-start | bytes 202760 | tf_op jit(solution)/shard_map/ppermute | solution.py:368
  13.3 1.5 %collective-permute-start.4 = (bf16[8,4224]{1,0:T(8,128)(2,1)}, bf16[8,4224]{1,0:T(8,128)(2,1)S(1)}, u32[]{:S(2)}, u32[]{:S(2)}) collective-permute-start(bf16[8,4224]{1,0:T(8,128)(2,1)} %get-tuple-element.48), channel_id=1, source_target_pairs={{0,4},{1,5},{2,6},{3,7},{4,0},{5,1},{6,2},{7,3},{8,12},{9,13},{10,... | collective-permute-start | bytes 202760 | tf_op jit(solution)/shard_map/ppermute | solution.py:368
  14.8 1.6 %collective-permute-start.5 = (bf16[8,4224]{1,0:T(8,128)(2,1)}, bf16[8,4224]{1,0:T(8,128)(2,1)S(1)}, u32[]{:S(2)}, u32[]{:S(2)}) collective-permute-start(bf16[8,4224]{1,0:T(8,128)(2,1)} %get-tuple-element.49), channel_id=1, source_target_pairs={{0,6},{1,7},{2,4},{3,5},{4,2},{5,3},{6,0},{7,1},{8,14},{9,15},{10,... | collective-permute-start | bytes 202760 | tf_op jit(solution)/shard_map/ppermute | solution.py:368
  17.1 1.4 %collective-permute-start.6 = (bf16[8,4224]{1,0:T(8,128)(2,1)}, bf16[8,4224]{1,0:T(8,128)(2,1)S(1)}, u32[]{:S(2)}, u32[]{:S(2)}) collective-permute-start(bf16[8,4224]{1,0:T(8,128)(2,1)} %get-tuple-element.51), channel_id=1, source_target_pairs={{0,2},{1,3},{2,0},{3,1},{4,6},{5,7},{6,4},{7,5},{8,10},{9,11},{10,... | collective-permute-start | bytes 202760 | tf_op jit(solution)/shard_map/ppermute | solution.py:368
  18.5 2.2 %collective-permute-done.2.refs_2_ = bf16[8,4224]{1,0:T(8,128)(2,1)S(1)} collective-permute-done((bf16[8,4224]{1,0:T(8,128)(2,1)}, bf16[8,4224]{1,0:T(8,128)(2,1)S(1)}, u32[]{:S(2)}, u32[]{:S(2)}) %collective-permute-start.2) | collective-permute-done | bytes 67616 | tf_op jit(solution)/shard_map/ppermute | solution.py:368
  20.7 1.7 %collective-permute-done.3.refs_3_ = bf16[8,4224]{1,0:T(8,128)(2,1)S(1)} collective-permute-done((bf16[8,4224]{1,0:T(8,128)(2,1)}, bf16[8,4224]{1,0:T(8,128)(2,1)S(1)}, u32[]{:S(2)}, u32[]{:S(2)}) %collective-permute-start.3) | collective-permute-done | bytes 67616 | tf_op jit(solution)/shard_map/ppermute | solution.py:368
  25.3 1.6 %shard_map.120 = (bf16[480,128]{1,0:T(8,128)(2,1)S(1)}, bf16[32,128]{1,0:T(8,128)(2,1)S(1)}, bf16[128,1024]{1,0:T(8,128)(2,1)S(1)}, bf16[128,1024]{1,0:T(8,128)(...) custom-call(s32[1]{0:T(128)} %bitcast.pos_ref, ...), custom_call_target="tpu_custom_call" | custom-call | tf_op jit(solution)/shard_map/pallas_call | solution.py:391
  27.6 2.4 %shard_map.121 = (bf16[176,128]{1,0:T(8,128)(2,1)S(1)}, bf16[2,256,32]{2,1,0:T(8,128)(2,1)S(1)}) custom-call(s32[1]{0:T(128)} %bitcast.pos_ref, bf16[256,2048]{1,0:T(8,128)(2,1)S(1)} %get-tuple-element.62.p_ref, bf16[128,1024]{1,0:T(8,128)(2,1)S(1)} %get-tuple-element.63.right_ref, bf16[128,1024]{1,0:T(8,128)(2,1)S(1)} %get-tuple-element.64.left_ref, ...), custom_call_target="tpu_custom_call" | custom-call | tf_op jit(solution)/shard_map/pallas_call | solution.py:406
  30.0 1.1 %collective-permute-start.17 = (bf16[176,128]{1,0:T(8,128)(2,1)S(1)}, bf16[176,128]{1,0:T(8,128)(2,1)S(1)}, u32[]{:S(2)}, u32[]{:S(2)}) collective-permute-start(bf16[176,128]{1,0:T(8,128)(2,1)S(1)} %get-tuple-element.70), channel_id=1, source_target_pairs={{0,4},{1,5},{2,6},{3,7},{4,0},{5,1},{6,2},{7,3},{8,12},{9,13},{10,... | collective-permute-start | bytes 135176 | tf_op jit(solution)/shard_map/ppermute | solution.py:368
  31.2 1.0 %shard_map.122 = bf16[32,8,256]{2,1,0:T(8,128)(2,1)} custom-call(bf16[32,8,256]{2,1,0:T(8,128)(2,1)S(1)} %copy-done.2, bf16[2,256,32]{2,1,0:T(8,128)(2,1)S(1)} %get-tuple-element.71.grads_ref, bf16[32,256]{1,0:T(8,128)(2,1)S(1)} %bitcast.9, bf16[32,256]{1,0:T(8,128)(2,1)S(1)} %bitcast.11), custom_call_target="tpu_custom_call" | custom-call | flops 8388608 | tf_op jit(solution)/shard_map/pallas_call | solution.py:428
  32.2 1.9 %collective-permute-done.17 = bf16[176,128]{1,0:T(8,128)(2,1)S(1)} collective-permute-done((bf16[176,128]{1,0:T(8,128)(2,1)S(1)}, bf16[176,128]{1,0:T(8,128)(2,1)S(1)}, u32[]{:S(2)}, u32[]{:S(2)}) %collective-permute-start.17) | collective-permute-done | bytes 45088 | tf_op jit(solution)/shard_map/ppermute | solution.py:368
  34.2 1.2 %collective-permute-start.20 = (bf16[480,128]{1,0:T(8,128)(2,1)S(1)}, bf16[480,128]{1,0:T(8,128)(2,1)S(1)}, u32[]{:S(2)}, u32[]{:S(2)}) collective-permute-start(bf16[480,128]{1,0:T(8,128)(2,1)S(1)} %add_convert_fusion.2), channel_id=1, source_target_pairs={{0,4},{1,5},{2,6},{3,7},{4,0},{5,1},{6,2},{7,3},{8,12},{9,13},{10,... | collective-permute-start | bytes 368648 | tf_op jit(solution)/shard_map/ppermute | solution.py:368
  35.4 2.6 %collective-permute-start.18 = (bf16[176,128]{1,0:T(8,128)(2,1)S(1)}, bf16[176,128]{1,0:T(8,128)(2,1)S(1)}, u32[]{:S(2)}, u32[]{:S(2)}) collective-permute-start(bf16[176,128]{1,0:T(8,128)(2,1)S(1)} %add_convert_fusion.5), channel_id=1, source_target_pairs={{0,8},{1,9},{2,10},{3,11},{4,12},{5,13},{6,14},{7,15},{8,0},{9,1},... | collective-permute-start | bytes 135176 | tf_op jit(solution)/shard_map/ppermute | solution.py:368
  38.6 1.7 %shard_map.123 = bf16[8,128,128]{2,1,0:T(8,128)(2,1)} custom-call(bf16[128,1024]{1,0:T(8,128)(2,1)S(1)} %get-tuple-element.63.right_ref, f32[128,1024]{1,0:T(8,128)S(1)} %get-tuple-element.66.inv_ref, bf16[256,32]{1,0:T(8,128)(2,1)S(1)} %copy-done.6, bf16[32,4096]{1,0:T(8,128)(2,1)S(1)} %shard_map.119.wleft_ref, f32[1,128]{1,0:T(1,128)S(1)} %bitcast.12), custom_call_target="tpu_custom_call" | custom-call | flops 268435456 | tf_op jit(solution)/shard_map/pallas_call | solution.py:418
  40.4 2.7 %collective-permute-start.21 = (bf16[480,128]{1,0:T(8,128)(2,1)S(1)}, bf16[480,128]{1,0:T(8,128)(2,1)S(1)}, u32[]{:S(2)}, u32[]{:S(2)}) collective-permute-start(bf16[480,128]{1,0:T(8,128)(2,1)S(1)} %add_convert_fusion.1), channel_id=1, source_target_pairs={{0,8},{1,9},{2,10},{3,11},{4,12},{5,13},{6,14},{7,15},{8,0},{9,1},... | collective-permute-start | bytes 368648 | tf_op jit(solution)/shard_map/ppermute | solution.py:368
  43.1 1.6 %collective-permute-start.23 = (bf16[176,128]{1,0:T(8,128)(2,1)S(1)}, bf16[176,128]{1,0:T(8,128)(2,1)S(1)}, u32[]{:S(2)}, u32[]{:S(2)}) collective-permute-start(bf16[176,128]{1,0:T(8,128)(2,1)S(1)} %add_convert_fusion.4), channel_id=1, source_target_pairs={{0,2},{1,3},{2,0},{3,1},{4,6},{5,7},{6,4},{7,5},{8,10},{9,11},{10,... | collective-permute-start | bytes 135176 | tf_op jit(solution)/shard_map/ppermute | solution.py:368
  44.7 1.6 %collective-permute-done.21 = bf16[480,128]{1,0:T(8,128)(2,1)S(1)} collective-permute-done((bf16[480,128]{1,0:T(8,128)(2,1)S(1)}, bf16[480,128]{1,0:T(8,128)(2,1)S(1)}, u32[]{:S(2)}, u32[]{:S(2)}) %collective-permute-start.21) | collective-permute-done | bytes 122912 | tf_op jit(solution)/shard_map/ppermute | solution.py:368
  46.4 0.8 %collective-permute-done.23 = bf16[176,128]{1,0:T(8,128)(2,1)S(1)} collective-permute-done((bf16[176,128]{1,0:T(8,128)(2,1)S(1)}, bf16[176,128]{1,0:T(8,128)(2,1)S(1)}, u32[]{:S(2)}, u32[]{:S(2)}) %collective-permute-start.23) | collective-permute-done | bytes 45088 | tf_op jit(solution)/shard_map/ppermute | solution.py:368
  47.3 1.2 %collective-permute-done.24.other_b_ref = bf16[176,128]{1,0:T(8,128)(2,1)S(1)} collective-permute-done((bf16[176,128]{1,0:T(8,128)(2,1)S(1)}, bf16[176,128]{1,0:T(8,128)(2,1)S(1)}, u32[]{:S(2)}, u32[]{:S(2)}) %collective-permute-start.24) | collective-permute-done | bytes 45088 | tf_op jit(solution)/shard_map/ppermute | solution.py:368
  48.5 0.8 %shard_map.124 = (f32[1024,128]{1,0:T(8,128)}, f32[32,256]{1,0:T(8,128)}, f32[32,256]{1,0:T(8,128)}, f32[1,128]{1,0:T(1,128)}) custom-call(s32[1]{0:T(128)} %bitcast.pos_ref, bf16[480,128]{1,0:T(8,128)(2,1)S(1)} %add_convert_fusion.own_a_ref, bf16[480,128]{1,0:T(8,128)(2,1)S(1)} %collective-permute-done.22.other_a_ref, ...), custom_call_target="tpu_custom_call" | custom-call | tf_op jit(solution)/shard_map/pallas_call | solution.py:449
  (61 shorter events, 5.9 us)
Async XLA Ops:
  3.8 9.5 %collective-permute-start.15 = (bf16[32,1024]{1,0:T(8,128)(2,1)}, bf16[32,1024]{1,0:T(8,128)(2,1)S(1)}, u32[]{:S(2)}, u32[]{:S(2)}) collective-permute-start(bf16[32,1024]{1,0:T(8,128)(2,1)} %get-tuple-element.60.refs_16_.maskb_ref), channel_id=1, source_target_pairs={{0,1},{1,0},{2,3},{3,2},{4,5},{5,4},{6,7},{7,6},{8,9},{9,8},{10,11... | collective-permute-start | bytes 196616 | tf_op jit(solution)/shard_map/ppermute | solution.py:368
  4.3 7.1 %collective-permute-start.16 = (bf16[256,32]{1,0:T(8,128)(2,1)}, bf16[256,32]{1,0:T(8,128)(2,1)S(1)}, u32[]{:S(2)}, u32[]{:S(2)}) collective-permute-start(bf16[256,32]{1,0:T(8,128)(2,1)} %get-tuple-element.61.refs_18_), channel_id=1, source_target_pairs={{0,1},{1,0},{2,3},{3,2},{4,5},{5,4},{6,7},{7,6},{8,9},{9,8},{10,11... | collective-permute-start | bytes 49160 | tf_op jit(solution)/shard_map/ppermute | solution.py:368
  4.4 10.4 %collective-permute-start = (bf16[8,4224]{1,0:T(8,128)(2,1)}, bf16[8,4224]{1,0:T(8,128)(2,1)S(1)}, u32[]{:S(2)}, u32[]{:S(2)}) collective-permute-start(bf16[8,4224]{1,0:T(8,128)(2,1)} %get-tuple-element.44), channel_id=1, source_target_pairs={{0,12},{1,13},{2,14},{3,15},{4,8},{5,9},{6,10},{7,11},{8,4},{9,5},... | collective-permute-start | bytes 202760 | tf_op jit(solution)/shard_map/ppermute | solution.py:368
  9.5 7.7 %collective-permute-start.1 = (bf16[8,4224]{1,0:T(8,128)(2,1)}, bf16[8,4224]{1,0:T(8,128)(2,1)S(1)}, u32[]{:S(2)}, u32[]{:S(2)}) collective-permute-start(bf16[8,4224]{1,0:T(8,128)(2,1)} %get-tuple-element.45), channel_id=1, source_target_pairs={{0,14},{1,15},{2,12},{3,13},{4,10},{5,11},{6,8},{7,9},{8,6},{9,7},... | collective-permute-start | bytes 202760 | tf_op jit(solution)/shard_map/ppermute | solution.py:368
  10.6 10.1 %collective-permute-start.2 = (bf16[8,4224]{1,0:T(8,128)(2,1)}, bf16[8,4224]{1,0:T(8,128)(2,1)S(1)}, u32[]{:S(2)}, u32[]{:S(2)}) collective-permute-start(bf16[8,4224]{1,0:T(8,128)(2,1)} %get-tuple-element.46), channel_id=1, source_target_pairs={{0,8},{1,9},{2,10},{3,11},{4,12},{5,13},{6,14},{7,15},{8,0},{9,1},... | collective-permute-start | bytes 202760 | tf_op jit(solution)/shard_map/ppermute | solution.py:368
  11.4 11.0 %collective-permute-start.3 = (bf16[8,4224]{1,0:T(8,128)(2,1)}, bf16[8,4224]{1,0:T(8,128)(2,1)S(1)}, u32[]{:S(2)}, u32[]{:S(2)}) collective-permute-start(bf16[8,4224]{1,0:T(8,128)(2,1)} %get-tuple-element.47), channel_id=1, source_target_pairs={{0,10},{1,11},{2,8},{3,9},{4,14},{5,15},{6,12},{7,13},{8,2},{9,3},... | collective-permute-start | bytes 202760 | tf_op jit(solution)/shard_map/ppermute | solution.py:368
  13.3 9.1 %collective-permute-start.4 = (bf16[8,4224]{1,0:T(8,128)(2,1)}, bf16[8,4224]{1,0:T(8,128)(2,1)S(1)}, u32[]{:S(2)}, u32[]{:S(2)}) collective-permute-start(bf16[8,4224]{1,0:T(8,128)(2,1)} %get-tuple-element.48), channel_id=1, source_target_pairs={{0,4},{1,5},{2,6},{3,7},{4,0},{5,1},{6,2},{7,3},{8,12},{9,13},{10,... | collective-permute-start | bytes 202760 | tf_op jit(solution)/shard_map/ppermute | solution.py:368
  14.8 8.1 %collective-permute-start.5 = (bf16[8,4224]{1,0:T(8,128)(2,1)}, bf16[8,4224]{1,0:T(8,128)(2,1)S(1)}, u32[]{:S(2)}, u32[]{:S(2)}) collective-permute-start(bf16[8,4224]{1,0:T(8,128)(2,1)} %get-tuple-element.49), channel_id=1, source_target_pairs={{0,6},{1,7},{2,4},{3,5},{4,2},{5,3},{6,0},{7,1},{8,14},{9,15},{10,... | collective-permute-start | bytes 202760 | tf_op jit(solution)/shard_map/ppermute | solution.py:368
  17.1 5.9 %collective-permute-start.6 = (bf16[8,4224]{1,0:T(8,128)(2,1)}, bf16[8,4224]{1,0:T(8,128)(2,1)S(1)}, u32[]{:S(2)}, u32[]{:S(2)}) collective-permute-start(bf16[8,4224]{1,0:T(8,128)(2,1)} %get-tuple-element.51), channel_id=1, source_target_pairs={{0,2},{1,3},{2,0},{3,1},{4,6},{5,7},{6,4},{7,5},{8,10},{9,11},{10,... | collective-permute-start | bytes 202760 | tf_op jit(solution)/shard_map/ppermute | solution.py:368
  20.7 2.7 %collective-permute-start.13 = (bf16[8,4224]{1,0:T(8,128)(2,1)}, bf16[8,4224]{1,0:T(8,128)(2,1)S(1)}, u32[]{:S(2)}, u32[]{:S(2)}) collective-permute-start(bf16[8,4224]{1,0:T(8,128)(2,1)} %get-tuple-element.58.refs_6_), channel_id=1, source_target_pairs={{0,1},{1,0},{2,3},{3,2},{4,5},{5,4},{6,7},{7,6},{8,9},{9,8},{10,11... | collective-permute-start | bytes 202760 | tf_op jit(solution)/shard_map/ppermute | solution.py:368
  22.4 1.5 %collective-permute-start.8 = (bf16[8,4224]{1,0:T(8,128)(2,1)S(1)}, bf16[8,4224]{1,0:T(8,128)(2,1)S(1)}, u32[]{:S(2)}, u32[]{:S(2)}) collective-permute-start(bf16[8,4224]{1,0:T(8,128)(2,1)S(1)} %collective-permute-done.1.refs_1_), channel_id=1, source_target_pairs={{0,1},{1,0},{2,3},{3,2},{4,5},{5,4},{6,7},{7,6},{8,9},{9,8},{10,11... | collective-permute-start | bytes 202760 | tf_op jit(solution)/shard_map/ppermute | solution.py:368
  22.9 1.6 %collective-permute-start.9 = (bf16[8,4224]{1,0:T(8,128)(2,1)S(1)}, bf16[8,4224]{1,0:T(8,128)(2,1)S(1)}, u32[]{:S(2)}, u32[]{:S(2)}) collective-permute-start(bf16[8,4224]{1,0:T(8,128)(2,1)S(1)} %collective-permute-done.2.refs_2_), channel_id=1, source_target_pairs={{0,1},{1,0},{2,3},{3,2},{4,5},{5,4},{6,7},{7,6},{8,9},{9,8},{10,11... | collective-permute-start | bytes 202760 | tf_op jit(solution)/shard_map/ppermute | solution.py:368
  23.0 1.6 %collective-permute-start.10 = (bf16[8,4224]{1,0:T(8,128)(2,1)S(1)}, bf16[8,4224]{1,0:T(8,128)(2,1)S(1)}, u32[]{:S(2)}, u32[]{:S(2)}) collective-permute-start(bf16[8,4224]{1,0:T(8,128)(2,1)S(1)} %collective-permute-done.3.refs_3_), channel_id=1, source_target_pairs={{0,1},{1,0},{2,3},{3,2},{4,5},{5,4},{6,7},{7,6},{8,9},{9,8},{10,11... | collective-permute-start | bytes 202760 | tf_op jit(solution)/shard_map/ppermute | solution.py:368
  23.5 1.3 %collective-permute-start.11 = (bf16[8,4224]{1,0:T(8,128)(2,1)S(1)}, bf16[8,4224]{1,0:T(8,128)(2,1)S(1)}, u32[]{:S(2)}, u32[]{:S(2)}) collective-permute-start(bf16[8,4224]{1,0:T(8,128)(2,1)S(1)} %collective-permute-done.4.refs_4_), channel_id=1, source_target_pairs={{0,1},{1,0},{2,3},{3,2},{4,5},{5,4},{6,7},{7,6},{8,9},{9,8},{10,11... | collective-permute-start | bytes 202760 | tf_op jit(solution)/shard_map/ppermute | solution.py:368
  23.7 1.3 %collective-permute-start.12 = (bf16[8,4224]{1,0:T(8,128)(2,1)S(1)}, bf16[8,4224]{1,0:T(8,128)(2,1)S(1)}, u32[]{:S(2)}, u32[]{:S(2)}) collective-permute-start(bf16[8,4224]{1,0:T(8,128)(2,1)S(1)} %collective-permute-done.5.refs_5_), channel_id=1, source_target_pairs={{0,1},{1,0},{2,3},{3,2},{4,5},{5,4},{6,7},{7,6},{8,9},{9,8},{10,11... | collective-permute-start | bytes 202760 | tf_op jit(solution)/shard_map/ppermute | solution.py:368
  24.0 1.3 %collective-permute-start.14 = (bf16[8,4224]{1,0:T(8,128)(2,1)S(1)}, bf16[8,4224]{1,0:T(8,128)(2,1)S(1)}, u32[]{:S(2)}, u32[]{:S(2)}) collective-permute-start(bf16[8,4224]{1,0:T(8,128)(2,1)S(1)} %collective-permute-done.6.refs_7_), channel_id=1, source_target_pairs={{0,1},{1,0},{2,3},{3,2},{4,5},{5,4},{6,7},{7,6},{8,9},{9,8},{10,11... | collective-permute-start | bytes 202760 | tf_op jit(solution)/shard_map/ppermute | solution.py:368
  26.9 7.2 %collective-permute-start.19 = (bf16[480,128]{1,0:T(8,128)(2,1)S(1)}, bf16[480,128]{1,0:T(8,128)(2,1)S(1)}, u32[]{:S(2)}, u32[]{:S(2)}) collective-permute-start(bf16[480,128]{1,0:T(8,128)(2,1)S(1)} %get-tuple-element.76), channel_id=1, source_target_pairs={{0,2},{1,3},{2,0},{3,1},{4,6},{5,7},{6,4},{7,5},{8,10},{9,11},{10,... | collective-permute-start | bytes 368648 | tf_op jit(solution)/shard_map/ppermute | solution.py:368
  30.0 4.1 %collective-permute-start.17 = (bf16[176,128]{1,0:T(8,128)(2,1)S(1)}, bf16[176,128]{1,0:T(8,128)(2,1)S(1)}, u32[]{:S(2)}, u32[]{:S(2)}) collective-permute-start(bf16[176,128]{1,0:T(8,128)(2,1)S(1)} %get-tuple-element.70), channel_id=1, source_target_pairs={{0,4},{1,5},{2,6},{3,7},{4,0},{5,1},{6,2},{7,3},{8,12},{9,13},{10,... | collective-permute-start | bytes 135176 | tf_op jit(solution)/shard_map/ppermute | solution.py:368
  34.2 6.2 %collective-permute-start.20 = (bf16[480,128]{1,0:T(8,128)(2,1)S(1)}, bf16[480,128]{1,0:T(8,128)(2,1)S(1)}, u32[]{:S(2)}, u32[]{:S(2)}) collective-permute-start(bf16[480,128]{1,0:T(8,128)(2,1)S(1)} %add_convert_fusion.2), channel_id=1, source_target_pairs={{0,4},{1,5},{2,6},{3,7},{4,0},{5,1},{6,2},{7,3},{8,12},{9,13},{10,... | collective-permute-start | bytes 368648 | tf_op jit(solution)/shard_map/ppermute | solution.py:368
  35.4 5.0 %collective-permute-start.18 = (bf16[176,128]{1,0:T(8,128)(2,1)S(1)}, bf16[176,128]{1,0:T(8,128)(2,1)S(1)}, u32[]{:S(2)}, u32[]{:S(2)}) collective-permute-start(bf16[176,128]{1,0:T(8,128)(2,1)S(1)} %add_convert_fusion.5), channel_id=1, source_target_pairs={{0,8},{1,9},{2,10},{3,11},{4,12},{5,13},{6,14},{7,15},{8,0},{9,1},... | collective-permute-start | bytes 135176 | tf_op jit(solution)/shard_map/ppermute | solution.py:368
  40.4 5.8 %collective-permute-start.21 = (bf16[480,128]{1,0:T(8,128)(2,1)S(1)}, bf16[480,128]{1,0:T(8,128)(2,1)S(1)}, u32[]{:S(2)}, u32[]{:S(2)}) collective-permute-start(bf16[480,128]{1,0:T(8,128)(2,1)S(1)} %add_convert_fusion.1), channel_id=1, source_target_pairs={{0,8},{1,9},{2,10},{3,11},{4,12},{5,13},{6,14},{7,15},{8,0},{9,1},... | collective-permute-start | bytes 368648 | tf_op jit(solution)/shard_map/ppermute | solution.py:368
  43.1 4.1 %collective-permute-start.23 = (bf16[176,128]{1,0:T(8,128)(2,1)S(1)}, bf16[176,128]{1,0:T(8,128)(2,1)S(1)}, u32[]{:S(2)}, u32[]{:S(2)}) collective-permute-start(bf16[176,128]{1,0:T(8,128)(2,1)S(1)} %add_convert_fusion.4), channel_id=1, source_target_pairs={{0,2},{1,3},{2,0},{3,1},{4,6},{5,7},{6,4},{7,5},{8,10},{9,11},{10,... | collective-permute-start | bytes 135176 | tf_op jit(solution)/shard_map/ppermute | solution.py:368
  46.3 2.2 %collective-permute-start.22 = (bf16[480,128]{1,0:T(8,128)(2,1)S(1)}, bf16[480,128]{1,0:T(8,128)(2,1)S(1)}, u32[]{:S(2)}, u32[]{:S(2)}) collective-permute-start(bf16[480,128]{1,0:T(8,128)(2,1)S(1)} %add_convert_fusion.own_a_ref), channel_id=1, source_target_pairs={{0,1},{1,0},{2,3},{3,2},{4,5},{5,4},{6,7},{7,6},{8,9},{9,8},{10,11... | collective-permute-start | bytes 368648 | tf_op jit(solution)/shard_map/ppermute | solution.py:368
  47.2 1.3 %collective-permute-start.24 = (bf16[176,128]{1,0:T(8,128)(2,1)S(1)}, bf16[176,128]{1,0:T(8,128)(2,1)S(1)}, u32[]{:S(2)}, u32[]{:S(2)}) collective-permute-start(bf16[176,128]{1,0:T(8,128)(2,1)S(1)} %add_convert_fusion.3.own_b_ref), channel_id=1, source_target_pairs={{0,1},{1,0},{2,3},{3,2},{4,5},{5,4},{6,7},{7,6},{8,9},{9,8},{10,11... | collective-permute-start | bytes 135176 | tf_op jit(solution)/shard_map/ppermute | solution.py:368
  (12 other events, 59.7 us)

commit v6 on v5

--- a/solution.py
+++ b/solution.py
@@ -85,22 +85,23 @@
         maskb_scr[:, k * LANES : (k + 1) * LANES] = cols[k].astype(BF16)
     send(maskb_scr, maskb_ref)
     mask_rows = jnp.concatenate(cols, axis=0)
-    left = (dot(low, wf_ref[...], 1, 1) * mask_rows[:, :width]).astype(BF16)
-    right = (dot(low, wl_ref[...], 1, 1) * mask_rows[:, :width]).astype(BF16)
+    weights = jnp.concatenate([wl_ref[...], wf_ref[...]], axis=0)
+    both = (dot(low, weights, 1, 1) * mask_rows[:, : 2 * width]).astype(BF16)
+    right, left = both[:, :width], both[:, width:]
     left_scr[...] = left
     right_scr[...] = right
     send(left_scr, left_ref)
     send(right_scr, right_ref)
     spread_to = (
-        lax.broadcasted_iota(jnp.int32, (width, wide), 1) // homologs
-        == lax.broadcasted_iota(jnp.int32, (width, wide), 0)
+        lax.broadcasted_iota(jnp.int32, (2 * width, 2 * wide), 1) // homologs
+        == lax.broadcasted_iota(jnp.int32, (2 * width, 2 * wide), 0)
     ).astype(BF16)
     own_tile = (
         lax.broadcasted_iota(jnp.int32, (homologs, LANES), 1) % homologs
         == lax.broadcasted_iota(jnp.int32, (homologs, LANES), 0)
     ).astype(F32)
     own_rows = jnp.concatenate([own_tile] * lines, axis=0)
-    own = jnp.concatenate([own_rows] * (wide // LANES), axis=1)
+    own = jnp.concatenate([own_rows] * (2 * wide // LANES), axis=1)
     first = (lax.broadcasted_iota(jnp.int32, (rows, LANES), 1) < homologs).astype(F32)
     fold = (
         lax.broadcasted_iota(jnp.int32, (lines, rows), 1) // homologs
@@ -108,13 +109,12 @@
     ).astype(BF16)
     same = jnp.concatenate(
         [
-            dot(fold, (dot(right, spread_to) * own).astype(BF16)),
-            dot(fold, (dot(left, spread_to) * own).astype(BF16)),
-            dot(fold, (mask_rows * own_rows * first).astype(BF16)),
+            (dot(both, spread_to) * own).astype(BF16),
+            (mask_rows * own_rows * first).astype(BF16),
         ],
         axis=1,
     )
-    same = same.astype(BF16)
+    same = dot(fold, same).astype(BF16)
     base = same.shape[1]
     cols = lines * pair_ch
     copies[4].wait()
@@ -290,7 +290,7 @@
 
 
 def last_kernel(
-    total, pos_ref, own_a_ref, other_a_ref, own_b_ref, other_b_ref,
+    total, pos_ref, own_b_ref, other_b_ref, own_a_ref, other_a_ref,
     out_ref, former_ref, latter_ref, offset_ref,
 ):
     scale = 1.0 / total
@@ -456,7 +456,7 @@
         ],
         smem=1,
         ins=4,
-    )(pos, sums, swap(sums, 1), parts, swap(parts, 1))
+    )(pos, parts, swap(parts, 1), sums, swap(sums, 1))
     return update, d_msa, d_former.T, d_latter.T, d_out, d_offset.reshape(pair_ch)
 
 

time: 49.5 us -> 49.4 us (level)
  no operation moved by 1% of the time
where the time goes in v6:
time: 49.4 us; the launch traced here: 49.3 us
  starting transfers between devices  25.6 us (52%)
  waiting for transfers between devices  11.1 us (22%)
  Pallas kernels  11 us (22%)
  between operations  0.8 us (2%)
  local copies, waits for them, and re-layouts  0.7 us (1%)
    ppermute x25, starting transfers between devices, swap(): lax.ppermute(x, ('chip', 'core'), [(i, i ^ step) for i in range(size)])  25.6 us
    ppermute x25, waiting for transfers between devices, swap(): lax.ppermute(x, ('chip', 'core'), [(i, i ^ step) for i in range(size)])  11.1 us
    pallas_call x1, Pallas kernels, body(): call(pre_kernel, [((rows, width), BF16), ((rows, width), BF16), ((homolog...  3.06 us
    pallas_call x1, Pallas kernels, body(): call(grads_kernel, [((half - early + 4 * width + 16, pair_ch), BF16), ((2...  2.45 us
    pallas_call x1, Pallas kernels, make_update(): call(update_kernel, [((lines, total, pair_ch), BF16)], [((wide, cols), BF...  1.68 us
    pallas_call x1, Pallas kernels, body(): call(functools.partial(half_kernel, offsets), [((early, pair_ch), BF16),...  1.61 us
    pallas_call x1, Pallas kernels, make_d_msa(): call(msa_kernel, [((homologs, lines, depth), BF16)], [((depth // LANES, r...  1.02 us
  transfers between devices with their start and end apart: 25, of which 12 were waited for; matrix products, arithmetic and copies ran while one was open for 0% of the time, Pallas kernels for 11%

profile of v6, /device:TPU:0, one launch (start us, length us, event | category | flops | bytes accessed | tf_op | source)
XLA Modules:
  0.0 49.3 jit_solution(8781066049472815056)
XLA Ops:
  0.6 3.1 %shard_map.118 = (bf16[256,32]{1,0:T(8,128)(2,1)}, bf16[256,32]{1,0:T(8,128)(2,1)}, bf16[32,1024]{1,0:T(8,128)(2,1)}, bf16[256,256]{1,0:T(8,128)(2,1)}, bf16[8,4...) custom-call(s32[1]{0:T(128)} %bitcast.pos_ref, ...), custom_call_target="tpu_custom_call" | custom-call | tf_op jit(solution)/shard_map/pallas_call | solution.py:343
  4.3 5.0 %collective-permute-start = (bf16[8,4224]{1,0:T(8,128)(2,1)}, bf16[8,4224]{1,0:T(8,128)(2,1)S(1)}, u32[]{:S(2)}, u32[]{:S(2)}) collective-permute-start(bf16[8,4224]{1,0:T(8,128)(2,1)} %get-tuple-element.44), channel_id=1, source_target_pairs={{0,12},{1,13},{2,14},{3,15},{4,8},{5,9},{6,10},{7,11},{8,4},{9,5},... | collective-permute-start | bytes 202760 | tf_op jit(solution)/shard_map/ppermute | solution.py:368
  9.3 1.1 %collective-permute-start.1 = (bf16[8,4224]{1,0:T(8,128)(2,1)}, bf16[8,4224]{1,0:T(8,128)(2,1)S(1)}, u32[]{:S(2)}, u32[]{:S(2)}) collective-permute-start(bf16[8,4224]{1,0:T(8,128)(2,1)} %get-tuple-element.45), channel_id=1, source_target_pairs={{0,14},{1,15},{2,12},{3,13},{4,10},{5,11},{6,8},{7,9},{8,6},{9,7},... | collective-permute-start | bytes 202760 | tf_op jit(solution)/shard_map/ppermute | solution.py:368
  10.5 0.8 %collective-permute-start.2 = (bf16[8,4224]{1,0:T(8,128)(2,1)}, bf16[8,4224]{1,0:T(8,128)(2,1)S(1)}, u32[]{:S(2)}, u32[]{:S(2)}) collective-permute-start(bf16[8,4224]{1,0:T(8,128)(2,1)} %get-tuple-element.46), channel_id=1, source_target_pairs={{0,8},{1,9},{2,10},{3,11},{4,12},{5,13},{6,14},{7,15},{8,0},{9,1},... | collective-permute-start | bytes 202760 | tf_op jit(solution)/shard_map/ppermute | solution.py:368
  11.3 1.9 %collective-permute-start.3 = (bf16[8,4224]{1,0:T(8,128)(2,1)}, bf16[8,4224]{1,0:T(8,128)(2,1)S(1)}, u32[]{:S(2)}, u32[]{:S(2)}) collective-permute-start(bf16[8,4224]{1,0:T(8,128)(2,1)} %get-tuple-element.47), channel_id=1, source_target_pairs={{0,10},{1,11},{2,8},{3,9},{4,14},{5,15},{6,12},{7,13},{8,2},{9,3},... | collective-permute-start | bytes 202760 | tf_op jit(solution)/shard_map/ppermute | solution.py:368
  13.2 1.5 %collective-permute-start.4 = (bf16[8,4224]{1,0:T(8,128)(2,1)}, bf16[8,4224]{1,0:T(8,128)(2,1)S(1)}, u32[]{:S(2)}, u32[]{:S(2)}) collective-permute-start(bf16[8,4224]{1,0:T(8,128)(2,1)} %get-tuple-element.48), channel_id=1, source_target_pairs={{0,4},{1,5},{2,6},{3,7},{4,0},{5,1},{6,2},{7,3},{8,12},{9,13},{10,... | collective-permute-start | bytes 202760 | tf_op jit(solution)/shard_map/ppermute | solution.py:368
  14.7 1.6 %collective-permute-start.5 = (bf16[8,4224]{1,0:T(8,128)(2,1)}, bf16[8,4224]{1,0:T(8,128)(2,1)S(1)}, u32[]{:S(2)}, u32[]{:S(2)}) collective-permute-start(bf16[8,4224]{1,0:T(8,128)(2,1)} %get-tuple-element.49), channel_id=1, source_target_pairs={{0,6},{1,7},{2,4},{3,5},{4,2},{5,3},{6,0},{7,1},{8,14},{9,15},{10,... | collective-permute-start | bytes 202760 | tf_op jit(solution)/shard_map/ppermute | solution.py:368
  17.0 1.4 %collective-permute-start.6 = (bf16[8,4224]{1,0:T(8,128)(2,1)}, bf16[8,4224]{1,0:T(8,128)(2,1)S(1)}, u32[]{:S(2)}, u32[]{:S(2)}) collective-permute-start(bf16[8,4224]{1,0:T(8,128)(2,1)} %get-tuple-element.51), channel_id=1, source_target_pairs={{0,2},{1,3},{2,0},{3,1},{4,6},{5,7},{6,4},{7,5},{8,10},{9,11},{10,... | collective-permute-start | bytes 202760 | tf_op jit(solution)/shard_map/ppermute | solution.py:368
  18.4 2.2 %collective-permute-done.2.refs_2_ = bf16[8,4224]{1,0:T(8,128)(2,1)S(1)} collective-permute-done((bf16[8,4224]{1,0:T(8,128)(2,1)}, bf16[8,4224]{1,0:T(8,128)(2,1)S(1)}, u32[]{:S(2)}, u32[]{:S(2)}) %collective-permute-start.2) | collective-permute-done | bytes 67616 | tf_op jit(solution)/shard_map/ppermute | solution.py:368
  20.6 1.7 %collective-permute-done.3.refs_3_ = bf16[8,4224]{1,0:T(8,128)(2,1)S(1)} collective-permute-done((bf16[8,4224]{1,0:T(8,128)(2,1)}, bf16[8,4224]{1,0:T(8,128)(2,1)S(1)}, u32[]{:S(2)}, u32[]{:S(2)}) %collective-permute-start.3) | collective-permute-done | bytes 67616 | tf_op jit(solution)/shard_map/ppermute | solution.py:368
  25.2 1.6 %shard_map.120 = (bf16[480,128]{1,0:T(8,128)(2,1)S(1)}, bf16[32,128]{1,0:T(8,128)(2,1)S(1)}, bf16[128,1024]{1,0:T(8,128)(2,1)S(1)}, bf16[128,1024]{1,0:T(8,128)(...) custom-call(s32[1]{0:T(128)} %bitcast.pos_ref, ...), custom_call_target="tpu_custom_call" | custom-call | tf_op jit(solution)/shard_map/pallas_call | solution.py:391
  27.5 2.5 %shard_map.121 = (bf16[176,128]{1,0:T(8,128)(2,1)S(1)}, bf16[2,256,32]{2,1,0:T(8,128)(2,1)S(1)}) custom-call(s32[1]{0:T(128)} %bitcast.pos_ref, bf16[256,2048]{1,0:T(8,128)(2,1)S(1)} %get-tuple-element.62.p_ref, bf16[128,1024]{1,0:T(8,128)(2,1)S(1)} %get-tuple-element.63.right_ref, bf16[128,1024]{1,0:T(8,128)(2,1)S(1)} %get-tuple-element.64.left_ref, ...), custom_call_target="tpu_custom_call" | custom-call | tf_op jit(solution)/shard_map/pallas_call | solution.py:406
  29.9 1.2 %collective-permute-start.17 = (bf16[176,128]{1,0:T(8,128)(2,1)S(1)}, bf16[176,128]{1,0:T(8,128)(2,1)S(1)}, u32[]{:S(2)}, u32[]{:S(2)}) collective-permute-start(bf16[176,128]{1,0:T(8,128)(2,1)S(1)} %get-tuple-element.70), channel_id=1, source_target_pairs={{0,4},{1,5},{2,6},{3,7},{4,0},{5,1},{6,2},{7,3},{8,12},{9,13},{10,... | collective-permute-start | bytes 135176 | tf_op jit(solution)/shard_map/ppermute | solution.py:368
  31.1 1.0 %shard_map.122 = bf16[32,8,256]{2,1,0:T(8,128)(2,1)} custom-call(bf16[32,8,256]{2,1,0:T(8,128)(2,1)S(1)} %copy-done.2, bf16[2,256,32]{2,1,0:T(8,128)(2,1)S(1)} %get-tuple-element.71.grads_ref, bf16[32,256]{1,0:T(8,128)(2,1)S(1)} %bitcast.9, bf16[32,256]{1,0:T(8,128)(2,1)S(1)} %bitcast.11), custom_call_target="tpu_custom_call" | custom-call | flops 8388608 | tf_op jit(solution)/shard_map/pallas_call | solution.py:428
  32.1 1.9 %collective-permute-done.17 = bf16[176,128]{1,0:T(8,128)(2,1)S(1)} collective-permute-done((bf16[176,128]{1,0:T(8,128)(2,1)S(1)}, bf16[176,128]{1,0:T(8,128)(2,1)S(1)}, u32[]{:S(2)}, u32[]{:S(2)}) %collective-permute-start.17) | collective-permute-done | bytes 45088 | tf_op jit(solution)/shard_map/ppermute | solution.py:368
  34.1 1.2 %collective-permute-start.22 = (bf16[480,128]{1,0:T(8,128)(2,1)S(1)}, bf16[480,128]{1,0:T(8,128)(2,1)S(1)}, u32[]{:S(2)}, u32[]{:S(2)}) collective-permute-start(bf16[480,128]{1,0:T(8,128)(2,1)S(1)} %add_convert_fusion.2), channel_id=1, source_target_pairs={{0,4},{1,5},{2,6},{3,7},{4,0},{5,1},{6,2},{7,3},{8,12},{9,13},{10,... | collective-permute-start | bytes 368648 | tf_op jit(solution)/shard_map/ppermute | solution.py:368
  35.3 2.5 %collective-permute-start.18 = (bf16[176,128]{1,0:T(8,128)(2,1)S(1)}, bf16[176,128]{1,0:T(8,128)(2,1)S(1)}, u32[]{:S(2)}, u32[]{:S(2)}) collective-permute-start(bf16[176,128]{1,0:T(8,128)(2,1)S(1)} %add_convert_fusion.5), channel_id=1, source_target_pairs={{0,8},{1,9},{2,10},{3,11},{4,12},{5,13},{6,14},{7,15},{8,0},{9,1},... | collective-permute-start | bytes 135176 | tf_op jit(solution)/shard_map/ppermute | solution.py:368
  38.5 1.7 %shard_map.123 = bf16[8,128,128]{2,1,0:T(8,128)(2,1)} custom-call(bf16[128,1024]{1,0:T(8,128)(2,1)S(1)} %get-tuple-element.63.right_ref, f32[128,1024]{1,0:T(8,128)S(1)} %get-tuple-element.66.inv_ref, bf16[256,32]{1,0:T(8,128)(2,1)S(1)} %copy-done.6, bf16[32,4096]{1,0:T(8,128)(2,1)S(1)} %shard_map.119.wleft_ref, f32[1,128]{1,0:T(1,128)S(1)} %bitcast.12), custom_call_target="tpu_custom_call" | custom-call | flops 268435456 | tf_op jit(solution)/shard_map/pallas_call | solution.py:418
  40.3 2.6 %collective-permute-start.23 = (bf16[480,128]{1,0:T(8,128)(2,1)S(1)}, bf16[480,128]{1,0:T(8,128)(2,1)S(1)}, u32[]{:S(2)}, u32[]{:S(2)}) collective-permute-start(bf16[480,128]{1,0:T(8,128)(2,1)S(1)} %add_convert_fusion.1), channel_id=1, source_target_pairs={{0,8},{1,9},{2,10},{3,11},{4,12},{5,13},{6,14},{7,15},{8,0},{9,1},... | collective-permute-start | bytes 368648 | tf_op jit(solution)/shard_map/ppermute | solution.py:368
  43.0 1.6 %collective-permute-start.19 = (bf16[176,128]{1,0:T(8,128)(2,1)S(1)}, bf16[176,128]{1,0:T(8,128)(2,1)S(1)}, u32[]{:S(2)}, u32[]{:S(2)}) collective-permute-start(bf16[176,128]{1,0:T(8,128)(2,1)S(1)} %add_convert_fusion.4), channel_id=1, source_target_pairs={{0,2},{1,3},{2,0},{3,1},{4,6},{5,7},{6,4},{7,5},{8,10},{9,11},{10,... | collective-permute-start | bytes 135176 | tf_op jit(solution)/shard_map/ppermute | solution.py:368
  44.6 1.6 %collective-permute-done.23 = bf16[480,128]{1,0:T(8,128)(2,1)S(1)} collective-permute-done((bf16[480,128]{1,0:T(8,128)(2,1)S(1)}, bf16[480,128]{1,0:T(8,128)(2,1)S(1)}, u32[]{:S(2)}, u32[]{:S(2)}) %collective-permute-start.23) | collective-permute-done | bytes 122912 | tf_op jit(solution)/shard_map/ppermute | solution.py:368
  46.3 0.8 %collective-permute-done.19 = bf16[176,128]{1,0:T(8,128)(2,1)S(1)} collective-permute-done((bf16[176,128]{1,0:T(8,128)(2,1)S(1)}, bf16[176,128]{1,0:T(8,128)(2,1)S(1)}, u32[]{:S(2)}, u32[]{:S(2)}) %collective-permute-start.19) | collective-permute-done | bytes 45088 | tf_op jit(solution)/shard_map/ppermute | solution.py:368
  47.2 1.2 %collective-permute-done.20.other_b_ref = bf16[176,128]{1,0:T(8,128)(2,1)S(1)} collective-permute-done((bf16[176,128]{1,0:T(8,128)(2,1)S(1)}, bf16[176,128]{1,0:T(8,128)(2,1)S(1)}, u32[]{:S(2)}, u32[]{:S(2)}) %collective-permute-start.20) | collective-permute-done | bytes 45088 | tf_op jit(solution)/shard_map/ppermute | solution.py:368
  48.4 0.8 %shard_map.124 = (f32[1024,128]{1,0:T(8,128)}, f32[32,256]{1,0:T(8,128)}, f32[32,256]{1,0:T(8,128)}, f32[1,128]{1,0:T(1,128)}) custom-call(s32[1]{0:T(128)} %bitcast.pos_ref, bf16[176,128]{1,0:T(8,128)(2,1)S(1)} %add_convert_fusion.3.own_b_ref, bf16[176,128]{1,0:T(8,128)(2,1)S(1)} %collective-permute-done.20.other_b_ref, ...), custom_call_target="tpu_custom_call" | custom-call | tf_op jit(solution)/shard_map/pallas_call | solution.py:449
  (61 shorter events, 5.8 us)
Async XLA Ops:
  3.7 9.5 %collective-permute-start.15 = (bf16[32,1024]{1,0:T(8,128)(2,1)}, bf16[32,1024]{1,0:T(8,128)(2,1)S(1)}, u32[]{:S(2)}, u32[]{:S(2)}) collective-permute-start(bf16[32,1024]{1,0:T(8,128)(2,1)} %get-tuple-element.60.refs_16_.maskb_ref), channel_id=1, source_target_pairs={{0,1},{1,0},{2,3},{3,2},{4,5},{5,4},{6,7},{7,6},{8,9},{9,8},{10,11... | collective-permute-start | bytes 196616 | tf_op jit(solution)/shard_map/ppermute | solution.py:368
  4.2 7.1 %collective-permute-start.16 = (bf16[256,32]{1,0:T(8,128)(2,1)}, bf16[256,32]{1,0:T(8,128)(2,1)S(1)}, u32[]{:S(2)}, u32[]{:S(2)}) collective-permute-start(bf16[256,32]{1,0:T(8,128)(2,1)} %get-tuple-element.61.refs_18_), channel_id=1, source_target_pairs={{0,1},{1,0},{2,3},{3,2},{4,5},{5,4},{6,7},{7,6},{8,9},{9,8},{10,11... | collective-permute-start | bytes 49160 | tf_op jit(solution)/shard_map/ppermute | solution.py:368
  4.3 10.4 %collective-permute-start = (bf16[8,4224]{1,0:T(8,128)(2,1)}, bf16[8,4224]{1,0:T(8,128)(2,1)S(1)}, u32[]{:S(2)}, u32[]{:S(2)}) collective-permute-start(bf16[8,4224]{1,0:T(8,128)(2,1)} %get-tuple-element.44), channel_id=1, source_target_pairs={{0,12},{1,13},{2,14},{3,15},{4,8},{5,9},{6,10},{7,11},{8,4},{9,5},... | collective-permute-start | bytes 202760 | tf_op jit(solution)/shard_map/ppermute | solution.py:368
  9.3 7.7 %collective-permute-start.1 = (bf16[8,4224]{1,0:T(8,128)(2,1)}, bf16[8,4224]{1,0:T(8,128)(2,1)S(1)}, u32[]{:S(2)}, u32[]{:S(2)}) collective-permute-start(bf16[8,4224]{1,0:T(8,128)(2,1)} %get-tuple-element.45), channel_id=1, source_target_pairs={{0,14},{1,15},{2,12},{3,13},{4,10},{5,11},{6,8},{7,9},{8,6},{9,7},... | collective-permute-start | bytes 202760 | tf_op jit(solution)/shard_map/ppermute | solution.py:368
  10.5 10.1 %collective-permute-start.2 = (bf16[8,4224]{1,0:T(8,128)(2,1)}, bf16[8,4224]{1,0:T(8,128)(2,1)S(1)}, u32[]{:S(2)}, u32[]{:S(2)}) collective-permute-start(bf16[8,4224]{1,0:T(8,128)(2,1)} %get-tuple-element.46), channel_id=1, source_target_pairs={{0,8},{1,9},{2,10},{3,11},{4,12},{5,13},{6,14},{7,15},{8,0},{9,1},... | collective-permute-start | bytes 202760 | tf_op jit(solution)/shard_map/ppermute | solution.py:368
  11.3 11.0 %collective-permute-start.3 = (bf16[8,4224]{1,0:T(8,128)(2,1)}, bf16[8,4224]{1,0:T(8,128)(2,1)S(1)}, u32[]{:S(2)}, u32[]{:S(2)}) collective-permute-start(bf16[8,4224]{1,0:T(8,128)(2,1)} %get-tuple-element.47), channel_id=1, source_target_pairs={{0,10},{1,11},{2,8},{3,9},{4,14},{5,15},{6,12},{7,13},{8,2},{9,3},... | collective-permute-start | bytes 202760 | tf_op jit(solution)/shard_map/ppermute | solution.py:368
  13.2 9.1 %collective-permute-start.4 = (bf16[8,4224]{1,0:T(8,128)(2,1)}, bf16[8,4224]{1,0:T(8,128)(2,1)S(1)}, u32[]{:S(2)}, u32[]{:S(2)}) collective-permute-start(bf16[8,4224]{1,0:T(8,128)(2,1)} %get-tuple-element.48), channel_id=1, source_target_pairs={{0,4},{1,5},{2,6},{3,7},{4,0},{5,1},{6,2},{7,3},{8,12},{9,13},{10,... | collective-permute-start | bytes 202760 | tf_op jit(solution)/shard_map/ppermute | solution.py:368
  14.7 8.1 %collective-permute-start.5 = (bf16[8,4224]{1,0:T(8,128)(2,1)}, bf16[8,4224]{1,0:T(8,128)(2,1)S(1)}, u32[]{:S(2)}, u32[]{:S(2)}) collective-permute-start(bf16[8,4224]{1,0:T(8,128)(2,1)} %get-tuple-element.49), channel_id=1, source_target_pairs={{0,6},{1,7},{2,4},{3,5},{4,2},{5,3},{6,0},{7,1},{8,14},{9,15},{10,... | collective-permute-start | bytes 202760 | tf_op jit(solution)/shard_map/ppermute | solution.py:368
  17.0 5.9 %collective-permute-start.6 = (bf16[8,4224]{1,0:T(8,128)(2,1)}, bf16[8,4224]{1,0:T(8,128)(2,1)S(1)}, u32[]{:S(2)}, u32[]{:S(2)}) collective-permute-start(bf16[8,4224]{1,0:T(8,128)(2,1)} %get-tuple-element.51), channel_id=1, source_target_pairs={{0,2},{1,3},{2,0},{3,1},{4,6},{5,7},{6,4},{7,5},{8,10},{9,11},{10,... | collective-permute-start | bytes 202760 | tf_op jit(solution)/shard_map/ppermute | solution.py:368
  20.6 2.7 %collective-permute-start.13 = (bf16[8,4224]{1,0:T(8,128)(2,1)}, bf16[8,4224]{1,0:T(8,128)(2,1)S(1)}, u32[]{:S(2)}, u32[]{:S(2)}) collective-permute-start(bf16[8,4224]{1,0:T(8,128)(2,1)} %get-tuple-element.58.refs_6_), channel_id=1, source_target_pairs={{0,1},{1,0},{2,3},{3,2},{4,5},{5,4},{6,7},{7,6},{8,9},{9,8},{10,11... | collective-permute-start | bytes 202760 | tf_op jit(solution)/shard_map/ppermute | solution.py:368
  22.3 1.3 %collective-permute-start.7 = (bf16[8,4224]{1,0:T(8,128)(2,1)S(1)}, bf16[8,4224]{1,0:T(8,128)(2,1)S(1)}, u32[]{:S(2)}, u32[]{:S(2)}) collective-permute-start(bf16[8,4224]{1,0:T(8,128)(2,1)S(1)} %collective-permute-done.refs_0_), channel_id=1, source_target_pairs={{0,1},{1,0},{2,3},{3,2},{4,5},{5,4},{6,7},{7,6},{8,9},{9,8},{10,11... | collective-permute-start | bytes 202760 | tf_op jit(solution)/shard_map/ppermute | solution.py:368
  22.3 1.5 %collective-permute-start.8 = (bf16[8,4224]{1,0:T(8,128)(2,1)S(1)}, bf16[8,4224]{1,0:T(8,128)(2,1)S(1)}, u32[]{:S(2)}, u32[]{:S(2)}) collective-permute-start(bf16[8,4224]{1,0:T(8,128)(2,1)S(1)} %collective-permute-done.1.refs_1_), channel_id=1, source_target_pairs={{0,1},{1,0},{2,3},{3,2},{4,5},{5,4},{6,7},{7,6},{8,9},{9,8},{10,11... | collective-permute-start | bytes 202760 | tf_op jit(solution)/shard_map/ppermute | solution.py:368
  22.9 1.6 %collective-permute-start.9 = (bf16[8,4224]{1,0:T(8,128)(2,1)S(1)}, bf16[8,4224]{1,0:T(8,128)(2,1)S(1)}, u32[]{:S(2)}, u32[]{:S(2)}) collective-permute-start(bf16[8,4224]{1,0:T(8,128)(2,1)S(1)} %collective-permute-done.2.refs_2_), channel_id=1, source_target_pairs={{0,1},{1,0},{2,3},{3,2},{4,5},{5,4},{6,7},{7,6},{8,9},{9,8},{10,11... | collective-permute-start | bytes 202760 | tf_op jit(solution)/shard_map/ppermute | solution.py:368
  22.9 1.6 %collective-permute-start.10 = (bf16[8,4224]{1,0:T(8,128)(2,1)S(1)}, bf16[8,4224]{1,0:T(8,128)(2,1)S(1)}, u32[]{:S(2)}, u32[]{:S(2)}) collective-permute-start(bf16[8,4224]{1,0:T(8,128)(2,1)S(1)} %collective-permute-done.3.refs_3_), channel_id=1, source_target_pairs={{0,1},{1,0},{2,3},{3,2},{4,5},{5,4},{6,7},{7,6},{8,9},{9,8},{10,11... | collective-permute-start | bytes 202760 | tf_op jit(solution)/shard_map/ppermute | solution.py:368
  23.4 1.3 %collective-permute-start.11 = (bf16[8,4224]{1,0:T(8,128)(2,1)S(1)}, bf16[8,4224]{1,0:T(8,128)(2,1)S(1)}, u32[]{:S(2)}, u32[]{:S(2)}) collective-permute-start(bf16[8,4224]{1,0:T(8,128)(2,1)S(1)} %collective-permute-done.4.refs_4_), channel_id=1, source_target_pairs={{0,1},{1,0},{2,3},{3,2},{4,5},{5,4},{6,7},{7,6},{8,9},{9,8},{10,11... | collective-permute-start | bytes 202760 | tf_op jit(solution)/shard_map/ppermute | solution.py:368
  23.9 1.3 %collective-permute-start.14 = (bf16[8,4224]{1,0:T(8,128)(2,1)S(1)}, bf16[8,4224]{1,0:T(8,128)(2,1)S(1)}, u32[]{:S(2)}, u32[]{:S(2)}) collective-permute-start(bf16[8,4224]{1,0:T(8,128)(2,1)S(1)} %collective-permute-done.6.refs_7_), channel_id=1, source_target_pairs={{0,1},{1,0},{2,3},{3,2},{4,5},{5,4},{6,7},{7,6},{8,9},{9,8},{10,11... | collective-permute-start | bytes 202760 | tf_op jit(solution)/shard_map/ppermute | solution.py:368
  26.8 7.2 %collective-permute-start.21 = (bf16[480,128]{1,0:T(8,128)(2,1)S(1)}, bf16[480,128]{1,0:T(8,128)(2,1)S(1)}, u32[]{:S(2)}, u32[]{:S(2)}) collective-permute-start(bf16[480,128]{1,0:T(8,128)(2,1)S(1)} %get-tuple-element.77), channel_id=1, source_target_pairs={{0,2},{1,3},{2,0},{3,1},{4,6},{5,7},{6,4},{7,5},{8,10},{9,11},{10,... | collective-permute-start | bytes 368648 | tf_op jit(solution)/shard_map/ppermute | solution.py:368
  29.9 4.1 %collective-permute-start.17 = (bf16[176,128]{1,0:T(8,128)(2,1)S(1)}, bf16[176,128]{1,0:T(8,128)(2,1)S(1)}, u32[]{:S(2)}, u32[]{:S(2)}) collective-permute-start(bf16[176,128]{1,0:T(8,128)(2,1)S(1)} %get-tuple-element.70), channel_id=1, source_target_pairs={{0,4},{1,5},{2,6},{3,7},{4,0},{5,1},{6,2},{7,3},{8,12},{9,13},{10,... | collective-permute-start | bytes 135176 | tf_op jit(solution)/shard_map/ppermute | solution.py:368
  34.1 6.2 %collective-permute-start.22 = (bf16[480,128]{1,0:T(8,128)(2,1)S(1)}, bf16[480,128]{1,0:T(8,128)(2,1)S(1)}, u32[]{:S(2)}, u32[]{:S(2)}) collective-permute-start(bf16[480,128]{1,0:T(8,128)(2,1)S(1)} %add_convert_fusion.2), channel_id=1, source_target_pairs={{0,4},{1,5},{2,6},{3,7},{4,0},{5,1},{6,2},{7,3},{8,12},{9,13},{10,... | collective-permute-start | bytes 368648 | tf_op jit(solution)/shard_map/ppermute | solution.py:368
  35.3 5.0 %collective-permute-start.18 = (bf16[176,128]{1,0:T(8,128)(2,1)S(1)}, bf16[176,128]{1,0:T(8,128)(2,1)S(1)}, u32[]{:S(2)}, u32[]{:S(2)}) collective-permute-start(bf16[176,128]{1,0:T(8,128)(2,1)S(1)} %add_convert_fusion.5), channel_id=1, source_target_pairs={{0,8},{1,9},{2,10},{3,11},{4,12},{5,13},{6,14},{7,15},{8,0},{9,1},... | collective-permute-start | bytes 135176 | tf_op jit(solution)/shard_map/ppermute | solution.py:368
  40.3 5.8 %collective-permute-start.23 = (bf16[480,128]{1,0:T(8,128)(2,1)S(1)}, bf16[480,128]{1,0:T(8,128)(2,1)S(1)}, u32[]{:S(2)}, u32[]{:S(2)}) collective-permute-start(bf16[480,128]{1,0:T(8,128)(2,1)S(1)} %add_convert_fusion.1), channel_id=1, source_target_pairs={{0,8},{1,9},{2,10},{3,11},{4,12},{5,13},{6,14},{7,15},{8,0},{9,1},... | collective-permute-start | bytes 368648 | tf_op jit(solution)/shard_map/ppermute | solution.py:368
  43.0 4.1 %collective-permute-start.19 = (bf16[176,128]{1,0:T(8,128)(2,1)S(1)}, bf16[176,128]{1,0:T(8,128)(2,1)S(1)}, u32[]{:S(2)}, u32[]{:S(2)}) collective-permute-start(bf16[176,128]{1,0:T(8,128)(2,1)S(1)} %add_convert_fusion.4), channel_id=1, source_target_pairs={{0,2},{1,3},{2,0},{3,1},{4,6},{5,7},{6,4},{7,5},{8,10},{9,11},{10,... | collective-permute-start | bytes 135176 | tf_op jit(solution)/shard_map/ppermute | solution.py:368
  46.2 2.2 %collective-permute-start.24 = (bf16[480,128]{1,0:T(8,128)(2,1)S(1)}, bf16[480,128]{1,0:T(8,128)(2,1)S(1)}, u32[]{:S(2)}, u32[]{:S(2)}) collective-permute-start(bf16[480,128]{1,0:T(8,128)(2,1)S(1)} %add_convert_fusion.own_a_ref), channel_id=1, source_target_pairs={{0,1},{1,0},{2,3},{3,2},{4,5},{5,4},{6,7},{7,6},{8,9},{9,8},{10,11... | collective-permute-start | bytes 368648 | tf_op jit(solution)/shard_map/ppermute | solution.py:368
  47.1 1.3 %collective-permute-start.20 = (bf16[176,128]{1,0:T(8,128)(2,1)S(1)}, bf16[176,128]{1,0:T(8,128)(2,1)S(1)}, u32[]{:S(2)}, u32[]{:S(2)}) collective-permute-start(bf16[176,128]{1,0:T(8,128)(2,1)S(1)} %add_convert_fusion.3.own_b_ref), channel_id=1, source_target_pairs={{0,1},{1,0},{2,3},{3,2},{4,5},{5,4},{6,7},{7,6},{8,9},{9,8},{10,11... | collective-permute-start | bytes 135176 | tf_op jit(solution)/shard_map/ppermute | solution.py:368
  (12 other events, 59.6 us)

commit v7 on v6

--- a/solution.py
+++ b/solution.py
@@ -143,7 +143,7 @@
 
 def half_kernel(offsets, pos_ref, *refs):
     early_ref, late_ref, right_ref, left_ref, by_col_ref, inv_ref, p_ref, got_scr, p_scr = refs[-9:]
-    slots, (mask_a_ref, mask_b_ref, right_a_ref, right_b_ref) = refs[:-13], refs[-13:-9]
+    slots, (mask_a_ref, right_a_ref) = refs[:-11], refs[-11:-9]
     near, far = slots[: len(slots) // 2], slots[len(slots) // 2 :]
     rows, width = right_a_ref.shape
     homologs, cols = mask_a_ref.shape
@@ -168,10 +168,28 @@
     left = left_ref[:, pl.ds(pl.multiple_of(core * span, span), span)]
     masks = load(cols + 2 * wide, LANES).astype(BF16)
     group = LANES // homologs
-    sides = (mask_a_ref, right_a_ref, 0, p_ref), (mask_b_ref, right_b_ref, base, p_scr)
+    mask_b = got_scr[2 * chip + 1 - core, :, cols + 2 * wide : base].astype(F32).T[:homologs]
+    mask_b = jnp.concatenate(
+        [jnp.broadcast_to(mask_b[:, k : k + 1], (homologs, LANES)) for k in range(lines)], axis=1
+    ).astype(BF16)
+    spread_to = (
+        lax.broadcasted_iota(jnp.int32, (width, wide), 1) // homologs
+        == lax.broadcasted_iota(jnp.int32, (width, wide), 0)
+    ).astype(BF16)
+    own_tile = (
+        lax.broadcasted_iota(jnp.int32, (homologs, LANES), 1) % homologs
+        == lax.broadcasted_iota(jnp.int32, (homologs, LANES), 0)
+    ).astype(F32)
+    own = jnp.concatenate([own_tile] * (wide // LANES), axis=1)
+    right_b = got_scr[2 * chip + 1 - core, :, cols : cols + wide].astype(F32)
+    right_b = jnp.concatenate(
+        [jnp.broadcast_to(right_b[k : k + 1], (homologs, wide)) * own for k in range(lines)], axis=0
+    ).astype(BF16)
+    right_b = dot(right_b, spread_to, 1, 1).astype(BF16)
+    sides = (mask_a_ref[...], right_a_ref[...], 0, p_ref), (mask_b, right_b, base, p_scr)
     out = 0.0
-    for m, (mask_ref, side_ref, start, to_ref) in enumerate(sides):
-        inv = 1.0 / (dot(masks[:, :homologs], mask_ref[...]) + 1.0)
+    for m, (mask, side, start, to_ref) in enumerate(sides):
+        inv = 1.0 / (dot(masks[:, :homologs], mask) + 1.0)
         cot = (load(start, cols) * inv).astype(BF16)
         if m == 0:
             inv_ref[...] = inv
@@ -185,7 +203,7 @@
                     to_ref[to : to + homologs, c * pair_ch : (c + 1) * pair_ch] = part[
                         b * homologs : (b + 1) * homologs, k * pair_ch : (k + 1) * pair_ch
                     ]
-        out = out + dot(side_ref[...], to_ref[...], 0, 0)
+        out = out + dot(side, to_ref[...], 0, 0)
     out = out.astype(BF16)
     cut = early_ref.shape[0] // width
     for c in range(width // PAIR):
@@ -378,7 +396,6 @@
         near = lax.all_to_all(jnp.stack(slots)[order], "chip", 0, 0)[order]
         near = [near[m] for m in offsets]
     far = [swap(slot, 1) for slot in near]
-    other_right, other_maskb = swap(right, 1), swap(maskb, 1)
     (wleft,) = call(
         weight_kernel,
         [((width, width * pair_ch), BF16)],
@@ -401,8 +418,8 @@
         ],
         [((size, lines, span), BF16), ((rows, width * pair_ch // PAIR), BF16)],
         smem=1,
-        ins=4 + 2 * chips,
-    )(pos, *near, *far, maskb, other_maskb, right, other_right)
+        ins=2 + 2 * chips,
+    )(pos, *near, *far, maskb, right)
     parts, grads = call(
         grads_kernel,
         [

time: 49.4 us -> 49 us (level)
  starting transfers between devices: 25.6 us -> 24.7 us
    ppermute x25 -> x23, starting transfers between devices: 25.6 us -> 24.7 us  [swap(): lax.ppermute(x, ('chip', 'core'), [(i, i ^ step) for i in range(size)])]
    ppermute x25 -> x23, waiting for transfers between devices: 11.1 us -> 11.5 us  [swap(): lax.ppermute(x, ('chip', 'core'), [(i, i ^ step) for i in range(size)])]
  transfers between devices with their start and end apart: 25 -> 23, of which waited for: 12 -> 11; matrix products, arithmetic and copies ran while one was open for 0% -> 0% of each run, Pallas kernels for 11% -> 11%
where the time goes in v7:
time: 49 us; the launch traced here: 48.8 us
  starting transfers between devices  24.7 us (50%)
  waiting for transfers between devices  11.5 us (23%)
  Pallas kernels  10.9 us (22%)
  between operations  0.8 us (2%)
  local copies, waits for them, and re-layouts  0.7 us (1%)
    ppermute x23, starting transfers between devices, swap(): lax.ppermute(x, ('chip', 'core'), [(i, i ^ step) for i in range(size)])  24.7 us
    ppermute x23, waiting for transfers between devices, swap(): lax.ppermute(x, ('chip', 'core'), [(i, i ^ step) for i in range(size)])  11.5 us
    pallas_call x1, Pallas kernels, body(): call(pre_kernel, [((rows, width), BF16), ((rows, width), BF16), ((homolog...  3.05 us
    pallas_call x1, Pallas kernels, body(): call(grads_kernel, [((half - early + 4 * width + 16, pair_ch), BF16), ((2...  2.46 us
    pallas_call x1, Pallas kernels, make_update(): call(update_kernel, [((lines, total, pair_ch), BF16)], [((wide, cols), BF...  1.68 us
    pallas_call x1, Pallas kernels, body(): call(functools.partial(half_kernel, offsets), [((early, pair_ch), BF16),...  1.51 us
    pallas_call x1, Pallas kernels, make_d_msa(): call(msa_kernel, [((homologs, lines, depth), BF16)], [((depth // LANES, r...  1.01 us
  transfers between devices with their start and end apart: 23, of which 11 were waited for; matrix products, arithmetic and copies ran while one was open for 0% of the time, Pallas kernels for 11%

profile of v7, /device:TPU:0, one launch (start us, length us, event | category | flops | bytes accessed | tf_op | source)
XLA Modules:
  0.0 48.8 jit_solution(1318049684117305369)
XLA Ops:
  0.6 3.0 %shard_map.118 = (bf16[256,32]{1,0:T(8,128)(2,1)}, bf16[256,32]{1,0:T(8,128)(2,1)}, bf16[32,1024]{1,0:T(8,128)(2,1)}, bf16[256,256]{1,0:T(8,128)(2,1)}, bf16[8,4...) custom-call(s32[1]{0:T(128)} %bitcast.pos_ref, ...), custom_call_target="tpu_custom_call" | custom-call | tf_op jit(solution)/shard_map/pallas_call | solution.py:361
  3.7 5.1 %collective-permute-start = (bf16[8,4224]{1,0:T(8,128)(2,1)}, bf16[8,4224]{1,0:T(8,128)(2,1)S(1)}, u32[]{:S(2)}, u32[]{:S(2)}) collective-permute-start(bf16[8,4224]{1,0:T(8,128)(2,1)} %get-tuple-element.44), channel_id=1, source_target_pairs={{0,12},{1,13},{2,14},{3,15},{4,8},{5,9},{6,10},{7,11},{8,4},{9,5},... | collective-permute-start | bytes 202760 | tf_op jit(solution)/shard_map/ppermute | solution.py:386
  8.8 1.1 %collective-permute-start.1 = (bf16[8,4224]{1,0:T(8,128)(2,1)}, bf16[8,4224]{1,0:T(8,128)(2,1)S(1)}, u32[]{:S(2)}, u32[]{:S(2)}) collective-permute-start(bf16[8,4224]{1,0:T(8,128)(2,1)} %get-tuple-element.45), channel_id=1, source_target_pairs={{0,14},{1,15},{2,12},{3,13},{4,10},{5,11},{6,8},{7,9},{8,6},{9,7},... | collective-permute-start | bytes 202760 | tf_op jit(solution)/shard_map/ppermute | solution.py:386
  10.0 0.8 %collective-permute-start.2 = (bf16[8,4224]{1,0:T(8,128)(2,1)}, bf16[8,4224]{1,0:T(8,128)(2,1)S(1)}, u32[]{:S(2)}, u32[]{:S(2)}) collective-permute-start(bf16[8,4224]{1,0:T(8,128)(2,1)} %get-tuple-element.46), channel_id=1, source_target_pairs={{0,8},{1,9},{2,10},{3,11},{4,12},{5,13},{6,14},{7,15},{8,0},{9,1},... | collective-permute-start | bytes 202760 | tf_op jit(solution)/shard_map/ppermute | solution.py:386
  10.8 2.0 %collective-permute-start.3 = (bf16[8,4224]{1,0:T(8,128)(2,1)}, bf16[8,4224]{1,0:T(8,128)(2,1)S(1)}, u32[]{:S(2)}, u32[]{:S(2)}) collective-permute-start(bf16[8,4224]{1,0:T(8,128)(2,1)} %get-tuple-element.47), channel_id=1, source_target_pairs={{0,10},{1,11},{2,8},{3,9},{4,14},{5,15},{6,12},{7,13},{8,2},{9,3},... | collective-permute-start | bytes 202760 | tf_op jit(solution)/shard_map/ppermute | solution.py:386
  12.7 1.4 %collective-permute-start.4 = (bf16[8,4224]{1,0:T(8,128)(2,1)}, bf16[8,4224]{1,0:T(8,128)(2,1)S(1)}, u32[]{:S(2)}, u32[]{:S(2)}) collective-permute-start(bf16[8,4224]{1,0:T(8,128)(2,1)} %get-tuple-element.48), channel_id=1, source_target_pairs={{0,4},{1,5},{2,6},{3,7},{4,0},{5,1},{6,2},{7,3},{8,12},{9,13},{10,... | collective-permute-start | bytes 202760 | tf_op jit(solution)/shard_map/ppermute | solution.py:386
  14.1 1.7 %collective-permute-start.5 = (bf16[8,4224]{1,0:T(8,128)(2,1)}, bf16[8,4224]{1,0:T(8,128)(2,1)S(1)}, u32[]{:S(2)}, u32[]{:S(2)}) collective-permute-start(bf16[8,4224]{1,0:T(8,128)(2,1)} %get-tuple-element.49), channel_id=1, source_target_pairs={{0,6},{1,7},{2,4},{3,5},{4,2},{5,3},{6,0},{7,1},{8,14},{9,15},{10,... | collective-permute-start | bytes 202760 | tf_op jit(solution)/shard_map/ppermute | solution.py:386
  16.2 1.6 %collective-permute-start.6 = (bf16[8,4224]{1,0:T(8,128)(2,1)}, bf16[8,4224]{1,0:T(8,128)(2,1)S(1)}, u32[]{:S(2)}, u32[]{:S(2)}) collective-permute-start(bf16[8,4224]{1,0:T(8,128)(2,1)} %get-tuple-element.51), channel_id=1, source_target_pairs={{0,2},{1,3},{2,0},{3,1},{4,6},{5,7},{6,4},{7,5},{8,10},{9,11},{10,... | collective-permute-start | bytes 202760 | tf_op jit(solution)/shard_map/ppermute | solution.py:386
  17.8 2.1 %collective-permute-done.2.refs_2_ = bf16[8,4224]{1,0:T(8,128)(2,1)S(1)} collective-permute-done((bf16[8,4224]{1,0:T(8,128)(2,1)}, bf16[8,4224]{1,0:T(8,128)(2,1)S(1)}, u32[]{:S(2)}, u32[]{:S(2)}) %collective-permute-start.2) | collective-permute-done | bytes 67616 | tf_op jit(solution)/shard_map/ppermute | solution.py:386
  19.9 1.8 %collective-permute-done.3.refs_3_ = bf16[8,4224]{1,0:T(8,128)(2,1)S(1)} collective-permute-done((bf16[8,4224]{1,0:T(8,128)(2,1)}, bf16[8,4224]{1,0:T(8,128)(2,1)S(1)}, u32[]{:S(2)}, u32[]{:S(2)}) %collective-permute-start.3) | collective-permute-done | bytes 67616 | tf_op jit(solution)/shard_map/ppermute | solution.py:386
  24.5 1.5 %shard_map.120 = (bf16[480,128]{1,0:T(8,128)(2,1)S(1)}, bf16[32,128]{1,0:T(8,128)(2,1)S(1)}, bf16[128,1024]{1,0:T(8,128)(2,1)S(1)}, bf16[128,1024]{1,0:T(8,128)(...) custom-call(s32[1]{0:T(128)} %bitcast.pos_ref, ...), custom_call_target="tpu_custom_call" | custom-call | tf_op jit(solution)/shard_map/pallas_call | solution.py:408
  26.8 2.5 %shard_map.121 = (bf16[176,128]{1,0:T(8,128)(2,1)S(1)}, bf16[2,256,32]{2,1,0:T(8,128)(2,1)S(1)}) custom-call(s32[1]{0:T(128)} %bitcast.pos_ref, bf16[256,2048]{1,0:T(8,128)(2,1)S(1)} %get-tuple-element.62.p_ref, bf16[128,1024]{1,0:T(8,128)(2,1)S(1)} %get-tuple-element.63.right_ref, bf16[128,1024]{1,0:T(8,128)(2,1)S(1)} %get-tuple-element.64.left_ref, ...), custom_call_target="tpu_custom_call" | custom-call | tf_op jit(solution)/shard_map/pallas_call | solution.py:423
  29.2 0.8 %collective-permute-start.15 = (bf16[176,128]{1,0:T(8,128)(2,1)S(1)}, bf16[176,128]{1,0:T(8,128)(2,1)S(1)}, u32[]{:S(2)}, u32[]{:S(2)}) collective-permute-start(bf16[176,128]{1,0:T(8,128)(2,1)S(1)} %get-tuple-element.70), channel_id=1, source_target_pairs={{0,4},{1,5},{2,6},{3,7},{4,0},{5,1},{6,2},{7,3},{8,12},{9,13},{10,... | collective-permute-start | bytes 135176 | tf_op jit(solution)/shard_map/ppermute | solution.py:386
  30.1 1.0 %shard_map.122 = bf16[32,8,256]{2,1,0:T(8,128)(2,1)} custom-call(bf16[32,8,256]{2,1,0:T(8,128)(2,1)S(1)} %copy-done.2, bf16[2,256,32]{2,1,0:T(8,128)(2,1)S(1)} %get-tuple-element.71.grads_ref, bf16[32,256]{1,0:T(8,128)(2,1)S(1)} %bitcast.9, bf16[32,256]{1,0:T(8,128)(2,1)S(1)} %bitcast.11), custom_call_target="tpu_custom_call" | custom-call | flops 8388608 | tf_op jit(solution)/shard_map/pallas_call | solution.py:445
  31.1 2.2 %collective-permute-done.15 = bf16[176,128]{1,0:T(8,128)(2,1)S(1)} collective-permute-done((bf16[176,128]{1,0:T(8,128)(2,1)S(1)}, bf16[176,128]{1,0:T(8,128)(2,1)S(1)}, u32[]{:S(2)}, u32[]{:S(2)}) %collective-permute-start.15) | collective-permute-done | bytes 45088 | tf_op jit(solution)/shard_map/ppermute | solution.py:386
  33.4 0.9 %collective-permute-start.20 = (bf16[480,128]{1,0:T(8,128)(2,1)S(1)}, bf16[480,128]{1,0:T(8,128)(2,1)S(1)}, u32[]{:S(2)}, u32[]{:S(2)}) collective-permute-start(bf16[480,128]{1,0:T(8,128)(2,1)S(1)} %add_convert_fusion.2), channel_id=1, source_target_pairs={{0,4},{1,5},{2,6},{3,7},{4,0},{5,1},{6,2},{7,3},{8,12},{9,13},{10,... | collective-permute-start | bytes 368648 | tf_op jit(solution)/shard_map/ppermute | solution.py:386
  34.2 3.1 %collective-permute-start.16 = (bf16[176,128]{1,0:T(8,128)(2,1)S(1)}, bf16[176,128]{1,0:T(8,128)(2,1)S(1)}, u32[]{:S(2)}, u32[]{:S(2)}) collective-permute-start(bf16[176,128]{1,0:T(8,128)(2,1)S(1)} %add_convert_fusion.5), channel_id=1, source_target_pairs={{0,8},{1,9},{2,10},{3,11},{4,12},{5,13},{6,14},{7,15},{8,0},{9,1},... | collective-permute-start | bytes 135176 | tf_op jit(solution)/shard_map/ppermute | solution.py:386
  38.0 1.7 %shard_map.123 = bf16[8,128,128]{2,1,0:T(8,128)(2,1)} custom-call(bf16[128,1024]{1,0:T(8,128)(2,1)S(1)} %get-tuple-element.63.right_ref, f32[128,1024]{1,0:T(8,128)S(1)} %get-tuple-element.66.inv_ref, bf16[256,32]{1,0:T(8,128)(2,1)S(1)} %copy-done.6, bf16[32,4096]{1,0:T(8,128)(2,1)S(1)} %shard_map.119.wleft_ref, f32[1,128]{1,0:T(1,128)S(1)} %bitcast.12), custom_call_target="tpu_custom_call" | custom-call | flops 268435456 | tf_op jit(solution)/shard_map/pallas_call | solution.py:435
  39.8 2.8 %collective-permute-start.21 = (bf16[480,128]{1,0:T(8,128)(2,1)S(1)}, bf16[480,128]{1,0:T(8,128)(2,1)S(1)}, u32[]{:S(2)}, u32[]{:S(2)}) collective-permute-start(bf16[480,128]{1,0:T(8,128)(2,1)S(1)} %add_convert_fusion.1), channel_id=1, source_target_pairs={{0,8},{1,9},{2,10},{3,11},{4,12},{5,13},{6,14},{7,15},{8,0},{9,1},... | collective-permute-start | bytes 368648 | tf_op jit(solution)/shard_map/ppermute | solution.py:386
  42.5 1.0 %collective-permute-start.17 = (bf16[176,128]{1,0:T(8,128)(2,1)S(1)}, bf16[176,128]{1,0:T(8,128)(2,1)S(1)}, u32[]{:S(2)}, u32[]{:S(2)}) collective-permute-start(bf16[176,128]{1,0:T(8,128)(2,1)S(1)} %add_convert_fusion.4), channel_id=1, source_target_pairs={{0,2},{1,3},{2,0},{3,1},{4,6},{5,7},{6,4},{7,5},{8,10},{9,11},{10,... | collective-permute-start | bytes 135176 | tf_op jit(solution)/shard_map/ppermute | solution.py:386
  43.5 2.1 %collective-permute-done.21 = bf16[480,128]{1,0:T(8,128)(2,1)S(1)} collective-permute-done((bf16[480,128]{1,0:T(8,128)(2,1)S(1)}, bf16[480,128]{1,0:T(8,128)(2,1)S(1)}, u32[]{:S(2)}, u32[]{:S(2)}) %collective-permute-start.21) | collective-permute-done | bytes 122912 | tf_op jit(solution)/shard_map/ppermute | solution.py:386
  45.7 0.9 %collective-permute-done.17 = bf16[176,128]{1,0:T(8,128)(2,1)S(1)} collective-permute-done((bf16[176,128]{1,0:T(8,128)(2,1)S(1)}, bf16[176,128]{1,0:T(8,128)(2,1)S(1)}, u32[]{:S(2)}, u32[]{:S(2)}) %collective-permute-start.17) | collective-permute-done | bytes 45088 | tf_op jit(solution)/shard_map/ppermute | solution.py:386
  46.8 1.2 %collective-permute-done.18.other_b_ref = bf16[176,128]{1,0:T(8,128)(2,1)S(1)} collective-permute-done((bf16[176,128]{1,0:T(8,128)(2,1)S(1)}, bf16[176,128]{1,0:T(8,128)(2,1)S(1)}, u32[]{:S(2)}, u32[]{:S(2)}) %collective-permute-start.18) | collective-permute-done | bytes 45088 | tf_op jit(solution)/shard_map/ppermute | solution.py:386
  48.0 0.8 %shard_map.124 = (f32[1024,128]{1,0:T(8,128)}, f32[32,256]{1,0:T(8,128)}, f32[32,256]{1,0:T(8,128)}, f32[1,128]{1,0:T(1,128)}) custom-call(s32[1]{0:T(128)} %bitcast.pos_ref, bf16[176,128]{1,0:T(8,128)(2,1)S(1)} %add_convert_fusion.3.own_b_ref, bf16[176,128]{1,0:T(8,128)(2,1)S(1)} %collective-permute-done.18.other_b_ref, ...), custom_call_target="tpu_custom_call" | custom-call | tf_op jit(solution)/shard_map/pallas_call | solution.py:466
  (57 shorter events, 4.9 us)
Async XLA Ops:
  0.6 22.8 %copy-start.1 = (bf16[1024,128]{1,0:T(8,128)(2,1)S(1)}, bf16[1024,128]{1,0:T(8,128)(2,1)}, u32[]{:S(2)}) copy-start(bf16[1024,128]{1,0:T(8,128)(2,1)} %wout_ref.3) | copy-start | bytes 786436
  3.7 10.4 %collective-permute-start = (bf16[8,4224]{1,0:T(8,128)(2,1)}, bf16[8,4224]{1,0:T(8,128)(2,1)S(1)}, u32[]{:S(2)}, u32[]{:S(2)}) collective-permute-start(bf16[8,4224]{1,0:T(8,128)(2,1)} %get-tuple-element.44), channel_id=1, source_target_pairs={{0,12},{1,13},{2,14},{3,15},{4,8},{5,9},{6,10},{7,11},{8,4},{9,5},... | collective-permute-start | bytes 202760 | tf_op jit(solution)/shard_map/ppermute | solution.py:386
  8.8 7.4 %collective-permute-start.1 = (bf16[8,4224]{1,0:T(8,128)(2,1)}, bf16[8,4224]{1,0:T(8,128)(2,1)S(1)}, u32[]{:S(2)}, u32[]{:S(2)}) collective-permute-start(bf16[8,4224]{1,0:T(8,128)(2,1)} %get-tuple-element.45), channel_id=1, source_target_pairs={{0,14},{1,15},{2,12},{3,13},{4,10},{5,11},{6,8},{7,9},{8,6},{9,7},... | collective-permute-start | bytes 202760 | tf_op jit(solution)/shard_map/ppermute | solution.py:386
  10.0 9.9 %collective-permute-start.2 = (bf16[8,4224]{1,0:T(8,128)(2,1)}, bf16[8,4224]{1,0:T(8,128)(2,1)S(1)}, u32[]{:S(2)}, u32[]{:S(2)}) collective-permute-start(bf16[8,4224]{1,0:T(8,128)(2,1)} %get-tuple-element.46), channel_id=1, source_target_pairs={{0,8},{1,9},{2,10},{3,11},{4,12},{5,13},{6,14},{7,15},{8,0},{9,1},... | collective-permute-start | bytes 202760 | tf_op jit(solution)/shard_map/ppermute | solution.py:386
  10.8 10.9 %collective-permute-start.3 = (bf16[8,4224]{1,0:T(8,128)(2,1)}, bf16[8,4224]{1,0:T(8,128)(2,1)S(1)}, u32[]{:S(2)}, u32[]{:S(2)}) collective-permute-start(bf16[8,4224]{1,0:T(8,128)(2,1)} %get-tuple-element.47), channel_id=1, source_target_pairs={{0,10},{1,11},{2,8},{3,9},{4,14},{5,15},{6,12},{7,13},{8,2},{9,3},... | collective-permute-start | bytes 202760 | tf_op jit(solution)/shard_map/ppermute | solution.py:386
  12.7 8.9 %collective-permute-start.4 = (bf16[8,4224]{1,0:T(8,128)(2,1)}, bf16[8,4224]{1,0:T(8,128)(2,1)S(1)}, u32[]{:S(2)}, u32[]{:S(2)}) collective-permute-start(bf16[8,4224]{1,0:T(8,128)(2,1)} %get-tuple-element.48), channel_id=1, source_target_pairs={{0,4},{1,5},{2,6},{3,7},{4,0},{5,1},{6,2},{7,3},{8,12},{9,13},{10,... | collective-permute-start | bytes 202760 | tf_op jit(solution)/shard_map/ppermute | solution.py:386
  14.1 8.0 %collective-permute-start.5 = (bf16[8,4224]{1,0:T(8,128)(2,1)}, bf16[8,4224]{1,0:T(8,128)(2,1)S(1)}, u32[]{:S(2)}, u32[]{:S(2)}) collective-permute-start(bf16[8,4224]{1,0:T(8,128)(2,1)} %get-tuple-element.49), channel_id=1, source_target_pairs={{0,6},{1,7},{2,4},{3,5},{4,2},{5,3},{6,0},{7,1},{8,14},{9,15},{10,... | collective-permute-start | bytes 202760 | tf_op jit(solution)/shard_map/ppermute | solution.py:386
  16.2 6.0 %collective-permute-start.6 = (bf16[8,4224]{1,0:T(8,128)(2,1)}, bf16[8,4224]{1,0:T(8,128)(2,1)S(1)}, u32[]{:S(2)}, u32[]{:S(2)}) collective-permute-start(bf16[8,4224]{1,0:T(8,128)(2,1)} %get-tuple-element.51), channel_id=1, source_target_pairs={{0,2},{1,3},{2,0},{3,1},{4,6},{5,7},{6,4},{7,5},{8,10},{9,11},{10,... | collective-permute-start | bytes 202760 | tf_op jit(solution)/shard_map/ppermute | solution.py:386
  19.9 2.8 %collective-permute-start.13 = (bf16[8,4224]{1,0:T(8,128)(2,1)}, bf16[8,4224]{1,0:T(8,128)(2,1)S(1)}, u32[]{:S(2)}, u32[]{:S(2)}) collective-permute-start(bf16[8,4224]{1,0:T(8,128)(2,1)} %get-tuple-element.58.refs_6_), channel_id=1, source_target_pairs={{0,1},{1,0},{2,3},{3,2},{4,5},{5,4},{6,7},{7,6},{8,9},{9,8},{10,11... | collective-permute-start | bytes 202760 | tf_op jit(solution)/shard_map/ppermute | solution.py:386
  21.7 1.3 %collective-permute-start.7 = (bf16[8,4224]{1,0:T(8,128)(2,1)S(1)}, bf16[8,4224]{1,0:T(8,128)(2,1)S(1)}, u32[]{:S(2)}, u32[]{:S(2)}) collective-permute-start(bf16[8,4224]{1,0:T(8,128)(2,1)S(1)} %collective-permute-done.refs_0_), channel_id=1, source_target_pairs={{0,1},{1,0},{2,3},{3,2},{4,5},{5,4},{6,7},{7,6},{8,9},{9,8},{10,11... | collective-permute-start | bytes 202760 | tf_op jit(solution)/shard_map/ppermute | solution.py:386
  21.7 1.5 %collective-permute-start.8 = (bf16[8,4224]{1,0:T(8,128)(2,1)S(1)}, bf16[8,4224]{1,0:T(8,128)(2,1)S(1)}, u32[]{:S(2)}, u32[]{:S(2)}) collective-permute-start(bf16[8,4224]{1,0:T(8,128)(2,1)S(1)} %collective-permute-done.1.refs_1_), channel_id=1, source_target_pairs={{0,1},{1,0},{2,3},{3,2},{4,5},{5,4},{6,7},{7,6},{8,9},{9,8},{10,11... | collective-permute-start | bytes 202760 | tf_op jit(solution)/shard_map/ppermute | solution.py:386
  22.2 1.6 %collective-permute-start.9 = (bf16[8,4224]{1,0:T(8,128)(2,1)S(1)}, bf16[8,4224]{1,0:T(8,128)(2,1)S(1)}, u32[]{:S(2)}, u32[]{:S(2)}) collective-permute-start(bf16[8,4224]{1,0:T(8,128)(2,1)S(1)} %collective-permute-done.2.refs_2_), channel_id=1, source_target_pairs={{0,1},{1,0},{2,3},{3,2},{4,5},{5,4},{6,7},{7,6},{8,9},{9,8},{10,11... | collective-permute-start | bytes 202760 | tf_op jit(solution)/shard_map/ppermute | solution.py:386
  22.3 1.5 %collective-permute-start.10 = (bf16[8,4224]{1,0:T(8,128)(2,1)S(1)}, bf16[8,4224]{1,0:T(8,128)(2,1)S(1)}, u32[]{:S(2)}, u32[]{:S(2)}) collective-permute-start(bf16[8,4224]{1,0:T(8,128)(2,1)S(1)} %collective-permute-done.3.refs_3_), channel_id=1, source_target_pairs={{0,1},{1,0},{2,3},{3,2},{4,5},{5,4},{6,7},{7,6},{8,9},{9,8},{10,11... | collective-permute-start | bytes 202760 | tf_op jit(solution)/shard_map/ppermute | solution.py:386
  22.7 1.3 %collective-permute-start.11 = (bf16[8,4224]{1,0:T(8,128)(2,1)S(1)}, bf16[8,4224]{1,0:T(8,128)(2,1)S(1)}, u32[]{:S(2)}, u32[]{:S(2)}) collective-permute-start(bf16[8,4224]{1,0:T(8,128)(2,1)S(1)} %collective-permute-done.4.refs_4_), channel_id=1, source_target_pairs={{0,1},{1,0},{2,3},{3,2},{4,5},{5,4},{6,7},{7,6},{8,9},{9,8},{10,11... | collective-permute-start | bytes 202760 | tf_op jit(solution)/shard_map/ppermute | solution.py:386
  22.9 1.3 %collective-permute-start.12 = (bf16[8,4224]{1,0:T(8,128)(2,1)S(1)}, bf16[8,4224]{1,0:T(8,128)(2,1)S(1)}, u32[]{:S(2)}, u32[]{:S(2)}) collective-permute-start(bf16[8,4224]{1,0:T(8,128)(2,1)S(1)} %collective-permute-done.5.refs_5_), channel_id=1, source_target_pairs={{0,1},{1,0},{2,3},{3,2},{4,5},{5,4},{6,7},{7,6},{8,9},{9,8},{10,11... | collective-permute-start | bytes 202760 | tf_op jit(solution)/shard_map/ppermute | solution.py:386
  23.2 1.3 %collective-permute-start.14 = (bf16[8,4224]{1,0:T(8,128)(2,1)S(1)}, bf16[8,4224]{1,0:T(8,128)(2,1)S(1)}, u32[]{:S(2)}, u32[]{:S(2)}) collective-permute-start(bf16[8,4224]{1,0:T(8,128)(2,1)S(1)} %collective-permute-done.6.refs_7_), channel_id=1, source_target_pairs={{0,1},{1,0},{2,3},{3,2},{4,5},{5,4},{6,7},{7,6},{8,9},{9,8},{10,11... | collective-permute-start | bytes 202760 | tf_op jit(solution)/shard_map/ppermute | solution.py:386
  26.0 7.3 %collective-permute-start.19 = (bf16[480,128]{1,0:T(8,128)(2,1)S(1)}, bf16[480,128]{1,0:T(8,128)(2,1)S(1)}, u32[]{:S(2)}, u32[]{:S(2)}) collective-permute-start(bf16[480,128]{1,0:T(8,128)(2,1)S(1)} %get-tuple-element.77), channel_id=1, source_target_pairs={{0,2},{1,3},{2,0},{3,1},{4,6},{5,7},{6,4},{7,5},{8,10},{9,11},{10,... | collective-permute-start | bytes 368648 | tf_op jit(solution)/shard_map/ppermute | solution.py:386
  29.2 4.1 %collective-permute-start.15 = (bf16[176,128]{1,0:T(8,128)(2,1)S(1)}, bf16[176,128]{1,0:T(8,128)(2,1)S(1)}, u32[]{:S(2)}, u32[]{:S(2)}) collective-permute-start(bf16[176,128]{1,0:T(8,128)(2,1)S(1)} %get-tuple-element.70), channel_id=1, source_target_pairs={{0,4},{1,5},{2,6},{3,7},{4,0},{5,1},{6,2},{7,3},{8,12},{9,13},{10,... | collective-permute-start | bytes 135176 | tf_op jit(solution)/shard_map/ppermute | solution.py:386
  33.4 6.4 %collective-permute-start.20 = (bf16[480,128]{1,0:T(8,128)(2,1)S(1)}, bf16[480,128]{1,0:T(8,128)(2,1)S(1)}, u32[]{:S(2)}, u32[]{:S(2)}) collective-permute-start(bf16[480,128]{1,0:T(8,128)(2,1)S(1)} %add_convert_fusion.2), channel_id=1, source_target_pairs={{0,4},{1,5},{2,6},{3,7},{4,0},{5,1},{6,2},{7,3},{8,12},{9,13},{10,... | collective-permute-start | bytes 368648 | tf_op jit(solution)/shard_map/ppermute | solution.py:386
  34.2 5.5 %collective-permute-start.16 = (bf16[176,128]{1,0:T(8,128)(2,1)S(1)}, bf16[176,128]{1,0:T(8,128)(2,1)S(1)}, u32[]{:S(2)}, u32[]{:S(2)}) collective-permute-start(bf16[176,128]{1,0:T(8,128)(2,1)S(1)} %add_convert_fusion.5), channel_id=1, source_target_pairs={{0,8},{1,9},{2,10},{3,11},{4,12},{5,13},{6,14},{7,15},{8,0},{9,1},... | collective-permute-start | bytes 135176 | tf_op jit(solution)/shard_map/ppermute | solution.py:386
  39.8 5.8 %collective-permute-start.21 = (bf16[480,128]{1,0:T(8,128)(2,1)S(1)}, bf16[480,128]{1,0:T(8,128)(2,1)S(1)}, u32[]{:S(2)}, u32[]{:S(2)}) collective-permute-start(bf16[480,128]{1,0:T(8,128)(2,1)S(1)} %add_convert_fusion.1), channel_id=1, source_target_pairs={{0,8},{1,9},{2,10},{3,11},{4,12},{5,13},{6,14},{7,15},{8,0},{9,1},... | collective-permute-start | bytes 368648 | tf_op jit(solution)/shard_map/ppermute | solution.py:386
  42.5 4.1 %collective-permute-start.17 = (bf16[176,128]{1,0:T(8,128)(2,1)S(1)}, bf16[176,128]{1,0:T(8,128)(2,1)S(1)}, u32[]{:S(2)}, u32[]{:S(2)}) collective-permute-start(bf16[176,128]{1,0:T(8,128)(2,1)S(1)} %add_convert_fusion.4), channel_id=1, source_target_pairs={{0,2},{1,3},{2,0},{3,1},{4,6},{5,7},{6,4},{7,5},{8,10},{9,11},{10,... | collective-permute-start | bytes 135176 | tf_op jit(solution)/shard_map/ppermute | solution.py:386
  45.6 2.3 %collective-permute-start.22 = (bf16[480,128]{1,0:T(8,128)(2,1)S(1)}, bf16[480,128]{1,0:T(8,128)(2,1)S(1)}, u32[]{:S(2)}, u32[]{:S(2)}) collective-permute-start(bf16[480,128]{1,0:T(8,128)(2,1)S(1)} %add_convert_fusion.own_a_ref), channel_id=1, source_target_pairs={{0,1},{1,0},{2,3},{3,2},{4,5},{5,4},{6,7},{7,6},{8,9},{9,8},{10,11... | collective-permute-start | bytes 368648 | tf_op jit(solution)/shard_map/ppermute | solution.py:386
  46.7 1.3 %collective-permute-start.18 = (bf16[176,128]{1,0:T(8,128)(2,1)S(1)}, bf16[176,128]{1,0:T(8,128)(2,1)S(1)}, u32[]{:S(2)}, u32[]{:S(2)}) collective-permute-start(bf16[176,128]{1,0:T(8,128)(2,1)S(1)} %add_convert_fusion.3.own_b_ref), channel_id=1, source_target_pairs={{0,1},{1,0},{2,3},{3,2},{4,5},{5,4},{6,7},{7,6},{8,9},{9,8},{10,11... | collective-permute-start | bytes 135176 | tf_op jit(solution)/shard_map/ppermute | solution.py:386
  (10 other events, 33.0 us)

commit v8 on v7

--- a/solution.py
+++ b/solution.py
@@ -65,7 +65,7 @@
     copies[0].wait()
     normed, _ = normalize(msa_ref)
     for h in range(depth // LANES):
-        norm_scr[h] = normed[:, h * LANES : (h + 1) * LANES]
+        norm_scr[h, :rows] = normed[:, h * LANES : (h + 1) * LANES]
     low = jnp.concatenate(
         [
             jnp.concatenate(
@@ -118,7 +118,7 @@
     base = same.shape[1]
     cols = lines * pair_ch
     copies[4].wait()
-    cot_scr[...] = cot_ref[...].astype(F32).reshape(lines * total, pair_ch)
+    cot_scr[: lines * total] = cot_ref[...].astype(F32).reshape(lines * total, pair_ch)
     for m, slot in enumerate(slots):
         slot_scr[m, :, cols : cols + base] = same
         for begin, to in ((0, core), (cols + base, 1 - core)):
@@ -134,7 +134,7 @@
 
 def weight_kernel(wout_ref, wleft_ref, w_scr):
     width, pair_ch = wleft_ref.shape[0], wout_ref.shape[1]
-    w_scr[...] = wout_ref[...].astype(F32)
+    w_scr[: wout_ref.shape[0]] = wout_ref[...].astype(F32)
     for e in range(width):
         wleft_ref[:, e * pair_ch : (e + 1) * pair_ch] = w_scr[
             pl.ds(e, width, stride=width), :
@@ -299,7 +299,9 @@
             scr[h, pl.ds(k, homologs, stride=lines), :] = derivative[
                 k * homologs : (k + 1) * homologs, h * LANES : (h + 1) * LANES
             ]
-    derivative = jnp.concatenate([scr[h] for h in range(depth // LANES)], axis=1)
+    derivative = jnp.concatenate(
+        [scr[h, : homologs * lines] for h in range(depth // LANES)], axis=1
+    )
     normed, spread = normalize(msa_ref)
     one = jnp.mean(derivative, axis=-1, keepdims=True)
     two = jnp.mean(derivative * normed, axis=-1, keepdims=True)
@@ -369,8 +371,8 @@
         + [((lines, span), BF16)] * chips,
         [(x.shape, x.dtype) for x in given]
         + [
-            ((depth // LANES, rows, LANES), F32),
-            ((lines * total, pair_ch), F32),
+            ((depth // LANES, rows + lines, LANES), F32),
+            (((lines + 1) * total, pair_ch), F32),
             ((rows, width), BF16),
             ((rows, width), BF16),
             ((homologs, lines * LANES), BF16),
@@ -399,7 +401,7 @@
     (wleft,) = call(
         weight_kernel,
         [((width, width * pair_ch), BF16)],
-        [((width * width, pair_ch), F32)],
+        [((width * width + width, pair_ch), F32)],
         ins=1,
     )(wout)
     near, wleft = lax.optimization_barrier((near, wleft))
@@ -445,7 +447,7 @@
         (out,) = call(
             msa_kernel,
             [((homologs, lines, depth), BF16)],
-            [((depth // LANES, rows, LANES), F32)],
+            [((depth // LANES, rows + lines, LANES), F32)],
             ins=4,
             flops=2 * rows * depth * 2 * width,
         )(msa, grads, wf, wl)

time: 49 us -> 48.9 us (level)
  transfers between devices with their start and end apart: 23 -> 23, of which waited for: 11 -> 12; matrix products, arithmetic and copies ran while one was open for 0% -> 0% of each run, Pallas kernels for 11% -> 11%
where the time goes in v8:
time: 48.9 us; the launch traced here: 48.8 us
  starting transfers between devices  24.7 us (51%)
  waiting for transfers between devices  11.5 us (24%)
  Pallas kernels  10.9 us (22%)
  between operations  0.8 us (2%)
  local copies, waits for them, and re-layouts  0.7 us (1%)
    ppermute x23, starting transfers between devices, swap(): lax.ppermute(x, ('chip', 'core'), [(i, i ^ step) for i in range(size)])  24.7 us
    ppermute x23, waiting for transfers between devices, swap(): lax.ppermute(x, ('chip', 'core'), [(i, i ^ step) for i in range(size)])  11.5 us
    pallas_call x1, Pallas kernels, body(): call(pre_kernel, [((rows, width), BF16), ((rows, width), BF16), ((homolog...  3.05 us
    pallas_call x1, Pallas kernels, body(): call(grads_kernel, [((half - early + 4 * width + 16, pair_ch), BF16), ((2...  2.45 us
    pallas_call x1, Pallas kernels, make_update(): call(update_kernel, [((lines, total, pair_ch), BF16)], [((wide, cols), BF...  1.68 us
    pallas_call x1, Pallas kernels, body(): call(functools.partial(half_kernel, offsets), [((early, pair_ch), BF16),...  1.51 us
    pallas_call x1, Pallas kernels, make_d_msa(): call(msa_kernel, [((homologs, lines, depth), BF16)], [((depth // LANES, r...  1.01 us
  transfers between devices with their start and end apart: 23, of which 12 were waited for; matrix products, arithmetic and copies ran while one was open for 0% of the time, Pallas kernels for 11%

profile of v8, /device:TPU:0, one launch (start us, length us, event | category | flops | bytes accessed | tf_op | source)
XLA Modules:
  0.0 48.8 jit_solution(5605810406463980370)
XLA Ops:
  0.6 3.1 %shard_map.118 = (bf16[256,32]{1,0:T(8,128)(2,1)}, bf16[256,32]{1,0:T(8,128)(2,1)}, bf16[32,1024]{1,0:T(8,128)(2,1)}, bf16[256,256]{1,0:T(8,128)(2,1)}, bf16[8,4...) custom-call(s32[1]{0:T(128)} %bitcast.pos_ref, ...), custom_call_target="tpu_custom_call" | custom-call | tf_op jit(solution)/shard_map/pallas_call | solution.py:363
  3.7 5.1 %collective-permute-start = (bf16[8,4224]{1,0:T(8,128)(2,1)}, bf16[8,4224]{1,0:T(8,128)(2,1)S(1)}, u32[]{:S(2)}, u32[]{:S(2)}) collective-permute-start(bf16[8,4224]{1,0:T(8,128)(2,1)} %get-tuple-element.44), channel_id=1, source_target_pairs={{0,12},{1,13},{2,14},{3,15},{4,8},{5,9},{6,10},{7,11},{8,4},{9,5},... | collective-permute-start | bytes 202760 | tf_op jit(solution)/shard_map/ppermute | solution.py:388
  8.8 1.1 %collective-permute-start.1 = (bf16[8,4224]{1,0:T(8,128)(2,1)}, bf16[8,4224]{1,0:T(8,128)(2,1)S(1)}, u32[]{:S(2)}, u32[]{:S(2)}) collective-permute-start(bf16[8,4224]{1,0:T(8,128)(2,1)} %get-tuple-element.45), channel_id=1, source_target_pairs={{0,14},{1,15},{2,12},{3,13},{4,10},{5,11},{6,8},{7,9},{8,6},{9,7},... | collective-permute-start | bytes 202760 | tf_op jit(solution)/shard_map/ppermute | solution.py:388
  10.0 0.8 %collective-permute-start.2 = (bf16[8,4224]{1,0:T(8,128)(2,1)}, bf16[8,4224]{1,0:T(8,128)(2,1)S(1)}, u32[]{:S(2)}, u32[]{:S(2)}) collective-permute-start(bf16[8,4224]{1,0:T(8,128)(2,1)} %get-tuple-element.46), channel_id=1, source_target_pairs={{0,8},{1,9},{2,10},{3,11},{4,12},{5,13},{6,14},{7,15},{8,0},{9,1},... | collective-permute-start | bytes 202760 | tf_op jit(solution)/shard_map/ppermute | solution.py:388
  10.8 2.0 %collective-permute-start.3 = (bf16[8,4224]{1,0:T(8,128)(2,1)}, bf16[8,4224]{1,0:T(8,128)(2,1)S(1)}, u32[]{:S(2)}, u32[]{:S(2)}) collective-permute-start(bf16[8,4224]{1,0:T(8,128)(2,1)} %get-tuple-element.47), channel_id=1, source_target_pairs={{0,10},{1,11},{2,8},{3,9},{4,14},{5,15},{6,12},{7,13},{8,2},{9,3},... | collective-permute-start | bytes 202760 | tf_op jit(solution)/shard_map/ppermute | solution.py:388
  12.7 1.4 %collective-permute-start.4 = (bf16[8,4224]{1,0:T(8,128)(2,1)}, bf16[8,4224]{1,0:T(8,128)(2,1)S(1)}, u32[]{:S(2)}, u32[]{:S(2)}) collective-permute-start(bf16[8,4224]{1,0:T(8,128)(2,1)} %get-tuple-element.48), channel_id=1, source_target_pairs={{0,4},{1,5},{2,6},{3,7},{4,0},{5,1},{6,2},{7,3},{8,12},{9,13},{10,... | collective-permute-start | bytes 202760 | tf_op jit(solution)/shard_map/ppermute | solution.py:388
  14.1 1.7 %collective-permute-start.5 = (bf16[8,4224]{1,0:T(8,128)(2,1)}, bf16[8,4224]{1,0:T(8,128)(2,1)S(1)}, u32[]{:S(2)}, u32[]{:S(2)}) collective-permute-start(bf16[8,4224]{1,0:T(8,128)(2,1)} %get-tuple-element.49), channel_id=1, source_target_pairs={{0,6},{1,7},{2,4},{3,5},{4,2},{5,3},{6,0},{7,1},{8,14},{9,15},{10,... | collective-permute-start | bytes 202760 | tf_op jit(solution)/shard_map/ppermute | solution.py:388
  16.2 1.6 %collective-permute-start.6 = (bf16[8,4224]{1,0:T(8,128)(2,1)}, bf16[8,4224]{1,0:T(8,128)(2,1)S(1)}, u32[]{:S(2)}, u32[]{:S(2)}) collective-permute-start(bf16[8,4224]{1,0:T(8,128)(2,1)} %get-tuple-element.51), channel_id=1, source_target_pairs={{0,2},{1,3},{2,0},{3,1},{4,6},{5,7},{6,4},{7,5},{8,10},{9,11},{10,... | collective-permute-start | bytes 202760 | tf_op jit(solution)/shard_map/ppermute | solution.py:388
  17.8 2.1 %collective-permute-done.2.refs_2_ = bf16[8,4224]{1,0:T(8,128)(2,1)S(1)} collective-permute-done((bf16[8,4224]{1,0:T(8,128)(2,1)}, bf16[8,4224]{1,0:T(8,128)(2,1)S(1)}, u32[]{:S(2)}, u32[]{:S(2)}) %collective-permute-start.2) | collective-permute-done | bytes 67616 | tf_op jit(solution)/shard_map/ppermute | solution.py:388
  19.9 1.8 %collective-permute-done.3.refs_3_ = bf16[8,4224]{1,0:T(8,128)(2,1)S(1)} collective-permute-done((bf16[8,4224]{1,0:T(8,128)(2,1)}, bf16[8,4224]{1,0:T(8,128)(2,1)S(1)}, u32[]{:S(2)}, u32[]{:S(2)}) %collective-permute-start.3) | collective-permute-done | bytes 67616 | tf_op jit(solution)/shard_map/ppermute | solution.py:388
  24.5 1.5 %shard_map.120 = (bf16[480,128]{1,0:T(8,128)(2,1)S(1)}, bf16[32,128]{1,0:T(8,128)(2,1)S(1)}, bf16[128,1024]{1,0:T(8,128)(2,1)S(1)}, bf16[128,1024]{1,0:T(8,128)(...) custom-call(s32[1]{0:T(128)} %bitcast.pos_ref, ...), custom_call_target="tpu_custom_call" | custom-call | tf_op jit(solution)/shard_map/pallas_call | solution.py:410
  26.8 2.4 %shard_map.121 = (bf16[176,128]{1,0:T(8,128)(2,1)S(1)}, bf16[2,256,32]{2,1,0:T(8,128)(2,1)S(1)}) custom-call(s32[1]{0:T(128)} %bitcast.pos_ref, bf16[256,2048]{1,0:T(8,128)(2,1)S(1)} %get-tuple-element.62.p_ref, bf16[128,1024]{1,0:T(8,128)(2,1)S(1)} %get-tuple-element.63.right_ref, bf16[128,1024]{1,0:T(8,128)(2,1)S(1)} %get-tuple-element.64.left_ref, ...), custom_call_target="tpu_custom_call" | custom-call | tf_op jit(solution)/shard_map/pallas_call | solution.py:425
  29.2 0.9 %collective-permute-start.15 = (bf16[176,128]{1,0:T(8,128)(2,1)S(1)}, bf16[176,128]{1,0:T(8,128)(2,1)S(1)}, u32[]{:S(2)}, u32[]{:S(2)}) collective-permute-start(bf16[176,128]{1,0:T(8,128)(2,1)S(1)} %get-tuple-element.70), channel_id=1, source_target_pairs={{0,4},{1,5},{2,6},{3,7},{4,0},{5,1},{6,2},{7,3},{8,12},{9,13},{10,... | collective-permute-start | bytes 135176 | tf_op jit(solution)/shard_map/ppermute | solution.py:388
  30.1 1.0 %shard_map.122 = bf16[32,8,256]{2,1,0:T(8,128)(2,1)} custom-call(bf16[32,8,256]{2,1,0:T(8,128)(2,1)S(1)} %copy-done.2, bf16[2,256,32]{2,1,0:T(8,128)(2,1)S(1)} %get-tuple-element.71.grads_ref, bf16[32,256]{1,0:T(8,128)(2,1)S(1)} %bitcast.9, bf16[32,256]{1,0:T(8,128)(2,1)S(1)} %bitcast.11), custom_call_target="tpu_custom_call" | custom-call | flops 8388608 | tf_op jit(solution)/shard_map/pallas_call | solution.py:447
  31.1 2.2 %collective-permute-done.15 = bf16[176,128]{1,0:T(8,128)(2,1)S(1)} collective-permute-done((bf16[176,128]{1,0:T(8,128)(2,1)S(1)}, bf16[176,128]{1,0:T(8,128)(2,1)S(1)}, u32[]{:S(2)}, u32[]{:S(2)}) %collective-permute-start.15) | collective-permute-done | bytes 45088 | tf_op jit(solution)/shard_map/ppermute | solution.py:388
  33.3 0.9 %collective-permute-start.20 = (bf16[480,128]{1,0:T(8,128)(2,1)S(1)}, bf16[480,128]{1,0:T(8,128)(2,1)S(1)}, u32[]{:S(2)}, u32[]{:S(2)}) collective-permute-start(bf16[480,128]{1,0:T(8,128)(2,1)S(1)} %add_convert_fusion.2), channel_id=1, source_target_pairs={{0,4},{1,5},{2,6},{3,7},{4,0},{5,1},{6,2},{7,3},{8,12},{9,13},{10,... | collective-permute-start | bytes 368648 | tf_op jit(solution)/shard_map/ppermute | solution.py:388
  34.2 3.1 %collective-permute-start.16 = (bf16[176,128]{1,0:T(8,128)(2,1)S(1)}, bf16[176,128]{1,0:T(8,128)(2,1)S(1)}, u32[]{:S(2)}, u32[]{:S(2)}) collective-permute-start(bf16[176,128]{1,0:T(8,128)(2,1)S(1)} %add_convert_fusion.5), channel_id=1, source_target_pairs={{0,8},{1,9},{2,10},{3,11},{4,12},{5,13},{6,14},{7,15},{8,0},{9,1},... | collective-permute-start | bytes 135176 | tf_op jit(solution)/shard_map/ppermute | solution.py:388
  38.0 1.7 %shard_map.123 = bf16[8,128,128]{2,1,0:T(8,128)(2,1)} custom-call(bf16[128,1024]{1,0:T(8,128)(2,1)S(1)} %get-tuple-element.63.right_ref, f32[128,1024]{1,0:T(8,128)S(1)} %get-tuple-element.66.inv_ref, bf16[256,32]{1,0:T(8,128)(2,1)S(1)} %copy-done.6, bf16[32,4096]{1,0:T(8,128)(2,1)S(1)} %shard_map.119.wleft_ref, f32[1,128]{1,0:T(1,128)S(1)} %bitcast.12), custom_call_target="tpu_custom_call" | custom-call | flops 268435456 | tf_op jit(solution)/shard_map/pallas_call | solution.py:437
  39.8 2.7 %collective-permute-start.21 = (bf16[480,128]{1,0:T(8,128)(2,1)S(1)}, bf16[480,128]{1,0:T(8,128)(2,1)S(1)}, u32[]{:S(2)}, u32[]{:S(2)}) collective-permute-start(bf16[480,128]{1,0:T(8,128)(2,1)S(1)} %add_convert_fusion.1), channel_id=1, source_target_pairs={{0,8},{1,9},{2,10},{3,11},{4,12},{5,13},{6,14},{7,15},{8,0},{9,1},... | collective-permute-start | bytes 368648 | tf_op jit(solution)/shard_map/ppermute | solution.py:388
  42.5 1.0 %collective-permute-start.17 = (bf16[176,128]{1,0:T(8,128)(2,1)S(1)}, bf16[176,128]{1,0:T(8,128)(2,1)S(1)}, u32[]{:S(2)}, u32[]{:S(2)}) collective-permute-start(bf16[176,128]{1,0:T(8,128)(2,1)S(1)} %add_convert_fusion.4), channel_id=1, source_target_pairs={{0,2},{1,3},{2,0},{3,1},{4,6},{5,7},{6,4},{7,5},{8,10},{9,11},{10,... | collective-permute-start | bytes 135176 | tf_op jit(solution)/shard_map/ppermute | solution.py:388
  43.5 2.1 %collective-permute-done.21 = bf16[480,128]{1,0:T(8,128)(2,1)S(1)} collective-permute-done((bf16[480,128]{1,0:T(8,128)(2,1)S(1)}, bf16[480,128]{1,0:T(8,128)(2,1)S(1)}, u32[]{:S(2)}, u32[]{:S(2)}) %collective-permute-start.21) | collective-permute-done | bytes 122912 | tf_op jit(solution)/shard_map/ppermute | solution.py:388
  45.8 0.9 %collective-permute-done.17 = bf16[176,128]{1,0:T(8,128)(2,1)S(1)} collective-permute-done((bf16[176,128]{1,0:T(8,128)(2,1)S(1)}, bf16[176,128]{1,0:T(8,128)(2,1)S(1)}, u32[]{:S(2)}, u32[]{:S(2)}) %collective-permute-start.17) | collective-permute-done | bytes 45088 | tf_op jit(solution)/shard_map/ppermute | solution.py:388
  46.7 1.2 %collective-permute-done.18.other_b_ref = bf16[176,128]{1,0:T(8,128)(2,1)S(1)} collective-permute-done((bf16[176,128]{1,0:T(8,128)(2,1)S(1)}, bf16[176,128]{1,0:T(8,128)(2,1)S(1)}, u32[]{:S(2)}, u32[]{:S(2)}) %collective-permute-start.18) | collective-permute-done | bytes 45088 | tf_op jit(solution)/shard_map/ppermute | solution.py:388
  48.0 0.8 %shard_map.124 = (f32[1024,128]{1,0:T(8,128)}, f32[32,256]{1,0:T(8,128)}, f32[32,256]{1,0:T(8,128)}, f32[1,128]{1,0:T(1,128)}) custom-call(s32[1]{0:T(128)} %bitcast.pos_ref, bf16[176,128]{1,0:T(8,128)(2,1)S(1)} %add_convert_fusion.3.own_b_ref, bf16[176,128]{1,0:T(8,128)(2,1)S(1)} %collective-permute-done.18.other_b_ref, ...), custom_call_target="tpu_custom_call" | custom-call | tf_op jit(solution)/shard_map/pallas_call | solution.py:468
  (57 shorter events, 4.9 us)
Async XLA Ops:
  0.6 22.8 %copy-start.1 = (bf16[1024,128]{1,0:T(8,128)(2,1)S(1)}, bf16[1024,128]{1,0:T(8,128)(2,1)}, u32[]{:S(2)}) copy-start(bf16[1024,128]{1,0:T(8,128)(2,1)} %wout_ref.3) | copy-start | bytes 786436
  3.7 10.4 %collective-permute-start = (bf16[8,4224]{1,0:T(8,128)(2,1)}, bf16[8,4224]{1,0:T(8,128)(2,1)S(1)}, u32[]{:S(2)}, u32[]{:S(2)}) collective-permute-start(bf16[8,4224]{1,0:T(8,128)(2,1)} %get-tuple-element.44), channel_id=1, source_target_pairs={{0,12},{1,13},{2,14},{3,15},{4,8},{5,9},{6,10},{7,11},{8,4},{9,5},... | collective-permute-start | bytes 202760 | tf_op jit(solution)/shard_map/ppermute | solution.py:388
  8.8 7.4 %collective-permute-start.1 = (bf16[8,4224]{1,0:T(8,128)(2,1)}, bf16[8,4224]{1,0:T(8,128)(2,1)S(1)}, u32[]{:S(2)}, u32[]{:S(2)}) collective-permute-start(bf16[8,4224]{1,0:T(8,128)(2,1)} %get-tuple-element.45), channel_id=1, source_target_pairs={{0,14},{1,15},{2,12},{3,13},{4,10},{5,11},{6,8},{7,9},{8,6},{9,7},... | collective-permute-start | bytes 202760 | tf_op jit(solution)/shard_map/ppermute | solution.py:388
  10.0 9.9 %collective-permute-start.2 = (bf16[8,4224]{1,0:T(8,128)(2,1)}, bf16[8,4224]{1,0:T(8,128)(2,1)S(1)}, u32[]{:S(2)}, u32[]{:S(2)}) collective-permute-start(bf16[8,4224]{1,0:T(8,128)(2,1)} %get-tuple-element.46), channel_id=1, source_target_pairs={{0,8},{1,9},{2,10},{3,11},{4,12},{5,13},{6,14},{7,15},{8,0},{9,1},... | collective-permute-start | bytes 202760 | tf_op jit(solution)/shard_map/ppermute | solution.py:388
  10.8 10.9 %collective-permute-start.3 = (bf16[8,4224]{1,0:T(8,128)(2,1)}, bf16[8,4224]{1,0:T(8,128)(2,1)S(1)}, u32[]{:S(2)}, u32[]{:S(2)}) collective-permute-start(bf16[8,4224]{1,0:T(8,128)(2,1)} %get-tuple-element.47), channel_id=1, source_target_pairs={{0,10},{1,11},{2,8},{3,9},{4,14},{5,15},{6,12},{7,13},{8,2},{9,3},... | collective-permute-start | bytes 202760 | tf_op jit(solution)/shard_map/ppermute | solution.py:388
  12.7 8.9 %collective-permute-start.4 = (bf16[8,4224]{1,0:T(8,128)(2,1)}, bf16[8,4224]{1,0:T(8,128)(2,1)S(1)}, u32[]{:S(2)}, u32[]{:S(2)}) collective-permute-start(bf16[8,4224]{1,0:T(8,128)(2,1)} %get-tuple-element.48), channel_id=1, source_target_pairs={{0,4},{1,5},{2,6},{3,7},{4,0},{5,1},{6,2},{7,3},{8,12},{9,13},{10,... | collective-permute-start | bytes 202760 | tf_op jit(solution)/shard_map/ppermute | solution.py:388
  14.1 8.0 %collective-permute-start.5 = (bf16[8,4224]{1,0:T(8,128)(2,1)}, bf16[8,4224]{1,0:T(8,128)(2,1)S(1)}, u32[]{:S(2)}, u32[]{:S(2)}) collective-permute-start(bf16[8,4224]{1,0:T(8,128)(2,1)} %get-tuple-element.49), channel_id=1, source_target_pairs={{0,6},{1,7},{2,4},{3,5},{4,2},{5,3},{6,0},{7,1},{8,14},{9,15},{10,... | collective-permute-start | bytes 202760 | tf_op jit(solution)/shard_map/ppermute | solution.py:388
  16.2 6.0 %collective-permute-start.6 = (bf16[8,4224]{1,0:T(8,128)(2,1)}, bf16[8,4224]{1,0:T(8,128)(2,1)S(1)}, u32[]{:S(2)}, u32[]{:S(2)}) collective-permute-start(bf16[8,4224]{1,0:T(8,128)(2,1)} %get-tuple-element.51), channel_id=1, source_target_pairs={{0,2},{1,3},{2,0},{3,1},{4,6},{5,7},{6,4},{7,5},{8,10},{9,11},{10,... | collective-permute-start | bytes 202760 | tf_op jit(solution)/shard_map/ppermute | solution.py:388
  19.9 2.8 %collective-permute-start.13 = (bf16[8,4224]{1,0:T(8,128)(2,1)}, bf16[8,4224]{1,0:T(8,128)(2,1)S(1)}, u32[]{:S(2)}, u32[]{:S(2)}) collective-permute-start(bf16[8,4224]{1,0:T(8,128)(2,1)} %get-tuple-element.58.refs_6_), channel_id=1, source_target_pairs={{0,1},{1,0},{2,3},{3,2},{4,5},{5,4},{6,7},{7,6},{8,9},{9,8},{10,11... | collective-permute-start | bytes 202760 | tf_op jit(solution)/shard_map/ppermute | solution.py:388
  21.7 1.3 %collective-permute-start.7 = (bf16[8,4224]{1,0:T(8,128)(2,1)S(1)}, bf16[8,4224]{1,0:T(8,128)(2,1)S(1)}, u32[]{:S(2)}, u32[]{:S(2)}) collective-permute-start(bf16[8,4224]{1,0:T(8,128)(2,1)S(1)} %collective-permute-done.refs_0_), channel_id=1, source_target_pairs={{0,1},{1,0},{2,3},{3,2},{4,5},{5,4},{6,7},{7,6},{8,9},{9,8},{10,11... | collective-permute-start | bytes 202760 | tf_op jit(solution)/shard_map/ppermute | solution.py:388
  21.7 1.5 %collective-permute-start.8 = (bf16[8,4224]{1,0:T(8,128)(2,1)S(1)}, bf16[8,4224]{1,0:T(8,128)(2,1)S(1)}, u32[]{:S(2)}, u32[]{:S(2)}) collective-permute-start(bf16[8,4224]{1,0:T(8,128)(2,1)S(1)} %collective-permute-done.1.refs_1_), channel_id=1, source_target_pairs={{0,1},{1,0},{2,3},{3,2},{4,5},{5,4},{6,7},{7,6},{8,9},{9,8},{10,11... | collective-permute-start | bytes 202760 | tf_op jit(solution)/shard_map/ppermute | solution.py:388
  22.2 1.6 %collective-permute-start.9 = (bf16[8,4224]{1,0:T(8,128)(2,1)S(1)}, bf16[8,4224]{1,0:T(8,128)(2,1)S(1)}, u32[]{:S(2)}, u32[]{:S(2)}) collective-permute-start(bf16[8,4224]{1,0:T(8,128)(2,1)S(1)} %collective-permute-done.2.refs_2_), channel_id=1, source_target_pairs={{0,1},{1,0},{2,3},{3,2},{4,5},{5,4},{6,7},{7,6},{8,9},{9,8},{10,11... | collective-permute-start | bytes 202760 | tf_op jit(solution)/shard_map/ppermute | solution.py:388
  22.3 1.5 %collective-permute-start.10 = (bf16[8,4224]{1,0:T(8,128)(2,1)S(1)}, bf16[8,4224]{1,0:T(8,128)(2,1)S(1)}, u32[]{:S(2)}, u32[]{:S(2)}) collective-permute-start(bf16[8,4224]{1,0:T(8,128)(2,1)S(1)} %collective-permute-done.3.refs_3_), channel_id=1, source_target_pairs={{0,1},{1,0},{2,3},{3,2},{4,5},{5,4},{6,7},{7,6},{8,9},{9,8},{10,11... | collective-permute-start | bytes 202760 | tf_op jit(solution)/shard_map/ppermute | solution.py:388
  22.7 1.3 %collective-permute-start.11 = (bf16[8,4224]{1,0:T(8,128)(2,1)S(1)}, bf16[8,4224]{1,0:T(8,128)(2,1)S(1)}, u32[]{:S(2)}, u32[]{:S(2)}) collective-permute-start(bf16[8,4224]{1,0:T(8,128)(2,1)S(1)} %collective-permute-done.4.refs_4_), channel_id=1, source_target_pairs={{0,1},{1,0},{2,3},{3,2},{4,5},{5,4},{6,7},{7,6},{8,9},{9,8},{10,11... | collective-permute-start | bytes 202760 | tf_op jit(solution)/shard_map/ppermute | solution.py:388
  22.9 1.3 %collective-permute-start.12 = (bf16[8,4224]{1,0:T(8,128)(2,1)S(1)}, bf16[8,4224]{1,0:T(8,128)(2,1)S(1)}, u32[]{:S(2)}, u32[]{:S(2)}) collective-permute-start(bf16[8,4224]{1,0:T(8,128)(2,1)S(1)} %collective-permute-done.5.refs_5_), channel_id=1, source_target_pairs={{0,1},{1,0},{2,3},{3,2},{4,5},{5,4},{6,7},{7,6},{8,9},{9,8},{10,11... | collective-permute-start | bytes 202760 | tf_op jit(solution)/shard_map/ppermute | solution.py:388
  23.2 1.3 %collective-permute-start.14 = (bf16[8,4224]{1,0:T(8,128)(2,1)S(1)}, bf16[8,4224]{1,0:T(8,128)(2,1)S(1)}, u32[]{:S(2)}, u32[]{:S(2)}) collective-permute-start(bf16[8,4224]{1,0:T(8,128)(2,1)S(1)} %collective-permute-done.6.refs_7_), channel_id=1, source_target_pairs={{0,1},{1,0},{2,3},{3,2},{4,5},{5,4},{6,7},{7,6},{8,9},{9,8},{10,11... | collective-permute-start | bytes 202760 | tf_op jit(solution)/shard_map/ppermute | solution.py:388
  26.0 7.2 %collective-permute-start.19 = (bf16[480,128]{1,0:T(8,128)(2,1)S(1)}, bf16[480,128]{1,0:T(8,128)(2,1)S(1)}, u32[]{:S(2)}, u32[]{:S(2)}) collective-permute-start(bf16[480,128]{1,0:T(8,128)(2,1)S(1)} %get-tuple-element.77), channel_id=1, source_target_pairs={{0,2},{1,3},{2,0},{3,1},{4,6},{5,7},{6,4},{7,5},{8,10},{9,11},{10,... | collective-permute-start | bytes 368648 | tf_op jit(solution)/shard_map/ppermute | solution.py:388
  29.2 4.1 %collective-permute-start.15 = (bf16[176,128]{1,0:T(8,128)(2,1)S(1)}, bf16[176,128]{1,0:T(8,128)(2,1)S(1)}, u32[]{:S(2)}, u32[]{:S(2)}) collective-permute-start(bf16[176,128]{1,0:T(8,128)(2,1)S(1)} %get-tuple-element.70), channel_id=1, source_target_pairs={{0,4},{1,5},{2,6},{3,7},{4,0},{5,1},{6,2},{7,3},{8,12},{9,13},{10,... | collective-permute-start | bytes 135176 | tf_op jit(solution)/shard_map/ppermute | solution.py:388
  33.3 6.4 %collective-permute-start.20 = (bf16[480,128]{1,0:T(8,128)(2,1)S(1)}, bf16[480,128]{1,0:T(8,128)(2,1)S(1)}, u32[]{:S(2)}, u32[]{:S(2)}) collective-permute-start(bf16[480,128]{1,0:T(8,128)(2,1)S(1)} %add_convert_fusion.2), channel_id=1, source_target_pairs={{0,4},{1,5},{2,6},{3,7},{4,0},{5,1},{6,2},{7,3},{8,12},{9,13},{10,... | collective-permute-start | bytes 368648 | tf_op jit(solution)/shard_map/ppermute | solution.py:388
  34.2 5.5 %collective-permute-start.16 = (bf16[176,128]{1,0:T(8,128)(2,1)S(1)}, bf16[176,128]{1,0:T(8,128)(2,1)S(1)}, u32[]{:S(2)}, u32[]{:S(2)}) collective-permute-start(bf16[176,128]{1,0:T(8,128)(2,1)S(1)} %add_convert_fusion.5), channel_id=1, source_target_pairs={{0,8},{1,9},{2,10},{3,11},{4,12},{5,13},{6,14},{7,15},{8,0},{9,1},... | collective-permute-start | bytes 135176 | tf_op jit(solution)/shard_map/ppermute | solution.py:388
  39.8 5.8 %collective-permute-start.21 = (bf16[480,128]{1,0:T(8,128)(2,1)S(1)}, bf16[480,128]{1,0:T(8,128)(2,1)S(1)}, u32[]{:S(2)}, u32[]{:S(2)}) collective-permute-start(bf16[480,128]{1,0:T(8,128)(2,1)S(1)} %add_convert_fusion.1), channel_id=1, source_target_pairs={{0,8},{1,9},{2,10},{3,11},{4,12},{5,13},{6,14},{7,15},{8,0},{9,1},... | collective-permute-start | bytes 368648 | tf_op jit(solution)/shard_map/ppermute | solution.py:388
  42.5 4.1 %collective-permute-start.17 = (bf16[176,128]{1,0:T(8,128)(2,1)S(1)}, bf16[176,128]{1,0:T(8,128)(2,1)S(1)}, u32[]{:S(2)}, u32[]{:S(2)}) collective-permute-start(bf16[176,128]{1,0:T(8,128)(2,1)S(1)} %add_convert_fusion.4), channel_id=1, source_target_pairs={{0,2},{1,3},{2,0},{3,1},{4,6},{5,7},{6,4},{7,5},{8,10},{9,11},{10,... | collective-permute-start | bytes 135176 | tf_op jit(solution)/shard_map/ppermute | solution.py:388
  45.7 2.3 %collective-permute-start.22 = (bf16[480,128]{1,0:T(8,128)(2,1)S(1)}, bf16[480,128]{1,0:T(8,128)(2,1)S(1)}, u32[]{:S(2)}, u32[]{:S(2)}) collective-permute-start(bf16[480,128]{1,0:T(8,128)(2,1)S(1)} %add_convert_fusion.own_a_ref), channel_id=1, source_target_pairs={{0,1},{1,0},{2,3},{3,2},{4,5},{5,4},{6,7},{7,6},{8,9},{9,8},{10,11... | collective-permute-start | bytes 368648 | tf_op jit(solution)/shard_map/ppermute | solution.py:388
  46.7 1.3 %collective-permute-start.18 = (bf16[176,128]{1,0:T(8,128)(2,1)S(1)}, bf16[176,128]{1,0:T(8,128)(2,1)S(1)}, u32[]{:S(2)}, u32[]{:S(2)}) collective-permute-start(bf16[176,128]{1,0:T(8,128)(2,1)S(1)} %add_convert_fusion.3.own_b_ref), channel_id=1, source_target_pairs={{0,1},{1,0},{2,3},{3,2},{4,5},{5,4},{6,7},{7,6},{8,9},{9,8},{10,11... | collective-permute-start | bytes 135176 | tf_op jit(solution)/shard_map/ppermute | solution.py:388
  (10 other events, 33.0 us)
